TPU v7x, 512 devices: a whole 4x4x16 slice. The times are simulated.
512 devices in a mesh: prow: 16 (over z), pcol: 32 (over x, y, core).
Axes of the slice: x: 4, y: 4, z: 16, core: 2. Of those that a mesh axis runs over, the one named last changes fastest.
Arguments:
- right_sides: bfloat16 [16, 32, 3, 1, 64, 128], P('prow', 'pcol'), may hold values from -6 to 6
- lower_inverse: bfloat16 [16, 32, 3, 1, 128, 128], P('prow', 'pcol')
- upper_inverse: bfloat16 [16, 32, 3, 1, 128, 128], P('prow', 'pcol')
- lower_tiles: bfloat16 [16, 32, 2, 4, 128, 128], P('prow', 'pcol'), may hold values from -0.25 to 0.25
- lower_source: int32 [16, 32, 2, 4], P('prow', 'pcol'), may hold values from 0 to 15
- lower_target: int32 [16, 32, 2, 4], P('prow', 'pcol'), may hold values from 0 to 63, as said below
- lower_rows: int32 [16, 32, 2, 4, 128], P('prow', 'pcol'), may hold values from 0 to 128, as said below
- lower_count: int32 [16, 32, 2], P('prow', 'pcol'), may hold values from 3 to 4, as said below
- upper_tiles: bfloat16 [16, 32, 2, 4, 128, 128], P('prow', 'pcol'), may hold values from -0.25 to 0.25
- upper_source: int32 [16, 32, 2, 4], P('prow', 'pcol'), may hold values from 0 to 15
- upper_target: int32 [16, 32, 2, 4], P('prow', 'pcol'), may hold values from 0 to 63, as said below
- upper_rows: int32 [16, 32, 2, 4, 128], P('prow', 'pcol'), may hold values from 0 to 128, as said below
- upper_count: int32 [16, 32, 2], P('prow', 'pcol'), may hold values from 3 to 4, as said below
Outputs:
- solution: bfloat16 [16, 32, 3, 1, 64, 128], P('prow', 'pcol')
Inputs may be any that keep to these rules, and one draw needn't show every extreme that they name: `lower_target`: in group g the value is t * 32 + i with level t < 2-g (an ancestor level). `upper_target`: in group g the value is (t - 1) * 32 + i with level t > g (a descendant level). `lower_rows`: within one block the entries below 128 are distinct; 128 marks an unused row, and every block has one or more. `upper_rows`: within one block the entries below 128 are distinct; 128 marks an unused row, and every block has one or more. `lower_count`: slots 0 to count - 1 of a group are live. `upper_count`: slots 0 to count - 1 of a group are live.
All inputs are finite; a program needn't handle non-finite values.
Results may differ from a plain program's by a relative error of at most 0.019.
Values may be sent and summed in bfloat16 or wider, within the bound.
No kernel may reach another device: no remote copies, remote signals or barrier semaphores. Data moves between devices by JAX's collectives and lax.ppermute only.
A program may use at most 64 MiB of HBM per device.

v0:
```python
import jax
import jax.numpy as jnp
from jax import lax
from jax.sharding import PartitionSpec as P


def apply_inverse(operand, inverse):
    product = jnp.einsum(
        "kns,kst->knt", operand, inverse.astype(jnp.float32), precision=lax.Precision.HIGHEST
    )
    return product.astype(jnp.bfloat16)


def select_tiles(column, source):
    selector = (source[:, None] == jnp.arange(column.shape[0], dtype=jnp.int32)[None, :]).astype(
        jnp.bfloat16
    )
    picked = jnp.einsum("bj,jns->bns", selector, column, preferred_element_type=jnp.float32)
    return picked.astype(jnp.bfloat16)


def row_table(row_index, dtype):
    extent = row_index.shape[1]
    return (row_index[:, :, None] == jnp.arange(extent, dtype=jnp.int32)[None, None, :]).astype(
        dtype
    )


def place_columns(products, row_index):
    table = row_table(row_index, jnp.float32)
    return jnp.einsum("bnp,bpq->bnq", products, table, precision=lax.Precision.HIGHEST)


def pick_columns(tiles, row_index):
    table = row_table(row_index, jnp.bfloat16)
    chosen = jnp.einsum("bnq,bpq->bnp", tiles, table, preferred_element_type=jnp.float32)
    return chosen.astype(jnp.bfloat16)


def accumulate(pending, products, target, live_count):
    blocks = products.shape[0]
    active = (jnp.arange(blocks, dtype=jnp.int32) < live_count).astype(jnp.float32)
    owners = (jnp.arange(pending.shape[0], dtype=jnp.int32)[:, None] == target[None, :]).astype(
        jnp.float32
    )
    owners = owners * active[None, :]
    return pending + jnp.einsum("tb,bnq->tnq", owners, products, precision=lax.Precision.HIGHEST)


def lower_total(partial_value):
    summed = lax.psum_scatter(
        partial_value.astype(jnp.bfloat16), "pcol", scatter_dimension=0, tiled=True
    ).astype(jnp.float32)
    return summed


def upper_total(partial_value):
    summed = lax.psum_scatter(
        partial_value.astype(jnp.bfloat16), "pcol", scatter_dimension=0, tiled=True
    ).astype(jnp.float32)
    return summed


def sweep(right_sides, factors):
    (
        lower_inverse,
        upper_inverse,
        lower_tiles,
        lower_source,
        lower_target,
        lower_rows,
        lower_count,
        upper_tiles,
        upper_source,
        upper_target,
        upper_rows,
        upper_count,
    ) = factors
    level_count, per_device, side_extent, node_extent = right_sides.shape
    row_group = per_device * lax.axis_size("pcol")
    buffer_rows = (level_count - 1) * row_group
    pending = jnp.zeros((buffer_rows, side_extent, node_extent), jnp.float32)
    forward = [None] * level_count
    for height in range(level_count - 1, -1, -1):
        operand = right_sides[height].astype(jnp.float32)
        if height < level_count - 1:
            operand = operand - lower_total(pending[height * row_group : (height + 1) * row_group])
        forward[height] = apply_inverse(operand, lower_inverse[height])
        if height > 0:
            source_group = level_count - 1 - height
            column = lax.all_gather(forward[height], "prow", axis=0, tiled=True)
            picked = select_tiles(column, lower_source[source_group])
            products = jnp.einsum(
                "bns,bst->bnt",
                picked,
                lower_tiles[source_group],
                preferred_element_type=jnp.float32,
            )
            moved = place_columns(products, lower_rows[source_group])
            pending = accumulate(
                pending, moved, lower_target[source_group], lower_count[source_group]
            )
    pending = jnp.zeros((buffer_rows, side_extent, node_extent), jnp.float32)
    solution = [None] * level_count
    for height in range(level_count):
        operand = forward[height].astype(jnp.float32)
        if height > 0:
            operand = operand - upper_total(pending[(height - 1) * row_group : height * row_group])
        solution[height] = apply_inverse(operand, upper_inverse[height])
        if height < level_count - 1:
            column = lax.all_gather(solution[height], "prow", axis=0, tiled=True)
            picked = select_tiles(column, upper_source[height])
            chosen = pick_columns(picked, upper_rows[height])
            products = jnp.einsum(
                "bns,bst->bnt", chosen, upper_tiles[height], preferred_element_type=jnp.float32
            )
            pending = accumulate(pending, products, upper_target[height], upper_count[height])
    return jnp.stack(solution, axis=0)


def body(
    right_sides,
    lower_inverse,
    upper_inverse,
    lower_tiles,
    lower_source,
    lower_target,
    lower_rows,
    lower_count,
    upper_tiles,
    upper_source,
    upper_target,
    upper_rows,
    upper_count,
):
    factors = tuple(
        (
            array[0, 0]
            for array in (
                lower_inverse,
                upper_inverse,
                lower_tiles,
                lower_source,
                lower_target,
                lower_rows,
                lower_count,
                upper_tiles,
                upper_source,
                upper_target,
                upper_rows,
                upper_count,
            )
        )
    )
    sides_local = right_sides[0, 0]
    solution = sweep(sides_local, factors)
    return solution[None, None]


def solution(mesh):
    placed = (
        P("prow", "pcol", None, None, None, None),
        P("prow", "pcol", None, None, None, None),
        P("prow", "pcol", None, None, None, None),
        P("prow", "pcol", None, None, None, None),
        P("prow", "pcol", None, None),
        P("prow", "pcol", None, None),
        P("prow", "pcol", None, None, None),
        P("prow", "pcol", None),
        P("prow", "pcol", None, None, None, None),
        P("prow", "pcol", None, None),
        P("prow", "pcol", None, None),
        P("prow", "pcol", None, None, None),
        P("prow", "pcol", None),
    )
    return jax.shard_map(
        body,
        mesh=mesh,
        in_specs=placed,
        out_specs=P("prow", "pcol", None, None, None, None),
        check_vma=False,
    )
```

profile of v0, /device:TPU:1, one launch (start us, length us, event | category | flops | bytes accessed | tf_op | source)
XLA Modules:
  0.0 555.4 jit_solution(5657598963333717819)
XLA Ops:
  6.5 0.8 slice_bitcast_fusion.8
  8.1 1.3 fusion.108
  10.6 0.9 convolution_convert_fusion.7
  11.5 30.5 %all-gather = bf16[1024,128]{1,0:T(8,128)(2,1)S(1)} all-gather(bf16[64,128]{1,0:T(8,128)(2,1)S(1)} %convolution_convert_fusion.7), channel_id=2, replica_groups=mesh['prow'=16,'pcol'=32] {'prow'}, dimensions={0}, use_global_device_ids=true | all-gather | bytes 278528 | tf_op jit(solution)/shard_map/all_gather | solution.py:91
  42.3 1.1 fusion.19
  43.7 1.9 fusion.27
  45.8 1.0 copy.18
  47.5 101.0 %reduce-scatter.5.cloned.1.call-done = bf16[1,64,128]{2,1,0:T(8,128)(2,1)} async-done(((bf16[32,64,128]{2,1,0:T(8,128)(2,1)}), bf16[1,64,128]{2,1,0:T(8,128)(2,1)}) %reduce-scatter.5.cloned.1.call-update) | async-done | bytes 16400 | tf_op jit(solution)/shard_map/reduce_scatter | solution.py:51
  148.5 0.9 convolution_convert_fusion.6
  149.4 24.2 %all-gather.1 = bf16[1024,128]{1,0:T(8,128)(2,1)S(1)} all-gather(bf16[64,128]{1,0:T(8,128)(2,1)S(1)} %convolution_convert_fusion.6), channel_id=3, replica_groups=mesh['prow'=16,'pcol'=32] {'prow'}, dimensions={0}, use_global_device_ids=true | all-gather | bytes 278528 | tf_op jit(solution)/shard_map/all_gather | solution.py:91
  174.4 1.9 fusion.25
  176.6 1.0 copy.19
  178.9 102.2 %reduce-scatter.7.cloned.1.call-done = bf16[1,64,128]{2,1,0:T(8,128)(2,1)} async-done(((bf16[32,64,128]{2,1,0:T(8,128)(2,1)}), bf16[1,64,128]{2,1,0:T(8,128)(2,1)}) %reduce-scatter.7.cloned.1.call-update) | async-done | bytes 16400 | tf_op jit(solution)/shard_map/reduce_scatter | solution.py:51
  281.2 0.9 convolution_convert_fusion.5
  282.2 24.5 %all-gather.2 = bf16[1024,128]{1,0:T(8,128)(2,1)S(1)} all-gather(bf16[64,128]{1,0:T(8,128)(2,1)S(1)} %convolution_convert_fusion.4), channel_id=4, replica_groups=mesh['prow'=16,'pcol'=32] {'prow'}, dimensions={0}, use_global_device_ids=true | all-gather | bytes 278528 | tf_op jit(solution)/shard_map/all_gather | solution.py:111
  307.4 1.9 fusion.23
  309.4 1.2 copy.70
  311.4 102.5 %reduce-scatter.9.cloned.1.call-done = bf16[1,64,128]{2,1,0:T(8,128)(2,1)} async-done(((bf16[32,64,128]{2,1,0:T(8,128)(2,1)}), bf16[1,64,128]{2,1,0:T(8,128)(2,1)}) %reduce-scatter.9.cloned.1.call-update) | async-done | bytes 16400 | tf_op jit(solution)/shard_map/reduce_scatter | solution.py:58
  413.9 0.9 convolution_convert_fusion.3
  414.8 25.7 %all-gather.3 = bf16[1024,128]{1,0:T(8,128)(2,1)S(1)} all-gather(bf16[64,128]{1,0:T(8,128)(2,1)S(1)} %convolution_convert_fusion.3), channel_id=5, replica_groups=mesh['prow'=16,'pcol'=32] {'prow'}, dimensions={0}, use_global_device_ids=true | all-gather | bytes 278528 | tf_op jit(solution)/shard_map/all_gather | solution.py:111
  441.1 1.9 fusion.21
  443.1 1.9 fusion.3
  445.1 102.2 %reduce-scatter.11.cloned.1.call-done = bf16[1,64,128]{2,1,0:T(8,128)(2,1)} async-done(((bf16[32,64,128]{2,1,0:T(8,128)(2,1)}), bf16[1,64,128]{2,1,0:T(8,128)(2,1)}) %reduce-scatter.11.cloned.1.call-update) | async-done | bytes 16400 | tf_op jit(solution)/shard_map/reduce_scatter | solution.py:58
  547.3 0.9 fusion.2
  (55 shorter events, 8.7 us)
Async XLA Ops:
  6.5 142.0 %reduce-scatter.5.cloned.1.call-start = ((), (), s32[]{:S(2)}) async-start(), calls=%async_computation.4 | async-start | bytes 540672 | tf_op jit(solution)/shard_map/reduce_scatter | solution.py:51
  43.7 104.8 %copy-start.2 = (bf16[1,1,3,1,128,128]{5,4,3,2,1,0:T(8,128)(2,1)S(1)}, bf16[1,1,3,1,128,128]{5,4,3,2,1,0:T(8,128)(2,1)}, u32[]{:S(2)}) copy-start(bf16[1,1,3,1,128,128]{5,4,3,2,1,0:T(8,128)(2,1)} %param.14) | copy-start | bytes 294916
  43.7 104.8 %copy-start.4 = (bf16[1,1,3,1,64,128]{5,4,3,2,1,0:T(8,128)(2,1)S(1)}, bf16[1,1,3,1,64,128]{5,4,3,2,1,0:T(8,128)(2,1)}, u32[]{:S(2)}) copy-start(bf16[1,1,3,1,64,128]{5,4,3,2,1,0:T(8,128)(2,1)} %param.13) | copy-start | bytes 147460
  45.7 128.2 %copy-start.1 = (bf16[1,1,2,4,128,128]{5,4,3,2,1,0:T(8,128)(2,1)S(1)}, bf16[1,1,2,4,128,128]{5,4,3,2,1,0:T(8,128)(2,1)}, u32[]{:S(2)}) copy-start(bf16[1,1,2,4,128,128]{5,4,3,2,1,0:T(8,128)(2,1)} %param.16) | copy-start | bytes 786436
  46.8 234.4 %reduce-scatter.7.cloned.1.call-start = ((), (), s32[]{:S(2)}) async-start(), calls=%async_computation.5 | async-start | bytes 540672 | tf_op jit(solution)/shard_map/reduce_scatter | solution.py:51
  176.3 1.4 copy-start.6
  176.3 2.5 copy-start.7
  176.3 2.5 copy-start.8
  176.4 2.6 copy-start.5
  176.4 105.7 %copy-start.3 = (bf16[1,1,3,1,128,128]{5,4,3,2,1,0:T(8,128)(2,1)S(1)}, bf16[1,1,3,1,128,128]{5,4,3,2,1,0:T(8,128)(2,1)}, u32[]{:S(2)}) copy-start(bf16[1,1,3,1,128,128]{5,4,3,2,1,0:T(8,128)(2,1)} %param.15) | copy-start | bytes 294916
  176.4 130.6 %copy-start.9 = (bf16[1,1,2,4,128,128]{5,4,3,2,1,0:T(8,128)(2,1)S(1)}, bf16[1,1,2,4,128,128]{5,4,3,2,1,0:T(8,128)(2,1)}, u32[]{:S(2)}) copy-start(bf16[1,1,2,4,128,128]{5,4,3,2,1,0:T(8,128)(2,1)} %param.21) | copy-start | bytes 786436
  177.7 236.2 %reduce-scatter.9.cloned.1.call-start = ((), (), s32[]{:S(2)}) async-start(), calls=%async_computation.6 | async-start | bytes 540672 | tf_op jit(solution)/shard_map/reduce_scatter | solution.py:58
  309.3 2.1 copy-start
  310.7 236.6 %reduce-scatter.11.cloned.1.call-start = ((), (), s32[]{:S(2)}) async-start(), calls=%async_computation.7 | async-start | bytes 540672 | tf_op jit(solution)/shard_map/reduce_scatter | solution.py:58
  441.1 2.0 slice-start
Sparse Core Ops, SparseCore 0:
  46.9 101.5 reduce-scatter.4
  177.8 103.3 reduce-scatter.6
  310.8 103.0 reduce-scatter.8
  445.2 102.0 reduce-scatter.10
where the time goes:
time: 557 us; the launch traced here: 555 us
  waiting for transfers between devices  408 us (73%)
  blocking collectives  105 us (19%)
  matrix products  16 us (3%)
  between operations  13.5 us (2%)
  local copies, waits for them, and re-layouts  7.72 us (1%)
    reduce_scatter x2, waiting for transfers between devices, upper_total(): lax.psum_scatter(partial_value.astype(jnp.bfloat16), 'pcol', scatter_dime...  205 us
    reduce_scatter x2, waiting for transfers between devices, lower_total(): lax.psum_scatter(partial_value.astype(jnp.bfloat16), 'pcol', scatter_dime...  203 us
    all_gather x2, blocking collectives, sweep(): column = lax.all_gather(forward[height], 'prow', axis=0, tiled=True)  54.7 us
    all_gather x2, blocking collectives, sweep(): column = lax.all_gather(solution[height], 'prow', axis=0, tiled=True)  50.2 us
  transfers between devices with their start and end apart: 4, of which 4 were waited for; matrix products, arithmetic and copies ran while one was open for 0% of the time, Pallas kernels for 0%

commit v1 on v0

--- a/solution.py
+++ b/solution.py
@@ -48,17 +48,18 @@
 
 
 def lower_total(partial_value):
-    summed = lax.psum_scatter(
-        partial_value.astype(jnp.bfloat16), "pcol", scatter_dimension=0, tiled=True
-    ).astype(jnp.float32)
-    return summed
+    pieces = lax.all_to_all(partial_value.astype(jnp.bfloat16), "pcol", 0, 0, tiled=True)
+    return jnp.sum(pieces.astype(jnp.float32), axis=0, keepdims=True)
 
 
 def upper_total(partial_value):
-    summed = lax.psum_scatter(
-        partial_value.astype(jnp.bfloat16), "pcol", scatter_dimension=0, tiled=True
-    ).astype(jnp.float32)
-    return summed
+    pieces = lax.all_to_all(partial_value.astype(jnp.bfloat16), "pcol", 0, 0, tiled=True)
+    return jnp.sum(pieces.astype(jnp.float32), axis=0, keepdims=True)
+
+
+def gather_column(tile):
+    copies = jnp.broadcast_to(tile, (lax.axis_size("prow"),) + tile.shape[1:])
+    return lax.all_to_all(copies, "prow", 0, 0, tiled=True)
 
 
 def sweep(right_sides, factors):
@@ -88,7 +89,7 @@
         forward[height] = apply_inverse(operand, lower_inverse[height])
         if height > 0:
             source_group = level_count - 1 - height
-            column = lax.all_gather(forward[height], "prow", axis=0, tiled=True)
+            column = gather_column(forward[height])
             picked = select_tiles(column, lower_source[source_group])
             products = jnp.einsum(
                 "bns,bst->bnt",
@@ -108,7 +109,7 @@
             operand = operand - upper_total(pending[(height - 1) * row_group : height * row_group])
         solution[height] = apply_inverse(operand, upper_inverse[height])
         if height < level_count - 1:
-            column = lax.all_gather(solution[height], "prow", axis=0, tiled=True)
+            column = gather_column(solution[height])
             picked = select_tiles(column, upper_source[height])
             chosen = pick_columns(picked, upper_rows[height])
             products = jnp.einsum(

time: 557 us -> 192 us (0.34)
  waiting for transfers between devices: 408 us -> 51.3 us
  starting transfers between devices: 0.13 us -> 32.6 us
  blocking collectives: 105 us -> 81.6 us
  between operations: 13.5 us -> 0.39 us
    reduce_scatter x4 -> x0, waiting for transfers between devices: 408 us -> none  [the longest x2 205 us: upper_total(): lax.psum_scatter(partial_value.astype(jnp.bfloat16), 'pcol', scatter_dime...]
    all_gather x4 -> x0, blocking collectives: 105 us -> none  [the longest x2 54.7 us: sweep(): column = lax.all_gather(forward[height], 'prow', axis=0, tiled=True)]
    all_to_all x0 -> x4, blocking collectives: none -> 81.6 us  [the longest x2 43.7 us: lower_total(): lax.all_to_all(partial_value.astype(jnp.bfloat16), 'pcol', 0, 0, tiled=True)]
    all_to_all x0 -> x4, waiting for transfers between devices: none -> 51.3 us  [gather_column(): return lax.all_to_all(copies, 'prow', 0, 0, tiled=True)]
    all_to_all x0 -> x4, starting transfers between devices: none -> 32.6 us  [gather_column(): return lax.all_to_all(copies, 'prow', 0, 0, tiled=True)]
  transfers between devices with their start and end apart: 4 -> 4, of which waited for: 4 -> 4; matrix products, arithmetic and copies ran while one was open for 0% -> 4% of each run, Pallas kernels for 0% -> 0%
where the time goes in v1:
time: 192 us; the launch traced here: 191 us
  blocking collectives  81.6 us (42%)
  waiting for transfers between devices  51.3 us (27%)
  starting transfers between devices  32.6 us (17%)
  matrix products  13.1 us (7%)
  local copies, waits for them, and re-layouts  8.22 us (4%)
  other arithmetic  4 us (2%)
    all_to_all x4, waiting for transfers between devices, gather_column(): return lax.all_to_all(copies, 'prow', 0, 0, tiled=True)  51.3 us
    all_to_all x2, blocking collectives, lower_total(): lax.all_to_all(partial_value.astype(jnp.bfloat16), 'pcol', 0, 0, tiled=True)  43.7 us
    all_to_all x2, blocking collectives, upper_total(): lax.all_to_all(partial_value.astype(jnp.bfloat16), 'pcol', 0, 0, tiled=True)  37.9 us
    all_to_all x4, starting transfers between devices, gather_column(): return lax.all_to_all(copies, 'prow', 0, 0, tiled=True)  32.6 us
    dot_general x4, matrix products, accumulate(): jnp.einsum('tb,bnq->tnq', owners, products, precision=lax.Precision.HIGHEST)  7.7 us
  transfers between devices with their start and end apart: 4, of which 4 were waited for; matrix products, arithmetic and copies ran while one was open for 4% of the time, Pallas kernels for 0%

profile of v1, /device:TPU:1, one launch (start us, length us, event | category | flops | bytes accessed | tf_op | source)
XLA Modules:
  0.0 191.2 jit_solution(870493759487618659)
XLA Ops:
  0.0 0.9 convolution_convert_fusion.7
  0.9 0.8 broadcast_in_dim.10
  1.7 15.7 %all-to-all-start = ((bf16[16,64,128]{2,1,0:T(8,128)(2,1)}), bf16[16,64,128]{2,1,0:T(8,128)(2,1)S(1)}, u32[]{:S(2)}, u32[]{:S(2)}) async-start(bf16[16,64,128]{2,1,0:T(8,128)(2,1)} %broadcast_in_dim.10), calls=%async_computation | async-start | bytes 524288 | tf_op jit(solution)/shard_map/all_to_all | solution.py:62
  17.4 1.3 fusion.100
  19.4 0.8 slice_bitcast_fusion.8
  20.1 0.8 slice_bitcast_fusion.9
  21.6 9.0 %all-to-all-done = bf16[16,64,128]{2,1,0:T(8,128)(2,1)S(1)} async-done(((bf16[16,64,128]{2,1,0:T(8,128)(2,1)}), bf16[16,64,128]{2,1,0:T(8,128)(2,1)S(1)}, u32[]{:S(2)}, u32[]{:S(2)}) %all-to-all-start) | async-done | bytes 262176 | tf_op jit(solution)/shard_map/all_to_all | solution.py:62
  30.8 1.1 fusion.19
  32.2 1.9 %fusion.27 = f32[64,64,128]{2,0,1:T(8,128)S(1)} fusion(f32[4,64,128]{2,1,0:T(8,128)S(1)} %fusion.13, f32[4]{0:T(128)S(1)} %compare_convert_fusion.3, s32[4]{0:T(128)S(1)} %get-tuple-element.14), kind=kOutput, calls=%fused_computation.50 | convolution fusion | flops 25166336 | bytes 2228256 | tf_op jit(solution)/shard_map/tb,bnq->tnq/dot_general | solution.py:47
  34.5 24.7 %all_to_all.40 = bf16[32,64,128]{2,1,0:T(8,128)(2,1)S(1)} all-to-all(bf16[32,64,128]{2,1,0:T(8,128)(2,1)S(1)} %copy.15), channel_id=1, replica_groups=mesh['prow'=16,'pcol'=32] {'pcol'}, dimensions={0} | all-to-all | bytes 1048576 | tf_op jit(solution)/shard_map/all_to_all | solution.py:51
  59.5 0.7 broadcast_in_dim.11
  60.2 5.5 %all-to-all-start.2 = ((bf16[16,64,128]{2,1,0:T(8,128)(2,1)}), bf16[16,64,128]{2,1,0:T(8,128)(2,1)S(1)}, u32[]{:S(2)}, u32[]{:S(2)}) async-start(bf16[16,64,128]{2,1,0:T(8,128)(2,1)} %broadcast_in_dim.11), calls=%async_computation.2 | async-start | bytes 524288 | tf_op jit(solution)/shard_map/all_to_all | solution.py:62
  66.4 14.3 %all-to-all-done.2 = bf16[16,64,128]{2,1,0:T(8,128)(2,1)S(1)} async-done(((bf16[16,64,128]{2,1,0:T(8,128)(2,1)}), bf16[16,64,128]{2,1,0:T(8,128)(2,1)S(1)}, u32[]{:S(2)}, u32[]{:S(2)}) %all-to-all-start.2) | async-done | bytes 262176 | tf_op jit(solution)/shard_map/all_to_all | solution.py:62
  81.5 1.9 %fusion.25 = f32[64,64,128]{2,0,1:T(8,128)S(1)} fusion(f32[4,64,128]{2,1,0:T(8,128)S(1)} %fusion.14, f32[4]{0:T(128)S(1)} %compare_convert_fusion.2, s32[4]{0:T(128)S(1)} %get-tuple-element.13), kind=kOutput, calls=%fused_computation.47 | convolution fusion | flops 25166336 | bytes 2228256 | tf_op jit(solution)/shard_map/tb,bnq->tnq/dot_general | solution.py:47
  84.0 19.0 %all_to_all.41 = bf16[32,64,128]{2,1,0:T(8,128)(2,1)S(1)} all-to-all(bf16[32,64,128]{2,1,0:T(8,128)(2,1)S(1)} %copy.16), channel_id=1, replica_groups=mesh['prow'=16,'pcol'=32] {'pcol'}, dimensions={0} | all-to-all | bytes 1048576 | tf_op jit(solution)/shard_map/all_to_all | solution.py:51
  103.4 0.8 broadcast_in_dim.12
  104.1 5.6 %all-to-all-start.4 = ((bf16[16,64,128]{2,1,0:T(8,128)(2,1)}), bf16[16,64,128]{2,1,0:T(8,128)(2,1)S(1)}, u32[]{:S(2)}, u32[]{:S(2)}) async-start(bf16[16,64,128]{2,1,0:T(8,128)(2,1)} %broadcast_in_dim.12), calls=%async_computation.4 | async-start | bytes 524288 | tf_op jit(solution)/shard_map/all_to_all | solution.py:62
  111.1 13.7 %all-to-all-done.4 = bf16[16,64,128]{2,1,0:T(8,128)(2,1)S(1)} async-done(((bf16[16,64,128]{2,1,0:T(8,128)(2,1)}), bf16[16,64,128]{2,1,0:T(8,128)(2,1)S(1)}, u32[]{:S(2)}, u32[]{:S(2)}) %all-to-all-start.4) | async-done | bytes 262176 | tf_op jit(solution)/shard_map/all_to_all | solution.py:62
  125.4 1.9 %fusion.23 = f32[64,64,128]{2,0,1:T(8,128)S(1)} fusion(f32[4,64,128]{2,1,0:T(8,128)S(1)} %fusion, f32[4]{0:T(128)S(1)} %compare_convert_fusion.1, s32[4]{0:T(128)S(1)} %get-tuple-element.10), kind=kOutput, calls=%fused_computation.44 | convolution fusion | flops 25166336 | bytes 2228256 | tf_op jit(solution)/shard_map/tb,bnq->tnq/dot_general | solution.py:47
  127.7 19.0 %all_to_all.42 = bf16[32,64,128]{2,1,0:T(8,128)(2,1)S(1)} all-to-all(bf16[32,64,128]{2,1,0:T(8,128)(2,1)S(1)} %copy.17), channel_id=1, replica_groups=mesh['prow'=16,'pcol'=32] {'pcol'}, dimensions={0} | all-to-all | bytes 1048576 | tf_op jit(solution)/shard_map/all_to_all | solution.py:56
  147.7 5.7 %all-to-all-start.6 = ((bf16[16,64,128]{2,1,0:T(8,128)(2,1)}), bf16[16,64,128]{2,1,0:T(8,128)(2,1)S(1)}, u32[]{:S(2)}, u32[]{:S(2)}) async-start(bf16[16,64,128]{2,1,0:T(8,128)(2,1)} %broadcast_in_dim.13), calls=%async_computation.6 | async-start | bytes 524288 | tf_op jit(solution)/shard_map/all_to_all | solution.py:62
  154.0 14.3 %all-to-all-done.6 = bf16[16,64,128]{2,1,0:T(8,128)(2,1)S(1)} async-done(((bf16[16,64,128]{2,1,0:T(8,128)(2,1)}), bf16[16,64,128]{2,1,0:T(8,128)(2,1)S(1)}, u32[]{:S(2)}, u32[]{:S(2)}) %all-to-all-start.6) | async-done | bytes 262176 | tf_op jit(solution)/shard_map/all_to_all | solution.py:62
  168.9 1.9 %fusion.21 = f32[64,64,128]{2,0,1:T(8,128)S(1)} fusion(f32[4,64,128]{2,1,0:T(8,128)S(1)} %fusion.1, f32[4]{0:T(128)S(1)} %compare_convert_fusion, s32[4]{0:T(128)S(1)} %get-tuple-element.9), kind=kOutput, calls=%fused_computation.41 | convolution fusion | flops 25166336 | bytes 2228256 | tf_op jit(solution)/shard_map/tb,bnq->tnq/dot_general | solution.py:47
  171.3 19.0 %all_to_all.43 = bf16[32,64,128]{2,1,0:T(8,128)(2,1)S(1)} all-to-all(bf16[32,64,128]{2,1,0:T(8,128)(2,1)S(1)} %copy.18), channel_id=1, replica_groups=mesh['prow'=16,'pcol'=32] {'pcol'}, dimensions={0} | all-to-all | bytes 1048576 | tf_op jit(solution)/shard_map/all_to_all | solution.py:56
  (55 shorter events, 10.6 us)
Async XLA Ops:
  1.7 28.9 %all-to-all-start = ((bf16[16,64,128]{2,1,0:T(8,128)(2,1)}), bf16[16,64,128]{2,1,0:T(8,128)(2,1)S(1)}, u32[]{:S(2)}, u32[]{:S(2)}) async-start(bf16[16,64,128]{2,1,0:T(8,128)(2,1)} %broadcast_in_dim.10), calls=%async_computation | async-start | bytes 524288 | tf_op jit(solution)/shard_map/all_to_all | solution.py:62
  34.2 25.1 %copy-start.1 = (bf16[1,1,3,1,128,128]{5,4,3,2,1,0:T(8,128)(2,1)S(1)}, bf16[1,1,3,1,128,128]{5,4,3,2,1,0:T(8,128)(2,1)}, u32[]{:S(2)}) copy-start(bf16[1,1,3,1,128,128]{5,4,3,2,1,0:T(8,128)(2,1)} %param.14) | copy-start | bytes 294916
  34.2 25.1 %copy-start.3 = (bf16[1,1,3,1,64,128]{5,4,3,2,1,0:T(8,128)(2,1)S(1)}, bf16[1,1,3,1,64,128]{5,4,3,2,1,0:T(8,128)(2,1)}, u32[]{:S(2)}) copy-start(bf16[1,1,3,1,64,128]{5,4,3,2,1,0:T(8,128)(2,1)} %param.13) | copy-start | bytes 147460
  34.3 46.7 %copy-start = (bf16[1,1,2,4,128,128]{5,4,3,2,1,0:T(8,128)(2,1)S(1)}, bf16[1,1,2,4,128,128]{5,4,3,2,1,0:T(8,128)(2,1)}, u32[]{:S(2)}) copy-start(bf16[1,1,2,4,128,128]{5,4,3,2,1,0:T(8,128)(2,1)} %param.16) | copy-start | bytes 786436
  60.2 20.5 %all-to-all-start.2 = ((bf16[16,64,128]{2,1,0:T(8,128)(2,1)}), bf16[16,64,128]{2,1,0:T(8,128)(2,1)S(1)}, u32[]{:S(2)}, u32[]{:S(2)}) async-start(bf16[16,64,128]{2,1,0:T(8,128)(2,1)} %broadcast_in_dim.11), calls=%async_computation.2 | async-start | bytes 524288 | tf_op jit(solution)/shard_map/all_to_all | solution.py:62
  83.5 19.8 %copy-start.2 = (bf16[1,1,3,1,128,128]{5,4,3,2,1,0:T(8,128)(2,1)S(1)}, bf16[1,1,3,1,128,128]{5,4,3,2,1,0:T(8,128)(2,1)}, u32[]{:S(2)}) copy-start(bf16[1,1,3,1,128,128]{5,4,3,2,1,0:T(8,128)(2,1)} %param.15) | copy-start | bytes 294916
  83.7 26.1 %copy-start.5 = (s32[1,1,2]{2,1,0:T(1,128)S(1)}, s32[1,1,2]{2,1,0:T(1,128)}, u32[]{:S(2)}) copy-start(s32[1,1,2]{2,1,0:T(1,128)} %param.25) | copy-start | bytes 28
  83.7 27.3 %copy-start.6 = (s32[1,1,2,4]{3,2,1,0:T(2,128)S(1)}, s32[1,1,2,4]{3,2,1,0:T(2,128)}, u32[]{:S(2)}) copy-start(s32[1,1,2,4]{3,2,1,0:T(2,128)} %param.22) | copy-start | bytes 100
  83.7 27.3 %copy-start.7 = (s32[1,1,2,4]{3,2,1,0:T(2,128)S(1)}, s32[1,1,2,4]{3,2,1,0:T(2,128)}, u32[]{:S(2)}) copy-start(s32[1,1,2,4]{3,2,1,0:T(2,128)} %param.23) | copy-start | bytes 100
  83.8 27.3 %copy-start.4 = (s32[1,1,2,4,128]{4,3,2,1,0:T(4,128)S(1)}, s32[1,1,2,4,128]{4,3,2,1,0:T(4,128)}, u32[]{:S(2)}) copy-start(s32[1,1,2,4,128]{4,3,2,1,0:T(4,128)} %param.24) | copy-start | bytes 12292
  83.8 41.3 %copy-start.8 = (bf16[1,1,2,4,128,128]{5,4,3,2,1,0:T(8,128)(2,1)S(1)}, bf16[1,1,2,4,128,128]{5,4,3,2,1,0:T(8,128)(2,1)}, u32[]{:S(2)}) copy-start(bf16[1,1,2,4,128,128]{5,4,3,2,1,0:T(8,128)(2,1)} %param.21) | copy-start | bytes 786436
  104.1 20.6 %all-to-all-start.4 = ((bf16[16,64,128]{2,1,0:T(8,128)(2,1)}), bf16[16,64,128]{2,1,0:T(8,128)(2,1)S(1)}, u32[]{:S(2)}, u32[]{:S(2)}) async-start(bf16[16,64,128]{2,1,0:T(8,128)(2,1)} %broadcast_in_dim.12), calls=%async_computation.4 | async-start | bytes 524288 | tf_op jit(solution)/shard_map/all_to_all | solution.py:62
  147.7 20.6 %all-to-all-start.6 = ((bf16[16,64,128]{2,1,0:T(8,128)(2,1)}), bf16[16,64,128]{2,1,0:T(8,128)(2,1)S(1)}, u32[]{:S(2)}, u32[]{:S(2)}) async-start(bf16[16,64,128]{2,1,0:T(8,128)(2,1)} %broadcast_in_dim.13), calls=%async_computation.6 | async-start | bytes 524288 | tf_op jit(solution)/shard_map/all_to_all | solution.py:62

commit v2 on v1

v2 whole, which is shorter than its diff:
```python
import jax
import jax.numpy as jnp
from jax import lax
from jax.sharding import Mesh
from jax.sharding import PartitionSpec as P

BF16 = jnp.bfloat16
F32 = jnp.float32
GROUP = ("zl", "core")
SPLIT = 4


def exact_product(operand, inverse):
    return jnp.einsum("qns,qst->qnt", operand, inverse, preferred_element_type=F32).astype(BF16)


def full_product(operand, inverse):
    return jnp.einsum(
        "qns,qst->qnt", operand, inverse.astype(F32), precision=lax.Precision.HIGHEST
    ).astype(BF16)


def moved_columns(tiles, rows):
    extent = tiles.shape[-1]
    table = (rows[..., :, None] == jnp.arange(extent, dtype=rows.dtype)).astype(BF16)
    return jnp.einsum("...sp,...pq->...sq", tiles, table, preferred_element_type=F32).astype(BF16)


def moved_rows(tiles, rows):
    extent = tiles.shape[-1]
    table = (rows[..., None, :] == jnp.arange(extent, dtype=rows.dtype)[:, None]).astype(BF16)
    return jnp.einsum("...qp,...pt->...qt", table, tiles, preferred_element_type=F32).astype(BF16)


def index_rows(source, target, live, extent):
    row = jnp.concatenate([source, target, live[None]]).astype(BF16)
    return jnp.pad(row, (0, extent - row.shape[0]))[None]


def read_index(rows, blocks):
    values = rows.astype(F32).astype(jnp.int32)
    source, target = values[:, :blocks], values[:, blocks : 2 * blocks]
    live = values[:, 2 * blocks : 2 * blocks + 1]
    active = jnp.arange(blocks, dtype=jnp.int32)[None, :] < live
    return source, jnp.where(active, target, -1)


def block_terms(column, tiles, source):
    members = jnp.arange(column.shape[0], dtype=jnp.int32)
    chosen = source[..., None] == members
    picked = jnp.zeros(source.shape + column.shape[2:], BF16)
    for j in range(column.shape[0]):
        here = chosen[..., j][..., None, None]
        picked = jnp.where(here, column[j][None, :, None], picked)
    return jnp.einsum("zcbns,zcbst->zcbnt", picked, tiles, preferred_element_type=F32)


def spread(term_groups, base, row_group):
    total = None
    slots = base + jnp.arange(row_group, dtype=jnp.int32)
    for terms, target in term_groups:
        for core in range(terms.shape[1]):
            for b in range(terms.shape[2]):
                mask = slots[:, None] == target[:, core, b][None, :]
                add = jnp.where(mask[..., None, None], terms[:, core, b][None], 0.0)
                total = add if total is None else total + add
    return total.astype(BF16)


def row_sum(partial):
    targets, pair, rows, extent = partial.shape
    cores = lax.axis_size("core")
    places = targets // cores
    chunks = partial.reshape(places, cores, pair, rows, extent)
    got = lax.all_to_all(chunks, ("x", "y"), 0, 0, tiled=True)
    total = jnp.sum(got.astype(F32), axis=0)
    return jnp.swapaxes(total, 0, 1).reshape(pair * cores, rows, extent)


def gather_column(tiles):
    copies = jnp.broadcast_to(tiles, (lax.axis_size("zh"),) + tiles.shape)
    got = lax.all_to_all(copies, "zh", 0, 0, tiled=True)
    return got.reshape((-1, lax.axis_size("core")) + tiles.shape[1:])


def body(
    right_sides,
    lower_inverse,
    upper_inverse,
    lower_tiles,
    lower_source,
    lower_target,
    lower_rows,
    lower_count,
    upper_tiles,
    upper_source,
    upper_target,
    upper_rows,
    upper_count,
):
    sides = right_sides[0, 0, :, 0]
    low_inv, up_inv = lower_inverse[0, 0, :, 0], upper_inverse[0, 0, :, 0]
    low_tiles, up_tiles = lower_tiles[0, 0], upper_tiles[0, 0]
    low_rows, up_rows = lower_rows[0, 0], upper_rows[0, 0]
    low_source, low_target, low_count = lower_source[0, 0], lower_target[0, 0], lower_count[0, 0]
    up_source, up_target, up_count = upper_source[0, 0], upper_target[0, 0], upper_count[0, 0]
    side_extent, extent = sides.shape[1:]
    blocks = low_tiles.shape[1]
    pair, cores = lax.axis_size("zl"), lax.axis_size("core")
    high = lax.axis_size("zh")
    row_group = lax.axis_size("x") * lax.axis_size("y") * cores
    rows = side_extent // SPLIT
    me = lax.axis_index("zl") * cores + lax.axis_index("core")

    late = jnp.concatenate(
        [
            low_tiles[1].reshape(-1, extent),
            up_tiles.reshape(-1, extent),
            low_inv[0],
            up_inv[0],
            up_inv[1],
            sides[0],
            low_rows[1].astype(BF16),
            up_rows.reshape(-1, extent).astype(BF16),
            index_rows(low_source[1], low_target[1], low_count[1], extent),
            index_rows(up_source[0], up_target[0], up_count[0], extent),
            index_rows(up_source[1], up_target[1], up_count[1], extent),
            jnp.zeros((1, extent), BF16),
        ],
        axis=0,
    )
    late = lax.all_gather(late, GROUP, axis=0)

    def late_tiles(at, number):
        piece = late[:, at : at + number * extent]
        return piece.reshape(pair, cores, number, extent, extent)

    forward_2 = jnp.dot(sides[2], low_inv[2], preferred_element_type=F32).astype(BF16)
    slices = forward_2.reshape(1, SPLIT, rows, extent)
    copies = jnp.broadcast_to(slices, (high,) + slices.shape[1:]).reshape(-1, rows, extent)
    column = lax.all_to_all(copies, ("zh", "zl", "core"), 0, 0, tiled=True)
    column = column.reshape(-1, cores, rows, extent)

    early = jnp.concatenate(
        [
            moved_columns(low_tiles[0], low_rows[0]).reshape(-1, extent),
            low_inv[1],
            sides[1],
            index_rows(low_source[0], low_target[0], low_count[0], extent),
            jnp.zeros((15, extent), BF16),
        ],
        axis=0,
    )
    early = lax.all_gather(early, GROUP, axis=0)
    at = blocks * extent
    tiles_l0 = early[:, :at].reshape(pair, cores, blocks, extent, extent)
    inv_l1 = early[:, at : at + extent]
    sides_1 = early[:, at + extent : at + extent + side_extent]
    index_l0 = early[:, at + extent + side_extent]

    at = blocks * extent
    raw_l1, raw_u0, raw_u1 = (late_tiles(g * at, blocks) for g in range(3))
    at = 3 * at
    inv_l0, inv_u0, inv_u1 = (late[:, at + i * extent : at + (i + 1) * extent] for i in range(3))
    at = at + 3 * extent
    sides_0 = late[:, at : at + side_extent]
    at = at + side_extent
    table = late[:, at : at + 3 * blocks].reshape(pair, cores, 3, blocks, extent)
    at = at + 3 * blocks
    index_l1, index_u0, index_u1 = (late[:, at + i] for i in range(3))
    table = table.astype(F32).astype(jnp.int32)
    tiles_l1 = moved_columns(raw_l1, table[:, :, 0])
    tiles_u0 = moved_rows(raw_u0, table[:, :, 1])
    tiles_u1 = moved_rows(raw_u1, table[:, :, 2])

    def indices(packed):
        source, target = read_index(packed, blocks)
        return source.reshape(pair, cores, blocks), target.reshape(pair, cores, blocks)

    def own_rows(tile):
        return lax.dynamic_slice_in_dim(tile, me * rows, rows, axis=1).astype(F32)

    source_l0, target_l0 = indices(index_l0)
    terms_l0 = block_terms(column, tiles_l0, source_l0)
    lower_sum = row_sum(spread([(terms_l0, target_l0)], row_group, row_group))
    forward_1 = full_product(own_rows(sides_1) - lower_sum, inv_l1)
    column = gather_column(forward_1)
    source_l1, target_l1 = indices(index_l1)
    terms_l1 = block_terms(column, tiles_l1, source_l1)
    lower_sum = row_sum(spread([(terms_l0, target_l0), (terms_l1, target_l1)], 0, row_group))
    forward_0 = full_product(own_rows(sides_0) - lower_sum, inv_l0)

    solution_0 = exact_product(forward_0, inv_u0)
    column = gather_column(solution_0)
    source_u0, target_u0 = indices(index_u0)
    terms_u0 = block_terms(column, tiles_u0, source_u0)
    upper_sum = row_sum(spread([(terms_u0, target_u0)], 0, row_group))
    solution_1 = full_product(forward_1.astype(F32) - upper_sum, inv_u1)
    column = gather_column(solution_1)

    done = lax.all_gather(jnp.stack([solution_0, solution_1], axis=1), GROUP, axis=0)
    done = lax.dynamic_index_in_dim(done, me, axis=1, keepdims=False)
    done = jnp.swapaxes(done, 0, 1).reshape(2, side_extent, extent)

    source_u1, target_u1 = indices(index_u1)
    terms_u1 = block_terms(column, tiles_u1, source_u1)
    partial = spread([(terms_u0, target_u0), (terms_u1, target_u1)], row_group, row_group)
    chunks = jnp.swapaxes(partial, 0, 1).reshape(-1, rows, extent)
    got = lax.all_to_all(chunks, ("zl", "x", "y", "core"), 0, 0, tiled=True)
    got = got.reshape(pair, row_group // cores, cores, rows, extent)
    upper_sum = jnp.sum(got.astype(F32), axis=1).reshape(side_extent, extent)
    operand = forward_2.astype(F32) - upper_sum
    solution_2 = full_product(operand[None], up_inv[2][None])
    return jnp.concatenate([done, solution_2], axis=0)[None, None, :, None]


def solution(mesh):
    z_extent = mesh.shape["prow"]
    grid = mesh.devices.reshape(z_extent // 2, 2, 4, 4, 2)
    split_mesh = Mesh(grid, ("zh", "zl", "x", "y", "core"))
    row, col = ("zh", "zl"), ("x", "y", "core")
    ranks = (6, 6, 6, 6, 4, 4, 5, 3, 6, 4, 4, 5, 3)
    placed = tuple(P(row, col, *([None] * (rank - 2))) for rank in ranks)
    return jax.shard_map(
        body,
        mesh=split_mesh,
        in_specs=placed,
        out_specs=P(row, col, None, None, None, None),
        check_vma=False,
    )
```

time: 192 us -> 220 us (1.15)
  blocking collectives: 81.6 us -> 22.6 us
  starting transfers between devices: 32.6 us -> 59.5 us
  other arithmetic: 4 us -> 22.7 us
  local copies, waits for them, and re-layouts: 8.22 us -> 24.3 us
  waiting for transfers between devices: 51.3 us -> 67 us
  between operations: 0.39 us -> 14.4 us
  matrix products: 13.1 us -> 7.53 us
    all_to_all x4 -> x0, blocking collectives: 81.6 us -> none  [the longest x2 43.7 us: lower_total(): lax.all_to_all(partial_value.astype(jnp.bfloat16), 'pcol', 0, 0, tiled=True)]
    all_to_all x4 -> x8, starting transfers between devices: 32.6 us -> 59.4 us  [the longest x3 17 us: gather_column(): got = lax.all_to_all(copies, 'zh', 0, 0, tiled=True)]
    all_gather x0 -> x2, blocking collectives: none -> 22.6 us  [the longest x1 15.4 us: body(): early = lax.all_gather(early, GROUP, axis=0)]
    all_gather x0 -> x1, waiting for transfers between devices: none -> 9.66 us  [body(): late = lax.all_gather(late, GROUP, axis=0)]
    concatenate x0 -> x2, local copies, waits for them, and re-layouts: none -> 8.14 us  [the longest x1 7.96 us: body(): jnp.concatenate([low_tiles[1].reshape(-1, extent), up_tiles.reshape(-1, e...]
    convert_element_type x4 -> x10, other arithmetic: 2.57 us -> 9.63 us  [the longest x4 7.5 us: spread(): return total.astype(BF16)]
    all_to_all x4 -> x8, waiting for transfers between devices: 51.3 us -> 57.3 us  [the longest x3 37.1 us: gather_column(): got = lax.all_to_all(copies, 'zh', 0, 0, tiled=True)]
    dot_general x20 -> x11, matrix products: 13.1 us -> 7.53 us  [the longest x4 4.65 us: block_terms(): jnp.einsum('zcbns,zcbst->zcbnt', picked, tiles, preferred_element_type=F32)]
  transfers between devices with their start and end apart: 4 -> 9, of which waited for: 4 -> 8; matrix products, arithmetic and copies ran while one was open for 4% -> 6% of each run, Pallas kernels for 0% -> 0%
where the time goes in v2:
time: 220 us; the launch traced here: 218 us
  waiting for transfers between devices  67 us (30%)
  starting transfers between devices  59.5 us (27%)
  local copies, waits for them, and re-layouts  24.3 us (11%)
  other arithmetic  22.7 us (10%)
  blocking collectives  22.6 us (10%)
  between operations  14.4 us (7%)
  matrix products  7.53 us (3%)
    all_to_all x3, waiting for transfers between devices, gather_column(): got = lax.all_to_all(copies, 'zh', 0, 0, tiled=True)  37.1 us
    all_to_all x3, waiting for transfers between devices, row_sum(): got = lax.all_to_all(chunks, ('x', 'y'), 0, 0, tiled=True)  17.5 us
    all_to_all x3, starting transfers between devices, gather_column(): got = lax.all_to_all(copies, 'zh', 0, 0, tiled=True)  17 us
    all_to_all x1, starting transfers between devices, body(): column = lax.all_to_all(copies, ('zh', 'zl', 'core'), 0, 0, tiled=True)  16.8 us
    all_gather x1, blocking collectives, body(): early = lax.all_gather(early, GROUP, axis=0)  15.4 us
    all_to_all x3, starting transfers between devices, row_sum(): got = lax.all_to_all(chunks, ('x', 'y'), 0, 0, tiled=True)  13.8 us
    all_to_all x1, starting transfers between devices, body(): got = lax.all_to_all(chunks, ('zl', 'x', 'y', 'core'), 0, 0, tiled=True)  11.9 us
    all_gather x1, waiting for transfers between devices, body(): late = lax.all_gather(late, GROUP, axis=0)  9.66 us
  transfers between devices with their start and end apart: 9, of which 8 were waited for; matrix products, arithmetic and copies ran while one was open for 6% of the time, Pallas kernels for 0%

profile of v2, /device:TPU:1, one launch (start us, length us, event | category | flops | bytes accessed | tf_op | source)
XLA Modules:
  0.0 217.9 jit_solution(904954249450004403)
XLA Ops:
  17.8 8.0 %concatenate.28 = bf16[2000,128]{1,0:T(8,128)(2,1)} concatenate(bf16[512,128]{1,0:T(8,128)(2,1)S(1)} %bitcast.523, bf16[1024,128]{1,0:T(8,128)(2,1)} %bitcast.531, bf16[128,128]{1,0:T(8,128)(2,1)S(1)} %get-tuple-element.140, bf16[128,128]{1,0:T(8,128)(2,1)S(1)} %get-tuple-element.294, bf16[128,128]{1,0:T(8,128)(2,1)S(1)} %get-tuple-element.295, ...), dimensions={0} | concatenate | bytes 1024000 | tf_op jit(solution)/shard_map/concatenate | solution.py:115
  27.4 16.8 %all-to-all-start = ((bf16[32,16,128]{2,1,0:T(8,128)(2,1)}), bf16[32,16,128]{2,1,0:T(8,128)(2,1)S(1)}, u32[]{:S(2)}, u32[]{:S(2)}) async-start(bf16[32,16,128]{2,1,0:T(8,128)(2,1)} %bitcast.39), calls=%async_computation | async-start | bytes 262144 | tf_op jit(solution)/shard_map/all_to_all | solution.py:141
  45.4 15.4 %all-gather.1 = bf16[2880,128]{1,0:T(8,128)(2,1)S(1)} all-gather(bf16[720,128]{1,0:T(8,128)(2,1)S(1)} %concatenate.30), channel_id=3, replica_groups=mesh['zh'=8,'zl'=2,'x'=4,'y'=4,'core'=2] {'zl','core'}, dimensions={0}, use_global_device_ids=true | all-gather | bytes 921600 | tf_op jit(solution)/shard_map/all_gather | solution.py:154
  63.5 9.7 %all-gather.5.cloned.1.call-done = bf16[8000,128]{1,0:T(8,128)(2,1)} async-done(((bf16[2000,128]{1,0:T(8,128)(2,1)}), bf16[8000,128]{1,0:T(8,128)(2,1)}) %all-gather.5.cloned.1.call-update) | async-done | bytes 2048016 | tf_op jit(solution)/shard_map/all_gather | solution.py:132
  79.8 6.8 %all-to-all-start.1 = ((bf16[16,2,2,16,128]{4,3,2,1,0:T(8,128)(2,1)}), bf16[16,2,2,16,128]{4,3,2,1,0:T(8,128)(2,1)S(1)}, u32[]{:S(2)}, u32[]{:S(2)}) async-start(bf16[16,2,2,16,128]{4,3,2,1,0:T(8,128)(2,1)} %add_convert_fusion.2), calls=%async_computation.1 | async-start | bytes 524288 | tf_op jit(solution)/shard_map/all_to_all | solution.py:75
  88.2 1.6 broadcast_compare_fusion.7
  89.9 4.2 %all-to-all-done.1 = bf16[16,2,2,16,128]{4,3,2,1,0:T(8,128)(2,1)S(1)} async-done(((bf16[16,2,2,16,128]{4,3,2,1,0:T(8,128)(2,1)}), bf16[16,2,2,16,128]{4,3,2,1,0:T(8,128)(2,1)S(1)}, u32[]{:S(2)}, u32[]{:S(2)}) %all-to-all-start.1) | async-done | bytes 262176 | tf_op jit(solution)/shard_map/all_to_all | solution.py:75
  95.0 10.3 %all-to-all-start.2 = ((bf16[8,4,16,128]{3,2,1,0:T(8,128)(2,1)}), bf16[8,4,16,128]{3,2,1,0:T(8,128)(2,1)S(1)}, u32[]{:S(2)}, u32[]{:S(2)}) async-start(bf16[8,4,16,128]{3,2,1,0:T(8,128)(2,1)} %broadcast_in_dim.1733), calls=%async_computation.2 | async-start | bytes 262144 | tf_op jit(solution)/shard_map/all_to_all | solution.py:82
  107.1 12.0 %all-to-all-done.2 = bf16[8,4,16,128]{3,2,1,0:T(8,128)(2,1)S(1)} async-done(((bf16[8,4,16,128]{3,2,1,0:T(8,128)(2,1)}), bf16[8,4,16,128]{3,2,1,0:T(8,128)(2,1)S(1)}, u32[]{:S(2)}, u32[]{:S(2)}) %all-to-all-start.2) | async-done | bytes 131104 | tf_op jit(solution)/shard_map/all_to_all | solution.py:82
  119.7 1.7 fusion
  121.7 2.4 %add_convert_fusion.1 = bf16[16,2,2,16,128]{4,3,2,1,0:T(8,128)(2,1)} fusion(f32[2,16,128]{2,1,0:T(8,128)S(1)} %get-tuple-element.92, f32[2,16,128]{2,1,0:T(8,128)S(1)} %get-tuple-element.93, f32[2,16,128]{2,1,0:T(8,128)S(1)} %get-tuple-element.94, f32[2,16,128]{2,1,0:T(8,128)S(1)} %get-tuple-element.95, f32[2,16,128]{2,1,0:T(8,128)S(1)} %get-tuple-element.96, ...), kind=kLoop, calls=%fused_computation.55 | loop fusion | flops 4194304 | bytes 525312 | tf_op jit(solution)/shard_map/convert_element_type | solution.py:67
  124.1 3.5 %all-to-all-start.3 = ((bf16[16,2,2,16,128]{4,3,2,1,0:T(8,128)(2,1)}), bf16[16,2,2,16,128]{4,3,2,1,0:T(8,128)(2,1)S(1)}, u32[]{:S(2)}, u32[]{:S(2)}) async-start(bf16[16,2,2,16,128]{4,3,2,1,0:T(8,128)(2,1)} %add_convert_fusion.1), calls=%async_computation.3 | async-start | bytes 524288 | tf_op jit(solution)/shard_map/all_to_all | solution.py:75
  128.4 6.5 %all-to-all-done.3 = bf16[16,2,2,16,128]{4,3,2,1,0:T(8,128)(2,1)S(1)} async-done(((bf16[16,2,2,16,128]{4,3,2,1,0:T(8,128)(2,1)}), bf16[16,2,2,16,128]{4,3,2,1,0:T(8,128)(2,1)S(1)}, u32[]{:S(2)}, u32[]{:S(2)}) %all-to-all-start.3) | async-done | bytes 262176 | tf_op jit(solution)/shard_map/all_to_all | solution.py:75
  136.0 3.4 %all-to-all-start.4 = ((bf16[8,4,16,128]{3,2,1,0:T(8,128)(2,1)}), bf16[8,4,16,128]{3,2,1,0:T(8,128)(2,1)S(1)}, u32[]{:S(2)}, u32[]{:S(2)}) async-start(bf16[8,4,16,128]{3,2,1,0:T(8,128)(2,1)} %broadcast_in_dim.1822), calls=%async_computation.4 | async-start | bytes 262144 | tf_op jit(solution)/shard_map/all_to_all | solution.py:82
  139.7 13.6 %all-to-all-done.4 = bf16[8,4,16,128]{3,2,1,0:T(8,128)(2,1)S(1)} async-done(((bf16[8,4,16,128]{3,2,1,0:T(8,128)(2,1)}), bf16[8,4,16,128]{3,2,1,0:T(8,128)(2,1)S(1)}, u32[]{:S(2)}, u32[]{:S(2)}) %all-to-all-start.4) | async-done | bytes 131104 | tf_op jit(solution)/shard_map/all_to_all | solution.py:82
  153.4 1.6 fusion.1
  156.5 3.5 %all-to-all-start.5 = ((bf16[16,2,2,16,128]{4,3,2,1,0:T(8,128)(2,1)}), bf16[16,2,2,16,128]{4,3,2,1,0:T(8,128)(2,1)S(1)}, u32[]{:S(2)}, u32[]{:S(2)}) async-start(bf16[16,2,2,16,128]{4,3,2,1,0:T(8,128)(2,1)} %add_convert_fusion), calls=%async_computation.5 | async-start | bytes 524288 | tf_op jit(solution)/shard_map/all_to_all | solution.py:75
  160.5 6.8 %all-to-all-done.5 = bf16[16,2,2,16,128]{4,3,2,1,0:T(8,128)(2,1)S(1)} async-done(((bf16[16,2,2,16,128]{4,3,2,1,0:T(8,128)(2,1)}), bf16[16,2,2,16,128]{4,3,2,1,0:T(8,128)(2,1)S(1)}, u32[]{:S(2)}, u32[]{:S(2)}) %all-to-all-start.5) | async-done | bytes 262176 | tf_op jit(solution)/shard_map/all_to_all | solution.py:75
  168.3 3.4 %all-to-all-start.6 = ((bf16[8,4,16,128]{3,2,1,0:T(8,128)(2,1)}), bf16[8,4,16,128]{3,2,1,0:T(8,128)(2,1)S(1)}, u32[]{:S(2)}, u32[]{:S(2)}) async-start(bf16[8,4,16,128]{3,2,1,0:T(8,128)(2,1)} %broadcast_in_dim.1936), calls=%async_computation.6 | async-start | bytes 262144 | tf_op jit(solution)/shard_map/all_to_all | solution.py:82
  173.2 11.5 %all-to-all-done.6 = bf16[8,4,16,128]{3,2,1,0:T(8,128)(2,1)S(1)} async-done(((bf16[8,4,16,128]{3,2,1,0:T(8,128)(2,1)}), bf16[8,4,16,128]{3,2,1,0:T(8,128)(2,1)S(1)}, u32[]{:S(2)}, u32[]{:S(2)}) %all-to-all-start.6) | async-done | bytes 131104 | tf_op jit(solution)/shard_map/all_to_all | solution.py:82
  185.4 2.4 %fusion.5 = bf16[64,16,128]{2,1,0:T(8,128)(2,1)} fusion(f32[2,16,128]{2,1,0:T(8,128)S(1)} %get-tuple-element.44, f32[2,16,128]{2,1,0:T(8,128)S(1)} %get-tuple-element.45, f32[2,16,128]{2,1,0:T(8,128)S(1)} %get-tuple-element.46, f32[2,16,128]{2,1,0:T(8,128)S(1)} %get-tuple-element.47, f32[2,16,128]{2,1,0:T(8,128)S(1)} %get-tuple-element.48, ...), kind=kLoop, calls=%fused_computation.20 | loop fusion | flops 4194304 | bytes 525312 | tf_op jit(solution)/shard_map/convert_element_type | solution.py:67
  187.7 11.9 %all-to-all-start.7 = ((bf16[64,16,128]{2,1,0:T(8,128)(2,1)}), bf16[64,16,128]{2,1,0:T(8,128)(2,1)S(1)}, u32[]{:S(2)}, u32[]{:S(2)}) async-start(bf16[64,16,128]{2,1,0:T(8,128)(2,1)} %fusion.5), calls=%async_computation.7 | async-start | bytes 524288 | tf_op jit(solution)/shard_map/all_to_all | solution.py:209
  199.6 7.2 %all-gather.2 = bf16[16,2,16,128]{3,2,0,1:T(8,128)(2,1)S(1)} all-gather(bf16[4,2,16,128]{3,2,0,1:T(8,128)(2,1)S(1)} %pad_maximum_fusion), channel_id=4, replica_groups=mesh['zh'=8,'zl'=2,'x'=4,'y'=4,'core'=2] {'zl','core'}, dimensions={0}, use_global_device_ids=true | all-gather | bytes 163840 | tf_op jit(solution)/shard_map/all_gather | solution.py:201
  206.8 2.7 %all-to-all-done.7 = bf16[64,16,128]{2,1,0:T(8,128)(2,1)S(1)} async-done(((bf16[64,16,128]{2,1,0:T(8,128)(2,1)}), bf16[64,16,128]{2,1,0:T(8,128)(2,1)S(1)}, u32[]{:S(2)}, u32[]{:S(2)}) %all-to-all-start.7) | async-done | bytes 262176 | tf_op jit(solution)/shard_map/all_to_all | solution.py:209
  (201 shorter events, 36.8 us)
Async XLA Ops:
  6.5 38.4 %copy-start.1 = (bf16[1,1,2,4,128,128]{5,4,3,2,1,0:T(8,128)(2,1)S(1)}, bf16[1,1,2,4,128,128]{5,4,3,2,1,0:T(8,128)(2,1)}, u32[]{:S(2)}) copy-start(bf16[1,1,2,4,128,128]{5,4,3,2,1,0:T(8,128)(2,1)} %param.16) | copy-start | bytes 786436
  6.5 66.7 %all-gather.5.cloned.1.call-start = ((), (), s32[]{:S(2)}) async-start(), calls=%async_computation.8 | async-start | bytes 2560000 | tf_op jit(solution)/shard_map/all_gather | solution.py:132
  27.4 35.4 %all-to-all-start = ((bf16[32,16,128]{2,1,0:T(8,128)(2,1)}), bf16[32,16,128]{2,1,0:T(8,128)(2,1)S(1)}, u32[]{:S(2)}, u32[]{:S(2)}) async-start(bf16[32,16,128]{2,1,0:T(8,128)(2,1)} %bitcast.39), calls=%async_computation | async-start | bytes 262144 | tf_op jit(solution)/shard_map/all_to_all | solution.py:141
  73.2 32.8 %copy-start = (bf16[8000,128]{1,0:T(8,128)(2,1)S(1)}, bf16[8000,128]{1,0:T(8,128)(2,1)}, u32[]{:S(2)}) copy-start(bf16[8000,128]{1,0:T(8,128)(2,1)} %all-gather.5.cloned.1.call-done) | copy-start | bytes 6144004
  76.6 28.7 %copy-start.26 = (s32[2]{0:T(128)}, s32[2]{0:T(128)S(1)}, u32[]{:S(2)}) copy-start(s32[2]{0:T(128)S(1)} %get-tuple-element.13) | copy-start | bytes 28
  76.7 28.7 %copy-start.34 = (s32[2]{0:T(128)}, s32[2]{0:T(128)S(1)}, u32[]{:S(2)}) copy-start(s32[2]{0:T(128)S(1)} %get-tuple-element.17) | copy-start | bytes 28
  76.7 28.7 %copy-start.36 = (s32[2]{0:T(128)}, s32[2]{0:T(128)S(1)}, u32[]{:S(2)}) copy-start(s32[2]{0:T(128)S(1)} %get-tuple-element.18) | copy-start | bytes 28
  76.7 28.7 %copy-start.38 = (s32[2]{0:T(128)}, s32[2]{0:T(128)S(1)}, u32[]{:S(2)}) copy-start(s32[2]{0:T(128)S(1)} %get-tuple-element.19) | copy-start | bytes 28
  76.7 28.7 %copy-start.40 = (s32[2]{0:T(128)}, s32[2]{0:T(128)S(1)}, u32[]{:S(2)}) copy-start(s32[2]{0:T(128)S(1)} %get-tuple-element.20) | copy-start | bytes 28
  79.8 14.3 %all-to-all-start.1 = ((bf16[16,2,2,16,128]{4,3,2,1,0:T(8,128)(2,1)}), bf16[16,2,2,16,128]{4,3,2,1,0:T(8,128)(2,1)S(1)}, u32[]{:S(2)}, u32[]{:S(2)}) async-start(bf16[16,2,2,16,128]{4,3,2,1,0:T(8,128)(2,1)} %add_convert_fusion.2), calls=%async_computation.1 | async-start | bytes 524288 | tf_op jit(solution)/shard_map/all_to_all | solution.py:75
  95.0 24.0 %all-to-all-start.2 = ((bf16[8,4,16,128]{3,2,1,0:T(8,128)(2,1)}), bf16[8,4,16,128]{3,2,1,0:T(8,128)(2,1)S(1)}, u32[]{:S(2)}, u32[]{:S(2)}) async-start(bf16[8,4,16,128]{3,2,1,0:T(8,128)(2,1)} %broadcast_in_dim.1733), calls=%async_computation.2 | async-start | bytes 262144 | tf_op jit(solution)/shard_map/all_to_all | solution.py:82
  119.7 19.9 %copy-start.24 = (s32[2,2,4,128]{3,1,0,2:T(2,128)S(1)}, s32[2,2,4,128]{3,1,0,2:T(2,128)}, u32[]{:S(2)}) copy-start(s32[2,2,4,128]{3,1,0,2:T(2,128)} %get-tuple-element.147) | copy-start | bytes 24580
  124.1 10.9 %all-to-all-start.3 = ((bf16[16,2,2,16,128]{4,3,2,1,0:T(8,128)(2,1)}), bf16[16,2,2,16,128]{4,3,2,1,0:T(8,128)(2,1)S(1)}, u32[]{:S(2)}, u32[]{:S(2)}) async-start(bf16[16,2,2,16,128]{4,3,2,1,0:T(8,128)(2,1)} %add_convert_fusion.1), calls=%async_computation.3 | async-start | bytes 524288 | tf_op jit(solution)/shard_map/all_to_all | solution.py:75
  127.6 27.4 %copy-start.2 = (pred[16,2,2]{2,1,0:T(4,128)(4,1)S(1)}, pred[16,2,2]{2,1,0:T(4,128)(4,1)}, u32[]{:S(2)}) copy-start(pred[16,2,2]{2,1,0:T(4,128)(4,1)} %get-tuple-element.233) | copy-start | bytes 196
  127.6 27.4 %copy-start.3 = (pred[16,2,2]{2,1,0:T(4,128)(4,1)S(1)}, pred[16,2,2]{2,1,0:T(4,128)(4,1)}, u32[]{:S(2)}) copy-start(pred[16,2,2]{2,1,0:T(4,128)(4,1)} %get-tuple-element.212) | copy-start | bytes 196
  127.6 27.4 %copy-start.4 = (pred[16,2,2]{2,1,0:T(4,128)(4,1)S(1)}, pred[16,2,2]{2,1,0:T(4,128)(4,1)}, u32[]{:S(2)}) copy-start(pred[16,2,2]{2,1,0:T(4,128)(4,1)} %get-tuple-element.227) | copy-start | bytes 196
  127.6 27.4 %copy-start.5 = (pred[16,2,2]{2,1,0:T(4,128)(4,1)S(1)}, pred[16,2,2]{2,1,0:T(4,128)(4,1)}, u32[]{:S(2)}) copy-start(pred[16,2,2]{2,1,0:T(4,128)(4,1)} %get-tuple-element.228) | copy-start | bytes 196
  127.7 27.4 %copy-start.6 = (pred[16,2,2]{2,1,0:T(4,128)(4,1)S(1)}, pred[16,2,2]{2,1,0:T(4,128)(4,1)}, u32[]{:S(2)}) copy-start(pred[16,2,2]{2,1,0:T(4,128)(4,1)} %get-tuple-element.229) | copy-start | bytes 196
  136.0 17.2 %all-to-all-start.4 = ((bf16[8,4,16,128]{3,2,1,0:T(8,128)(2,1)}), bf16[8,4,16,128]{3,2,1,0:T(8,128)(2,1)S(1)}, u32[]{:S(2)}, u32[]{:S(2)}) async-start(bf16[8,4,16,128]{3,2,1,0:T(8,128)(2,1)} %broadcast_in_dim.1822), calls=%async_computation.4 | async-start | bytes 262144 | tf_op jit(solution)/shard_map/all_to_all | solution.py:82
  153.3 18.3 %copy-start.27 = (s32[2]{0:T(128)S(1)}, s32[2]{0:T(128)}, u32[]{:S(2)}) copy-start(s32[2]{0:T(128)} %copy-done.26) | copy-start | bytes 28
  153.4 19.8 %copy-start.23 = (s32[2,2,4,128]{3,1,0,2:T(2,128)S(1)}, s32[2,2,4,128]{3,1,0,2:T(2,128)}, u32[]{:S(2)}) copy-start(s32[2,2,4,128]{3,1,0,2:T(2,128)} %get-tuple-element.146) | copy-start | bytes 24580
  156.5 10.8 %all-to-all-start.5 = ((bf16[16,2,2,16,128]{4,3,2,1,0:T(8,128)(2,1)}), bf16[16,2,2,16,128]{4,3,2,1,0:T(8,128)(2,1)S(1)}, u32[]{:S(2)}, u32[]{:S(2)}) async-start(bf16[16,2,2,16,128]{4,3,2,1,0:T(8,128)(2,1)} %add_convert_fusion), calls=%async_computation.5 | async-start | bytes 524288 | tf_op jit(solution)/shard_map/all_to_all | solution.py:75
  168.3 16.5 %all-to-all-start.6 = ((bf16[8,4,16,128]{3,2,1,0:T(8,128)(2,1)}), bf16[8,4,16,128]{3,2,1,0:T(8,128)(2,1)S(1)}, u32[]{:S(2)}, u32[]{:S(2)}) async-start(bf16[8,4,16,128]{3,2,1,0:T(8,128)(2,1)} %broadcast_in_dim.1936), calls=%async_computation.6 | async-start | bytes 262144 | tf_op jit(solution)/shard_map/all_to_all | solution.py:82
  187.7 21.7 %all-to-all-start.7 = ((bf16[64,16,128]{2,1,0:T(8,128)(2,1)}), bf16[64,16,128]{2,1,0:T(8,128)(2,1)S(1)}, u32[]{:S(2)}, u32[]{:S(2)}) async-start(bf16[64,16,128]{2,1,0:T(8,128)(2,1)} %fusion.5), calls=%async_computation.7 | async-start | bytes 524288 | tf_op jit(solution)/shard_map/all_to_all | solution.py:209
  (27 other events, 409.8 us)
Sparse Core Ops, SparseCore 0:
  26.0 47.2 all-gather.4

commit v3 on v2

v3 whole, which is shorter than its diff:
```python
import jax
import jax.numpy as jnp
from jax import lax
from jax.sharding import Mesh
from jax.sharding import PartitionSpec as P

BF16 = jnp.bfloat16
F32 = jnp.float32
GROUP = ("zl", "core")
SPLIT = 4
NOWHERE = 255


def exact_product(operand, inverse):
    return jnp.einsum("qns,qst->qnt", operand, inverse, preferred_element_type=F32).astype(BF16)


def full_product(operand, inverse):
    return jnp.einsum(
        "qns,qst->qnt", operand, inverse.astype(F32), precision=lax.Precision.HIGHEST
    ).astype(BF16)


def moved_columns(tiles, rows):
    extent = tiles.shape[-1]
    table = (rows[..., :, None] == jnp.arange(extent, dtype=rows.dtype)).astype(BF16)
    return jnp.einsum("...sp,...pq->...sq", tiles, table, preferred_element_type=F32).astype(BF16)


def moved_rows(tiles, rows):
    extent = tiles.shape[-1]
    table = (rows[..., None, :] == jnp.arange(extent, dtype=rows.dtype)[:, None]).astype(BF16)
    return jnp.einsum("...qp,...pt->...qt", table, tiles, preferred_element_type=F32).astype(BF16)


def gather_group(pieces):
    packed = jnp.concatenate(pieces, axis=0) if len(pieces) > 1 else pieces[0]
    return lax.all_gather(packed, GROUP, axis=0)


def beside(exchange, operand, pieces):
    packed = jnp.concatenate(pieces, axis=0) if len(pieces) > 1 else pieces[0]
    operand, packed = lax.optimization_barrier((operand, packed))
    gathered = lax.all_gather(packed, GROUP, axis=0)
    return lax.optimization_barrier((exchange(operand), gathered))


def index_rows(source, target, live):
    active = jnp.arange(source.shape[1], dtype=jnp.int32)[None, :] < live[:, None]
    return jnp.concatenate([source, jnp.where(active, target, NOWHERE)], axis=1)


def block_terms(column, tiles, source):
    picked = jnp.zeros(source.shape[:3] + column.shape[2:], BF16)
    for j in range(column.shape[0]):
        here = (source == j)[..., None, :]
        picked = jnp.where(here, column[j][None, :, None], picked)
    return jnp.einsum("zcbns,zcbst->zcbnt", picked, tiles, preferred_element_type=F32)


def spread(term_groups, base, row_group):
    total = None
    slots = (base + jnp.arange(row_group, dtype=jnp.int32)).astype(BF16)
    for terms, target in term_groups:
        for core in range(terms.shape[1]):
            for b in range(terms.shape[2]):
                mask = slots[:, None, None] == target[:, core, b][None]
                add = jnp.where(mask[:, :, None], terms[:, core, b][None], 0.0)
                total = add if total is None else total + add
    return total.astype(BF16)


def row_exchange(partial):
    targets, pair, rows, extent = partial.shape
    cores = lax.axis_size("core")
    chunks = partial.reshape(targets // cores, cores, pair, rows, extent)
    return lax.all_to_all(chunks, ("x", "y"), 0, 0, tiled=True)


def row_sum(got):
    total = jnp.sum(got.astype(F32), axis=0)
    return jnp.swapaxes(total, 0, 1).reshape((-1,) + total.shape[2:])


def gather_column(tiles):
    copies = jnp.broadcast_to(tiles, (lax.axis_size("zh"),) + tiles.shape)
    got = lax.all_to_all(copies, "zh", 0, 0, tiled=True)
    return got.reshape((-1, lax.axis_size("core")) + tiles.shape[1:])


def body(
    right_sides,
    lower_inverse,
    upper_inverse,
    lower_tiles,
    lower_source,
    lower_target,
    lower_rows,
    lower_count,
    upper_tiles,
    upper_source,
    upper_target,
    upper_rows,
    upper_count,
):
    sides = right_sides[0, 0, :, 0]
    low_inv, up_inv = lower_inverse[0, 0, :, 0], upper_inverse[0, 0, :, 0]
    low_tiles, up_tiles = lower_tiles[0, 0], upper_tiles[0, 0]
    low_rows, up_rows = lower_rows[0, 0], upper_rows[0, 0]
    low_source, low_target, low_count = lower_source[0, 0], lower_target[0, 0], lower_count[0, 0]
    up_source, up_target, up_count = upper_source[0, 0], upper_target[0, 0], upper_count[0, 0]
    side_extent, extent = sides.shape[1:]
    blocks = low_tiles.shape[1]
    pair, cores = lax.axis_size("zl"), lax.axis_size("core")
    high = lax.axis_size("zh")
    row_group = lax.axis_size("x") * lax.axis_size("y") * cores
    rows = side_extent // SPLIT
    me = lax.axis_index("zl") * cores + lax.axis_index("core")

    forward_2 = jnp.dot(sides[2], low_inv[2], preferred_element_type=F32).astype(BF16)
    slices = forward_2.reshape(1, SPLIT, rows, extent)
    copies = jnp.broadcast_to(slices, (high,) + slices.shape[1:]).reshape(-1, rows, extent)
    column = lax.all_to_all(copies, ("zh", "zl", "core"), 0, 0, tiled=True)
    column = column.reshape(-1, cores, rows, extent)

    tile_rows = blocks * extent

    def parts(gathered, *sizes):
        ends = [sum(sizes[: i + 1]) for i in range(len(sizes))]
        return [gathered[:, end - size : end] for end, size in zip(ends, sizes)]

    def as_tiles(piece):
        return piece.reshape(pair, cores, blocks, extent, extent)

    index = jnp.concatenate(
        [
            index_rows(low_source, low_target, low_count),
            index_rows(up_source, up_target, up_count),
        ],
        axis=0,
    ).astype(BF16)
    index = jnp.broadcast_to(index.reshape(-1, 1), (4 * 2 * blocks, extent))
    moved = moved_columns(low_tiles, low_rows).reshape(2, tile_rows, extent)
    moved_up = moved_rows(up_tiles, up_rows).reshape(2, tile_rows, extent)

    gathered = gather_group([moved[0], low_inv[1], sides[1], index])
    tiles_l0, inv_l1, sides_1, index = parts(gathered, tile_rows, extent, side_extent, 8 * blocks)
    tiles_l0 = as_tiles(tiles_l0)

    index = index.reshape(pair, cores, 4, 2, blocks, extent)
    sources, targets = (
        [index[:, :, group, kind] for group in range(4)] for kind in range(2)
    )

    def own_rows(tile):
        return lax.dynamic_slice_in_dim(tile, me * rows, rows, axis=1).astype(F32)

    terms_l0 = block_terms(column, tiles_l0, sources[0])
    partial = spread([(terms_l0, targets[0])], row_group, row_group)
    got, gathered = beside(row_exchange, partial, [moved[1], low_inv[0], up_inv[0], sides[0]])
    tiles_l1, inv_l0, inv_u0, sides_0 = parts(gathered, tile_rows, extent, extent, side_extent)
    forward_1 = full_product(own_rows(sides_1) - row_sum(got), inv_l1)
    column = gather_column(forward_1)
    terms_l1 = block_terms(column, as_tiles(tiles_l1), sources[1])
    partial = spread([(terms_l0, targets[0]), (terms_l1, targets[1])], 0, row_group)
    got, gathered = beside(row_exchange, partial, [moved_up[0], up_inv[1]])
    tiles_u0, inv_u1 = parts(gathered, tile_rows, extent)
    forward_0 = full_product(own_rows(sides_0) - row_sum(got), inv_l0)

    solution_0 = exact_product(forward_0, inv_u0)
    column = gather_column(solution_0)
    terms_u0 = block_terms(column, as_tiles(tiles_u0), sources[2])
    partial = spread([(terms_u0, targets[2])], 0, row_group)
    got, tiles_u1 = beside(row_exchange, partial, [moved_up[1]])
    solution_1 = full_product(forward_1.astype(F32) - row_sum(got), inv_u1)
    column = gather_column(solution_1)

    terms_u1 = block_terms(column, as_tiles(tiles_u1), sources[3])
    partial = spread([(terms_u0, targets[2]), (terms_u1, targets[3])], row_group, row_group)
    chunks = jnp.swapaxes(partial, 0, 1).reshape(-1, rows, extent)

    def home(operand):
        return lax.all_to_all(operand, ("zl", "x", "y", "core"), 0, 0, tiled=True)

    done = jnp.stack([solution_0, solution_1], axis=1)
    got, done = beside(home, chunks, [done])
    done = lax.dynamic_index_in_dim(done, me, axis=1, keepdims=False)
    done = jnp.swapaxes(done, 0, 1).reshape(2, side_extent, extent)
    got = got.reshape(pair, row_group // cores, cores, rows, extent)
    upper_sum = jnp.sum(got.astype(F32), axis=1).reshape(side_extent, extent)
    operand = forward_2.astype(F32) - upper_sum
    solution_2 = full_product(operand[None], up_inv[2][None])
    return jnp.concatenate([done, solution_2], axis=0)[None, None, :, None]


def solution(mesh):
    z_extent = mesh.shape["prow"]
    grid = mesh.devices.reshape(z_extent // 2, 2, 4, 4, 2)
    split_mesh = Mesh(grid, ("zh", "zl", "x", "y", "core"))
    row, col = ("zh", "zl"), ("x", "y", "core")
    ranks = (6, 6, 6, 6, 4, 4, 5, 3, 6, 4, 4, 5, 3)
    placed = tuple(P(row, col, *([None] * (rank - 2))) for rank in ranks)
    return jax.shard_map(
        body,
        mesh=split_mesh,
        in_specs=placed,
        out_specs=P(row, col, None, None, None, None),
        check_vma=False,
    )
```

time: 220 us -> 176 us (0.80)
  waiting for transfers between devices: 67 us -> 42.6 us
  blocking collectives: 22.6 us -> 46.3 us
  local copies, waits for them, and re-layouts: 24.3 us -> 6.21 us
  other arithmetic: 22.7 us -> 8.79 us
  between operations: 14.4 us -> 0.54 us
  starting transfers between devices: 59.5 us -> 66.9 us
  matrix products: 7.53 us -> 3.82 us
    all_gather x2 -> x5, blocking collectives: 22.6 us -> 46.3 us  [the longest x4 35.4 us: beside(): gathered = lax.all_gather(packed, GROUP, axis=0)]
    all_to_all x4, waiting for transfers between devices: 20.2 us -> 2.72 us  [the longest x1 2.71 us: home(): return lax.all_to_all(operand, ('zl', 'x', 'y', 'core'), 0, 0, tiled=True)]
    all_gather x1 -> x0, waiting for transfers between devices: 9.66 us -> none  [body(): late = lax.all_gather(late, GROUP, axis=0)]
    all_to_all x4, starting transfers between devices: 25.7 us -> 33.8 us  [the longest x3 22.3 us: row_exchange(): return lax.all_to_all(chunks, ('x', 'y'), 0, 0, tiled=True)]
    concatenate x2 -> x1, local copies, waits for them, and re-layouts: 8.14 us -> 0.08 us  [gather_group(): packed = jnp.concatenate(pieces, axis=0) if len(pieces) > 1 else pieces[0]]
    slice x16 -> x9, local copies, waits for them, and re-layouts: 7.57 us -> 0.17 us  [the longest x6 0.12 us: parts(): return [gathered[:, end - size:end] for end, size in zip(ends, sizes)]]
    another operation x7 -> x2, other arithmetic: 4.09 us -> 0.08 us
    eq x9 -> x7, other arithmetic: 4.57 us -> 1.2 us  [the longest x3 1.03 us: spread(): mask = slots[:, None, None] == target[:, core, b][None]]
  transfers between devices with their start and end apart: 9 -> 8, of which waited for: 8 -> 4; matrix products, arithmetic and copies ran while one was open for 6% -> 2% of each run, Pallas kernels for 0% -> 0%
where the time goes in v3:
time: 176 us; the launch traced here: 175 us
  starting transfers between devices  66.9 us (38%)
  blocking collectives  46.3 us (26%)
  waiting for transfers between devices  42.6 us (24%)
  other arithmetic  8.79 us (5%)
  local copies, waits for them, and re-layouts  6.21 us (4%)
  matrix products  3.82 us (2%)
    all_to_all x3, waiting for transfers between devices, gather_column(): got = lax.all_to_all(copies, 'zh', 0, 0, tiled=True)  39.9 us
    all_gather x4, blocking collectives, beside(): gathered = lax.all_gather(packed, GROUP, axis=0)  35.4 us
    all_to_all x3, starting transfers between devices, row_exchange(): return lax.all_to_all(chunks, ('x', 'y'), 0, 0, tiled=True)  22.3 us
    all_to_all x1, starting transfers between devices, body(): column = lax.all_to_all(copies, ('zh', 'zl', 'core'), 0, 0, tiled=True)  16.9 us
    all_to_all x3, starting transfers between devices, gather_column(): got = lax.all_to_all(copies, 'zh', 0, 0, tiled=True)  16.2 us
    all_to_all x1, starting transfers between devices, home(): return lax.all_to_all(operand, ('zl', 'x', 'y', 'core'), 0, 0, tiled=True)  11.6 us
    all_gather x1, blocking collectives, gather_group(): return lax.all_gather(packed, GROUP, axis=0)  10.9 us
    convert_element_type x4, other arithmetic, spread(): return total.astype(BF16)  6.38 us
  transfers between devices with their start and end apart: 8, of which 4 were waited for; matrix products, arithmetic and copies ran while one was open for 2% of the time, Pallas kernels for 0%

profile of v3, /device:TPU:1, one launch (start us, length us, event | category | flops | bytes accessed | tf_op | source)
XLA Modules:
  0.0 175.2 jit_solution(51775755234323880)
XLA Ops:
  0.0 0.9 convolution_convert_fusion.7
  1.6 16.9 %all-to-all-start = ((bf16[32,16,128]{2,1,0:T(8,128)(2,1)}), bf16[32,16,128]{2,1,0:T(8,128)(2,1)S(1)}, u32[]{:S(2)}, u32[]{:S(2)}) async-start(bf16[32,16,128]{2,1,0:T(8,128)(2,1)} %bitcast.24), calls=%async_computation | async-start | bytes 262144 | tf_op jit(solution)/shard_map/all_to_all | solution.py:123
  21.5 10.9 %all-gather = bf16[2944,128]{1,0:T(8,128)(2,1)S(1)} all-gather(bf16[736,128]{1,0:T(8,128)(2,1)S(1)} %maximum_maximum_fusion), channel_id=2, replica_groups=mesh['zh'=8,'zl'=2,'x'=4,'y'=4,'core'=2] {'zl','core'}, dimensions={0}, use_global_device_ids=true | all-gather | bytes 942080 | tf_op jit(solution)/shard_map/all_gather | solution.py:38
  32.8 0.9 copy-done.1
  33.9 0.7 broadcast_compare_fusion.7
  35.0 1.3 add_convert_fusion.2
  36.3 6.8 %all-to-all-start.1 = ((bf16[16,2,2,16,128]{4,3,2,1,0:T(8,128)(2,1)}), bf16[16,2,2,16,128]{4,3,2,1,0:T(8,128)(2,1)S(1)}, u32[]{:S(2)}, u32[]{:S(2)}) async-start(bf16[16,2,2,16,128]{4,3,2,1,0:T(8,128)(2,1)} %bitcast.60), calls=%async_computation.1 | async-start | bytes 524288 | tf_op jit(solution)/shard_map/all_to_all | solution.py:77
  43.0 9.6 %all-gather.1 = bf16[3328,128]{1,0:T(8,128)(2,1)S(1)} all-gather(bf16[832,128]{1,0:T(8,128)(2,1)S(1)} %pad_maximum_fusion), channel_id=3, replica_groups=mesh['zh'=8,'zl'=2,'x'=4,'y'=4,'core'=2] {'zl','core'}, dimensions={0}, use_global_device_ids=true | all-gather | bytes 1064960 | tf_op jit(solution)/shard_map/all_gather | solution.py:44
  53.6 9.5 %all-to-all-start.2 = ((bf16[8,4,16,128]{3,2,1,0:T(8,128)(2,1)}), bf16[8,4,16,128]{3,2,1,0:T(8,128)(2,1)S(1)}, u32[]{:S(2)}, u32[]{:S(2)}) async-start(bf16[8,4,16,128]{3,2,1,0:T(8,128)(2,1)} %broadcast_in_dim.1627), calls=%async_computation.2 | async-start | bytes 262144 | tf_op jit(solution)/shard_map/all_to_all | solution.py:87
  63.2 14.1 %all-to-all-done.2 = bf16[8,4,16,128]{3,2,1,0:T(8,128)(2,1)S(1)} async-done(((bf16[8,4,16,128]{3,2,1,0:T(8,128)(2,1)}), bf16[8,4,16,128]{3,2,1,0:T(8,128)(2,1)S(1)}, u32[]{:S(2)}, u32[]{:S(2)}) %all-to-all-start.2) | async-done | bytes 131104 | tf_op jit(solution)/shard_map/all_to_all | solution.py:87
  77.7 1.9 %add_convert_fusion.1 = bf16[32,2,16,128]{3,2,1,0:T(8,128)(2,1)} fusion(f32[2,16,128]{2,1,0:T(8,128)S(1)} %get-tuple-element.90, f32[2,16,128]{2,1,0:T(8,128)S(1)} %get-tuple-element.91, f32[2,16,128]{2,1,0:T(8,128)S(1)} %get-tuple-element.92, f32[2,16,128]{2,1,0:T(8,128)S(1)} %get-tuple-element.93, f32[2,16,128]{2,1,0:T(8,128)S(1)} %get-tuple-element.94, ...), kind=kLoop, calls=%fused_computation.47 | loop fusion | flops 4194304 | bytes 655360 | tf_op jit(solution)/shard_map/convert_element_type | solution.py:70
  79.6 6.2 %all-to-all-start.3 = ((bf16[16,2,2,16,128]{4,3,2,1,0:T(8,128)(2,1)}), bf16[16,2,2,16,128]{4,3,2,1,0:T(8,128)(2,1)S(1)}, u32[]{:S(2)}, u32[]{:S(2)}) async-start(bf16[16,2,2,16,128]{4,3,2,1,0:T(8,128)(2,1)} %bitcast.119), calls=%async_computation.3 | async-start | bytes 524288 | tf_op jit(solution)/shard_map/all_to_all | solution.py:77
  85.9 10.8 %all-gather.2 = bf16[2560,128]{1,0:T(8,128)(2,1)S(1)} all-gather(bf16[640,128]{1,0:T(8,128)(2,1)S(1)} %pad_maximum_fusion.1), channel_id=4, replica_groups=mesh['zh'=8,'zl'=2,'x'=4,'y'=4,'core'=2] {'zl','core'}, dimensions={0}, use_global_device_ids=true | all-gather | bytes 819200 | tf_op jit(solution)/shard_map/all_gather | solution.py:44
  97.7 3.4 %all-to-all-start.4 = ((bf16[8,4,16,128]{3,2,1,0:T(8,128)(2,1)}), bf16[8,4,16,128]{3,2,1,0:T(8,128)(2,1)S(1)}, u32[]{:S(2)}, u32[]{:S(2)}) async-start(bf16[8,4,16,128]{3,2,1,0:T(8,128)(2,1)} %broadcast_in_dim.1698), calls=%async_computation.4 | async-start | bytes 262144 | tf_op jit(solution)/shard_map/all_to_all | solution.py:87
  101.4 12.8 %all-to-all-done.4 = bf16[8,4,16,128]{3,2,1,0:T(8,128)(2,1)S(1)} async-done(((bf16[8,4,16,128]{3,2,1,0:T(8,128)(2,1)}), bf16[8,4,16,128]{3,2,1,0:T(8,128)(2,1)S(1)}, u32[]{:S(2)}, u32[]{:S(2)}) %all-to-all-start.4) | async-done | bytes 131104 | tf_op jit(solution)/shard_map/all_to_all | solution.py:87
  114.6 1.3 add_convert_fusion
  115.9 9.3 %all-to-all-start.5 = ((bf16[16,2,2,16,128]{4,3,2,1,0:T(8,128)(2,1)}), bf16[16,2,2,16,128]{4,3,2,1,0:T(8,128)(2,1)S(1)}, u32[]{:S(2)}, u32[]{:S(2)}) async-start(bf16[16,2,2,16,128]{4,3,2,1,0:T(8,128)(2,1)} %bitcast.191), calls=%async_computation.5 | async-start | bytes 524288 | tf_op jit(solution)/shard_map/all_to_all | solution.py:77
  125.2 7.9 %all-gather.3 = bf16[2048,128]{1,0:T(8,128)(2,1)S(1)} all-gather(bf16[512,128]{1,0:T(8,128)(2,1)S(1)} %bitcast.601), channel_id=5, replica_groups=mesh['zh'=8,'zl'=2,'x'=4,'y'=4,'core'=2] {'zl','core'}, dimensions={0}, use_global_device_ids=true | all-gather | bytes 655360 | tf_op jit(solution)/shard_map/all_gather | solution.py:44
  134.0 3.4 %all-to-all-start.6 = ((bf16[8,4,16,128]{3,2,1,0:T(8,128)(2,1)}), bf16[8,4,16,128]{3,2,1,0:T(8,128)(2,1)S(1)}, u32[]{:S(2)}, u32[]{:S(2)}) async-start(bf16[8,4,16,128]{3,2,1,0:T(8,128)(2,1)} %broadcast_in_dim.1796), calls=%async_computation.6 | async-start | bytes 262144 | tf_op jit(solution)/shard_map/all_to_all | solution.py:87
  137.7 13.0 %all-to-all-done.6 = bf16[8,4,16,128]{3,2,1,0:T(8,128)(2,1)S(1)} async-done(((bf16[8,4,16,128]{3,2,1,0:T(8,128)(2,1)}), bf16[8,4,16,128]{3,2,1,0:T(8,128)(2,1)S(1)}, u32[]{:S(2)}, u32[]{:S(2)}) %all-to-all-start.6) | async-done | bytes 131104 | tf_op jit(solution)/shard_map/all_to_all | solution.py:87
  151.0 1.9 %fusion.3 = bf16[64,16,128]{2,1,0:T(8,128)(2,1)} fusion(f32[2,16,128]{2,1,0:T(8,128)S(1)} %get-tuple-element.42, f32[2,16,128]{2,1,0:T(8,128)S(1)} %get-tuple-element.43, f32[2,16,128]{2,1,0:T(8,128)S(1)} %get-tuple-element.44, f32[2,16,128]{2,1,0:T(8,128)S(1)} %get-tuple-element.45, f32[2,16,128]{2,1,0:T(8,128)S(1)} %get-tuple-element.46, ...), kind=kLoop, calls=%fused_computation.13 | loop fusion | flops 4194304 | bytes 655360 | tf_op jit(solution)/shard_map/convert_element_type | solution.py:70
  152.9 11.6 %all-to-all-start.7 = ((bf16[64,16,128]{2,1,0:T(8,128)(2,1)}), bf16[64,16,128]{2,1,0:T(8,128)(2,1)S(1)}, u32[]{:S(2)}, u32[]{:S(2)}) async-start(bf16[64,16,128]{2,1,0:T(8,128)(2,1)} %fusion.3), calls=%async_computation.7 | async-start | bytes 524288 | tf_op jit(solution)/shard_map/all_to_all | solution.py:183
  164.5 7.1 %all-gather.4 = bf16[16,2,16,128]{3,2,0,1:T(8,128)(2,1)S(1)} all-gather(bf16[4,2,16,128]{3,2,0,1:T(8,128)(2,1)S(1)} %pad_maximum_fusion.2), channel_id=6, replica_groups=mesh['zh'=8,'zl'=2,'x'=4,'y'=4,'core'=2] {'zl','core'}, dimensions={0}, use_global_device_ids=true | all-gather | bytes 163840 | tf_op jit(solution)/shard_map/all_gather | solution.py:44
  171.6 2.7 %all-to-all-done.7 = bf16[64,16,128]{2,1,0:T(8,128)(2,1)S(1)} async-done(((bf16[64,16,128]{2,1,0:T(8,128)(2,1)}), bf16[64,16,128]{2,1,0:T(8,128)(2,1)S(1)}, u32[]{:S(2)}, u32[]{:S(2)}) %all-to-all-start.7) | async-done | bytes 262176 | tf_op jit(solution)/shard_map/all_to_all | solution.py:183
  (102 shorter events, 10.0 us)
Async XLA Ops:
  0.0 20.2 %copy-start = (bf16[1,1,2,4,128,128]{5,4,3,2,1,0:T(8,128)(2,1)S(1)}, bf16[1,1,2,4,128,128]{5,4,3,2,1,0:T(8,128)(2,1)}, u32[]{:S(2)}) copy-start(bf16[1,1,2,4,128,128]{5,4,3,2,1,0:T(8,128)(2,1)} %param.16) | copy-start | bytes 786436
  1.6 16.9 %copy-start.4 = (bf16[1,1,3,1,64,128]{5,4,3,2,1,0:T(8,128)(2,1)S(1)}, bf16[1,1,3,1,64,128]{5,4,3,2,1,0:T(8,128)(2,1)}, u32[]{:S(2)}) copy-start(bf16[1,1,3,1,64,128]{5,4,3,2,1,0:T(8,128)(2,1)} %param.13) | copy-start | bytes 147460
  1.6 18.5 %copy-start.2 = (bf16[1,1,3,1,128,128]{5,4,3,2,1,0:T(8,128)(2,1)S(1)}, bf16[1,1,3,1,128,128]{5,4,3,2,1,0:T(8,128)(2,1)}, u32[]{:S(2)}) copy-start(bf16[1,1,3,1,128,128]{5,4,3,2,1,0:T(8,128)(2,1)} %param.14) | copy-start | bytes 294916
  1.6 18.5 %copy-start.3 = (bf16[1,1,3,1,128,128]{5,4,3,2,1,0:T(8,128)(2,1)S(1)}, bf16[1,1,3,1,128,128]{5,4,3,2,1,0:T(8,128)(2,1)}, u32[]{:S(2)}) copy-start(bf16[1,1,3,1,128,128]{5,4,3,2,1,0:T(8,128)(2,1)} %param.15) | copy-start | bytes 294916
  1.6 32.9 %all-to-all-start = ((bf16[32,16,128]{2,1,0:T(8,128)(2,1)}), bf16[32,16,128]{2,1,0:T(8,128)(2,1)S(1)}, u32[]{:S(2)}, u32[]{:S(2)}) async-start(bf16[32,16,128]{2,1,0:T(8,128)(2,1)} %bitcast.24), calls=%async_computation | async-start | bytes 262144 | tf_op jit(solution)/shard_map/all_to_all | solution.py:123
  18.5 0.7 copy-start.7
  18.5 0.7 copy-start.8
  18.6 0.7 copy-start.10
  18.6 0.7 copy-start.12
  19.2 0.7 copy-start.9
  19.2 0.7 copy-start.11
  20.2 0.7 copy-start.5
  32.7 1.0 copy-start.1
  32.8 0.9 copy-start.6
  36.3 16.4 %all-to-all-start.1 = ((bf16[16,2,2,16,128]{4,3,2,1,0:T(8,128)(2,1)}), bf16[16,2,2,16,128]{4,3,2,1,0:T(8,128)(2,1)S(1)}, u32[]{:S(2)}, u32[]{:S(2)}) async-start(bf16[16,2,2,16,128]{4,3,2,1,0:T(8,128)(2,1)} %bitcast.60), calls=%async_computation.1 | async-start | bytes 524288 | tf_op jit(solution)/shard_map/all_to_all | solution.py:77
  53.6 23.7 %all-to-all-start.2 = ((bf16[8,4,16,128]{3,2,1,0:T(8,128)(2,1)}), bf16[8,4,16,128]{3,2,1,0:T(8,128)(2,1)S(1)}, u32[]{:S(2)}, u32[]{:S(2)}) async-start(bf16[8,4,16,128]{3,2,1,0:T(8,128)(2,1)} %broadcast_in_dim.1627), calls=%async_computation.2 | async-start | bytes 262144 | tf_op jit(solution)/shard_map/all_to_all | solution.py:87
  79.6 17.0 %all-to-all-start.3 = ((bf16[16,2,2,16,128]{4,3,2,1,0:T(8,128)(2,1)}), bf16[16,2,2,16,128]{4,3,2,1,0:T(8,128)(2,1)S(1)}, u32[]{:S(2)}, u32[]{:S(2)}) async-start(bf16[16,2,2,16,128]{4,3,2,1,0:T(8,128)(2,1)} %bitcast.119), calls=%async_computation.3 | async-start | bytes 524288 | tf_op jit(solution)/shard_map/all_to_all | solution.py:77
  97.7 16.5 %all-to-all-start.4 = ((bf16[8,4,16,128]{3,2,1,0:T(8,128)(2,1)}), bf16[8,4,16,128]{3,2,1,0:T(8,128)(2,1)S(1)}, u32[]{:S(2)}, u32[]{:S(2)}) async-start(bf16[8,4,16,128]{3,2,1,0:T(8,128)(2,1)} %broadcast_in_dim.1698), calls=%async_computation.4 | async-start | bytes 262144 | tf_op jit(solution)/shard_map/all_to_all | solution.py:87
  115.9 17.2 %all-to-all-start.5 = ((bf16[16,2,2,16,128]{4,3,2,1,0:T(8,128)(2,1)}), bf16[16,2,2,16,128]{4,3,2,1,0:T(8,128)(2,1)S(1)}, u32[]{:S(2)}, u32[]{:S(2)}) async-start(bf16[16,2,2,16,128]{4,3,2,1,0:T(8,128)(2,1)} %bitcast.191), calls=%async_computation.5 | async-start | bytes 524288 | tf_op jit(solution)/shard_map/all_to_all | solution.py:77
  134.0 16.6 %all-to-all-start.6 = ((bf16[8,4,16,128]{3,2,1,0:T(8,128)(2,1)}), bf16[8,4,16,128]{3,2,1,0:T(8,128)(2,1)S(1)}, u32[]{:S(2)}, u32[]{:S(2)}) async-start(bf16[8,4,16,128]{3,2,1,0:T(8,128)(2,1)} %broadcast_in_dim.1796), calls=%async_computation.6 | async-start | bytes 262144 | tf_op jit(solution)/shard_map/all_to_all | solution.py:87
  152.9 21.4 %all-to-all-start.7 = ((bf16[64,16,128]{2,1,0:T(8,128)(2,1)}), bf16[64,16,128]{2,1,0:T(8,128)(2,1)S(1)}, u32[]{:S(2)}, u32[]{:S(2)}) async-start(bf16[64,16,128]{2,1,0:T(8,128)(2,1)} %fusion.3), calls=%async_computation.7 | async-start | bytes 524288 | tf_op jit(solution)/shard_map/all_to_all | solution.py:183

commit v4 on v3

v4 whole, which is shorter than its diff:
```python
import functools

import jax
import jax.numpy as jnp
from jax import lax
from jax.experimental import pallas as pl
from jax.experimental.pallas import tpu as pltpu
from jax.sharding import Mesh
from jax.sharding import PartitionSpec as P

BF16 = jnp.bfloat16
F32 = jnp.float32
GROUP = ("zl", "core")
SPLIT = 4
NOWHERE = 255


def row_table(rows):
    places = lax.broadcasted_iota(jnp.int32, (rows.shape[-1],) * 2, 0)
    return [jnp.where(rows[b : b + 1] == places, 1.0, 0.0).astype(BF16) for b in range(rows.shape[0])]


def moved_columns(tile, table):
    return lax.dot_general(
        tile, table, (((1,), (1,)), ((), ())), preferred_element_type=F32
    ).astype(BF16)


def moved_rows(tile, table):
    return jnp.dot(table, tile, preferred_element_type=F32).astype(BF16)


def whole(array):
    return pl.BlockSpec(array.shape, lambda i: (0,) * array.ndim)


def one_of(array, place):
    return pl.BlockSpec((1,) + array.shape[1:], lambda i: (place,) + (0,) * (array.ndim - 1))


def scalars():
    return pl.BlockSpec(memory_space=pltpu.SMEM)


def first_kernel(
    sides_1, sides_2, inv_1, inv_2, tiles, rows, ls, lt, lc, us, ut, uc, packed, copies, forward, index
):
    solved = jnp.dot(sides_2[0], inv_2[0], preferred_element_type=F32).astype(BF16)
    forward[...] = solved
    for i in range(copies.shape[0]):
        copies[i] = solved
    blocks, extent = tiles.shape[1], tiles.shape[2]
    for b, table in enumerate(row_table(rows[0])):
        packed[b * extent : (b + 1) * extent] = moved_columns(tiles[0, b], table)
    at = blocks * extent
    packed[at : at + extent] = inv_1[0]
    at = at + extent
    packed[at : at + sides_1.shape[1]] = sides_1[0]
    at = at + sides_1.shape[1]
    for side, (source, target, count) in enumerate(((ls, lt, lc), (us, ut, uc))):
        for g in range(2):
            row = (2 * side + g) * 2 * blocks
            for b in range(blocks):
                goal = jnp.where(b < count[g], target[g, b], NOWHERE)
                index[row + b : row + b + 1] = jnp.full((1, extent), source[g, b], jnp.int32)
                index[row + blocks + b : row + blocks + b + 1] = jnp.full((1, extent), goal, jnp.int32)
    packed[at : at + index.shape[0]] = index[...].astype(F32).astype(BF16)


def later_kernel(sides_0, low_inv_0, up_inv_0, up_inv_1, low, up, low_rows, up_rows, start, packed):
    blocks, extent = low.shape[1], low.shape[2]
    for b, table in enumerate(row_table(low_rows[0])):
        packed[b * extent : (b + 1) * extent] = moved_columns(low[0, b], table)
    for g in range(2):
        for b, table in enumerate(row_table(up_rows[g])):
            at = ((1 + g) * blocks + b) * extent
            packed[at : at + extent] = moved_rows(up[g, b], table)
    at = 3 * blocks * extent
    for piece in (low_inv_0, up_inv_0, up_inv_1):
        packed[at : at + extent] = piece[0]
        at = at + extent
    packed[at : at + sides_0.shape[1]] = sides_0[0]


def swapped(value, axis):
    return lax.ppermute(value, axis, [(0, 1), (1, 0)])


def offsets():
    return [(step // 2, step % 2) for step in range(SPLIT)]


def spread_kernel(group, level, by_target, after, place, column, *refs):
    tiles, indices, refs = refs[:SPLIT], refs[SPLIT : 2 * SPLIT], refs[2 * SPLIT :]
    before = refs[0] if after else None
    partial, terms = refs[-2:]
    zl, core = place[0], place[1]
    extent = column.shape[3]
    rows, blocks = column.shape[2], tiles[0].shape[0] // extent
    goals = []
    for step, (dz, dc) in enumerate(offsets()):
        index = indices[step][...].astype(F32)
        half = lax.bitwise_xor(core, dc)
        held = [column[j, pl.ds(half, 1)][0].astype(F32) for j in range(column.shape[0])]
        first = 2 * blocks * group
        goals.append([index[first + blocks + b : first + blocks + b + 1] for b in range(blocks)])
        if after:
            first = first - 2 * blocks
            goals[-1] += [index[first + blocks + b : first + blocks + b + 1] for b in range(blocks)]
        first = 2 * blocks * group
        for b in range(blocks):
            source = index[first + b : first + b + 1]
            picked = jnp.zeros((rows, extent), F32)
            for j, tile in enumerate(held):
                picked = jnp.where(source == float(j), tile, picked)
            terms[step, b] = jnp.dot(
                picked.astype(BF16),
                tiles[step][b * extent : (b + 1) * extent],
                preferred_element_type=F32,
            )

    targets = partial.shape[1] if by_target else partial.shape[0]

    def one_target(t, carry):
        slot = (t + level * targets).astype(F32)
        for dz in range(2):
            total = jnp.zeros((rows, extent), F32)
            for dc in range(2):
                step = 2 * dz + dc
                for b in range(blocks):
                    total = total + jnp.where(goals[step][b] == slot, terms[step, b], 0.0)
                    if after:
                        hit = goals[step][blocks + b] == slot
                        total = total + jnp.where(hit, before[step, b], 0.0)
            row = lax.bitwise_xor(zl, dz)
            if by_target:
                partial[pl.ds(row, 1), pl.ds(t, 1)] = total.astype(BF16)[None, None]
            else:
                partial[pl.ds(t, 1), pl.ds(row, 1)] = total.astype(BF16)[None, None]
        return carry

    lax.fori_loop(0, targets, one_target, 0, unroll=4)


def full_product(operand, inverse):
    high = operand.astype(BF16)
    rest = operand - high.astype(F32)
    middle = rest.astype(BF16)
    low = (rest - middle.astype(F32)).astype(BF16)
    parts = jnp.concatenate([high, middle, low], axis=0)
    product = jnp.dot(parts, inverse, preferred_element_type=F32)
    rows = operand.shape[0]
    return product[:rows] + (product[rows : 2 * rows] + product[2 * rows :])


def solve_kernel(kind, place, got, *refs):
    inverses, refs = refs[:SPLIT], refs[SPLIT:]
    zl, core = place[0], place[1]
    rows = got.shape[3]
    me = 2 * zl + core
    if kind == 2:
        held, (solved, copies) = refs[0], refs[1:]
    elif kind == 1:
        sides, uppers, (solved, copies) = refs[:SPLIT], refs[SPLIT : 2 * SPLIT], refs[2 * SPLIT :]
    else:
        sides, (solved, copies) = refs[:SPLIT], refs[SPLIT:]
    for step, (dz, dc) in enumerate(offsets()):
        row, col = lax.bitwise_xor(zl, dz), lax.bitwise_xor(core, dc)
        total = jnp.zeros(got.shape[3:], F32)
        for i in range(got.shape[0]):
            total = total + got[i, pl.ds(col, 1), pl.ds(row, 1)][0, 0].astype(F32)
        if kind == 2:
            operand = held[step].astype(F32) - total
        else:
            mine = sides[step][pl.ds(pl.multiple_of(me * rows, rows), rows)]
            operand = mine.astype(F32) - total
        result = full_product(operand, inverses[step][...]).astype(BF16)
        if kind == 1:
            result = jnp.dot(result, uppers[step][...], preferred_element_type=F32).astype(BF16)
        solved[step] = result
        for i in range(copies.shape[0]):
            copies[i, pl.ds(row, 1), pl.ds(col, 1)] = result[None, None]


def last_kernel(place, got, forward, inverse, home_0, home_1, home_2, home_3, out):
    zl, core = place[0], place[1]
    rows = got.shape[3]
    me = 2 * zl + core
    for step, home in enumerate((home_0, home_1, home_2, home_3)):
        at = pl.multiple_of(lax.bitwise_xor(me, step) * rows, rows)
        for level in range(2):
            out[level, pl.ds(at, rows)] = home[level]
    for pair in range(got.shape[0]):
        for core_at in range(got.shape[2]):
            total = jnp.zeros(got.shape[3:], F32)
            for i in range(got.shape[1]):
                total = total + got[pair, i, core_at].astype(F32)
            at = (2 * pair + core_at) * rows
            operand = forward[at : at + rows].astype(F32) - total
            out[2, at : at + rows] = full_product(operand, inverse[0]).astype(BF16)


def row_exchange(partial):
    cores = lax.axis_size("core")
    chunks = partial.reshape((-1, cores) + partial.shape[1:])
    return lax.all_to_all(chunks, ("x", "y"), 0, 0, tiled=True)


def gather_column(copies):
    got = lax.all_to_all(copies, "zh", 0, 0, tiled=True)
    return got.reshape((-1,) + got.shape[2:])


def body(
    right_sides,
    lower_inverse,
    upper_inverse,
    lower_tiles,
    lower_source,
    lower_target,
    lower_rows,
    lower_count,
    upper_tiles,
    upper_source,
    upper_target,
    upper_rows,
    upper_count,
):
    sides = right_sides[0, 0, :, 0]
    low_inv, up_inv = lower_inverse[0, 0, :, 0], upper_inverse[0, 0, :, 0]
    low_tiles, up_tiles = lower_tiles[0, 0], upper_tiles[0, 0]
    low_rows, up_rows = lower_rows[0, 0], upper_rows[0, 0]
    low_source, low_target, low_count = lower_source[0, 0], lower_target[0, 0], lower_count[0, 0]
    up_source, up_target, up_count = upper_source[0, 0], upper_target[0, 0], upper_count[0, 0]
    side_extent, extent = sides.shape[1:]
    blocks = low_tiles.shape[1]
    pair, cores = lax.axis_size("zl"), lax.axis_size("core")
    high = lax.axis_size("zh")
    row_group = lax.axis_size("x") * lax.axis_size("y") * cores
    rows = side_extent // SPLIT
    tile_rows = blocks * extent

    first_sizes = [tile_rows, extent, side_extent, 8 * blocks]
    packed, copies, forward_2 = pl.pallas_call(
        first_kernel,
        grid=(1,),
        in_specs=[one_of(sides, 1), one_of(sides, 2), one_of(low_inv, 1), one_of(low_inv, 2)]
        + [one_of(low_tiles, 0), one_of(low_rows, 0)]
        + [scalars()] * 6,
        out_shape=[
            jax.ShapeDtypeStruct((sum(first_sizes), extent), BF16),
            jax.ShapeDtypeStruct((high, side_extent, extent), BF16),
            jax.ShapeDtypeStruct((side_extent, extent), BF16),
        ],
        out_specs=[
            pl.BlockSpec((sum(first_sizes), extent), lambda i: (0, 0)),
            pl.BlockSpec((high, side_extent, extent), lambda i: (0, 0, 0)),
            pl.BlockSpec((side_extent, extent), lambda i: (0, 0)),
        ],
        scratch_shapes=[pltpu.VMEM((8 * blocks, extent), jnp.int32)],
        compiler_params=pltpu.CompilerParams(vmem_limit_bytes=16 << 20),
    )(
        *(sides, sides, low_inv, low_inv, low_tiles, low_rows),
        *(low_source, low_target, low_count, up_source, up_target, up_count),
    )
    z_mate = swapped(packed, "zl")
    copies = copies.reshape(-1, rows, extent)
    column = lax.all_to_all(copies, ("zh", "zl", "core"), 0, 0, tiled=True)
    column = column.reshape(-1, cores, rows, extent)
    packed, z_mate = lax.optimization_barrier((packed, z_mate))
    first = (packed, swapped(packed, "core"), z_mate, swapped(z_mate, "core"))

    later_sizes = [tile_rows] * 3 + [extent] * 3 + [side_extent]
    start = first[3][:16]
    packed = pl.pallas_call(
        later_kernel,
        grid=(1,),
        in_specs=[one_of(sides, 0), one_of(low_inv, 0), one_of(up_inv, 0), one_of(up_inv, 1)]
        + [one_of(low_tiles, 1), whole(up_tiles), one_of(low_rows, 1), whole(up_rows), whole(start)],
        out_shape=jax.ShapeDtypeStruct((sum(later_sizes), extent), BF16),
        out_specs=pl.BlockSpec((sum(later_sizes), extent), lambda i: (0, 0)),
        compiler_params=pltpu.CompilerParams(vmem_limit_bytes=16 << 20),
    )(sides, low_inv, up_inv, up_inv, low_tiles, up_tiles, low_rows, up_rows, start)
    z_mate = swapped(packed, "zl")
    later = (packed, swapped(packed, "core"), z_mate, swapped(z_mate, "core"))

    place = jnp.stack([lax.axis_index("zl"), lax.axis_index("core")]).astype(jnp.int32)

    def rows_of(sizes, number):
        start, size = sum(sizes[:number]), sizes[number]
        return pl.BlockSpec((size, extent), lambda i: (start // size, 0))

    index_block = rows_of(first_sizes, 3)

    def edge(column, buffers, tile_block, group, level, before=None, by_target=False):
        shape = (row_group, pair) if not by_target else (pair, row_group)
        partial = jax.ShapeDtypeStruct(shape + (rows, extent), BF16)
        terms = jax.ShapeDtypeStruct((SPLIT, blocks, rows, extent), F32)
        extra = () if before is None else (before,)
        return pl.pallas_call(
            functools.partial(spread_kernel, group, level, by_target, before is not None),
            grid=(1,),
            in_specs=[scalars(), whole(column)]
            + [tile_block] * SPLIT
            + [index_block] * SPLIT
            + [whole(array) for array in extra],
            out_shape=[partial, terms],
            out_specs=[whole(partial), whole(terms)],
            compiler_params=pltpu.CompilerParams(vmem_limit_bytes=16 << 20),
        )(place, column, *buffers, *first, *extra)

    def solve(kind, got, *pieces):
        solved = jax.ShapeDtypeStruct((SPLIT, rows, extent), BF16)
        copies = jax.ShapeDtypeStruct((high, pair, cores, rows, extent), BF16)
        arrays, specs = [], []
        for buffers, block in pieces:
            arrays += buffers
            specs += [block] * len(buffers)
        return pl.pallas_call(
            functools.partial(solve_kernel, kind),
            grid=(1,),
            in_specs=[scalars(), whole(got)] + specs,
            out_shape=[solved, copies],
            out_specs=[whole(solved), whole(copies)],
            compiler_params=pltpu.CompilerParams(vmem_limit_bytes=16 << 20),
        )(place, got, *arrays)

    partial, terms = edge(column, first, rows_of(first_sizes, 0), 0, 1)
    got = row_exchange(partial)
    inverse, side = rows_of(first_sizes, 1), rows_of(first_sizes, 2)
    forward_1, copies = solve(0, got, (first, inverse), (first, side))
    column = gather_column(copies)
    partial, _ = edge(column, later, rows_of(later_sizes, 0), 1, 0, terms)
    got = row_exchange(partial)
    inverse, upper, side = (rows_of(later_sizes, i) for i in (3, 4, 6))
    solution_0, copies = solve(1, got, (later, inverse), (later, side), (later, upper))

    column = gather_column(copies)
    partial, terms = edge(column, later, rows_of(later_sizes, 1), 2, 0)
    got = row_exchange(partial)
    solution_1, copies = solve(2, got, (later, rows_of(later_sizes, 5)), ([forward_1], whole(forward_1)))
    column = gather_column(copies)

    done = jnp.stack([solution_0, solution_1], axis=1)
    home = [done[0]]
    for step in range(1, SPLIT):
        home.append(lax.ppermute(done[step], GROUP, [(i, i ^ step) for i in range(SPLIT)]))
    column, *home = lax.optimization_barrier((column, *home))
    partial, _ = edge(column, later, rows_of(later_sizes, 2), 3, 1, terms, by_target=True)
    got = lax.all_to_all(partial.reshape(-1, rows, extent), ("zl", "x", "y", "core"), 0, 0, tiled=True)
    got = got.reshape(pair, row_group // cores, cores, rows, extent)
    result = jax.ShapeDtypeStruct(sides.shape, BF16)
    result = pl.pallas_call(
        last_kernel,
        grid=(1,),
        in_specs=[scalars(), whole(got), whole(forward_2), one_of(up_inv, 2)]
        + [whole(piece) for piece in home],
        out_shape=result,
        out_specs=whole(result),
        compiler_params=pltpu.CompilerParams(vmem_limit_bytes=16 << 20),
    )(place, got, forward_2, up_inv, *home)
    return result[None, None, :, None]


def solution(mesh):
    z_extent = mesh.shape["prow"]
    grid = mesh.devices.reshape(z_extent // 2, 2, 4, 4, 2)
    split_mesh = Mesh(grid, ("zh", "zl", "x", "y", "core"))
    row, col = ("zh", "zl"), ("x", "y", "core")
    ranks = (6, 6, 6, 6, 4, 4, 5, 3, 6, 4, 4, 5, 3)
    placed = tuple(P(row, col, *([None] * (rank - 2))) for rank in ranks)
    return jax.shard_map(
        body,
        mesh=split_mesh,
        in_specs=placed,
        out_specs=P(row, col, None, None, None, None),
        check_vma=False,
    )
```

time: 176 us -> 165 us (0.938)
  waiting for transfers between devices: 42.6 us -> 23.8 us
  Pallas kernels: 0 us -> 14.8 us
  blocking collectives: 46.3 us -> 56.9 us
  other arithmetic: 8.79 us -> 0.08 us
  matrix products: 3.82 us -> 0 us
  starting transfers between devices: 66.9 us -> 63.8 us
  local copies, waits for them, and re-layouts: 6.21 us -> 4.03 us
    all_to_all x0 -> x4, blocking collectives: none -> 56.9 us  [the longest x2 21.4 us: row_exchange(): return lax.all_to_all(chunks, ('x', 'y'), 0, 0, tiled=True)]
    all_gather x5 -> x0, blocking collectives: 46.3 us -> none  [the longest x4 35.4 us: beside(): gathered = lax.all_gather(packed, GROUP, axis=0)]
    ppermute x0 -> x9, starting transfers between devices: none -> 32.5 us  [the longest x6 18.3 us: swapped(): return lax.ppermute(value, axis, [(0, 1), (1, 0)])]
    all_to_all x3 -> x2, waiting for transfers between devices: 39.9 us -> 13.7 us  [gather_column(): got = lax.all_to_all(copies, 'zh', 0, 0, tiled=True)]
    all_to_all x3 -> x1, starting transfers between devices: 22.3 us -> 6.76 us  [row_exchange(): return lax.all_to_all(chunks, ('x', 'y'), 0, 0, tiled=True)]
    pallas_call x0 -> x10, Pallas kernels: none -> 14.8 us  [the longest x4 8.15 us: edge(): pl.pallas_call(functools.partial(spread_kernel, group, level, by_target,...]
    all_to_all x1 -> x0, starting transfers between devices: 11.6 us -> none  [home(): return lax.all_to_all(operand, ('zl', 'x', 'y', 'core'), 0, 0, tiled=True)]
    all_to_all x3 -> x2, starting transfers between devices: 16.2 us -> 9.24 us  [gather_column(): got = lax.all_to_all(copies, 'zh', 0, 0, tiled=True)]
  transfers between devices with their start and end apart: 8 -> 13, of which waited for: 4 -> 6; matrix products, arithmetic and copies ran while one was open for 2% -> 0% of each run, Pallas kernels for 0% -> 2%
where the time goes in v4:
time: 165 us; the launch traced here: 164 us
  starting transfers between devices  63.8 us (39%)
  blocking collectives  56.9 us (34%)
  waiting for transfers between devices  23.8 us (14%)
  Pallas kernels  14.8 us (9%)
  local copies, waits for them, and re-layouts  4.03 us (2%)
    all_to_all x2, blocking collectives, row_exchange(): return lax.all_to_all(chunks, ('x', 'y'), 0, 0, tiled=True)  21.4 us
    all_to_all x1, blocking collectives, body(): lax.all_to_all(partial.reshape(-1, rows, extent), ('zl', 'x', 'y', 'core'...  19.1 us
    ppermute x6, starting transfers between devices, swapped(): return lax.ppermute(value, axis, [(0, 1), (1, 0)])  18.3 us
    all_to_all x1, blocking collectives, gather_column(): got = lax.all_to_all(copies, 'zh', 0, 0, tiled=True)  16.5 us
    all_to_all x1, starting transfers between devices, body(): column = lax.all_to_all(copies, ('zh', 'zl', 'core'), 0, 0, tiled=True)  15.3 us
    ppermute x3, starting transfers between devices, body(): lax.ppermute(done[step], GROUP, [(i, i ^ step) for i in range(SPLIT)])  14.2 us
    all_to_all x2, waiting for transfers between devices, gather_column(): got = lax.all_to_all(copies, 'zh', 0, 0, tiled=True)  13.7 us
    all_to_all x2, starting transfers between devices, gather_column(): got = lax.all_to_all(copies, 'zh', 0, 0, tiled=True)  9.24 us
  transfers between devices with their start and end apart: 13, of which 6 were waited for; matrix products, arithmetic and copies ran while one was open for 0% of the time, Pallas kernels for 2%

profile of v4, /device:TPU:1, one launch (start us, length us, event | category | flops | bytes accessed | tf_op | source)
XLA Modules:
  0.0 163.7 jit_solution(14995840349944180818)
XLA Ops:
  4.8 4.5 %collective-permute-start = (bf16[736,128]{1,0:T(8,128)(2,1)S(1)}, bf16[736,128]{1,0:T(8,128)(2,1)S(1)}, u32[]{:S(2)}, u32[]{:S(2)}) collective-permute-start(bf16[736,128]{1,0:T(8,128)(2,1)S(1)} %get-tuple-element.29.refs_0_.refs_4_), channel_id=1, source_target_pairs={{0,32},{32,0},{1,33},{33,1},{2,34},{34,2},{3,35},{35,3},{4,36},{36... | collective-permute-start | bytes 565256 | tf_op jit(solution)/shard_map/ppermute | solution.py:86
  9.3 15.3 %all-to-all-start = ((bf16[32,16,128]{2,1,0:T(8,128)(2,1)}), bf16[32,16,128]{2,1,0:T(8,128)(2,1)S(1)}, u32[]{:S(2)}, u32[]{:S(2)}) async-start(bf16[32,16,128]{2,1,0:T(8,128)(2,1)} %bitcast.12), calls=%async_computation | async-start | bytes 262144 | tf_op jit(solution)/shard_map/all_to_all | solution.py:268
  24.7 2.1 %collective-permute-start.2 = (bf16[736,128]{1,0:T(8,128)(2,1)S(1)}, bf16[736,128]{1,0:T(8,128)(2,1)S(1)}, u32[]{:S(2)}, u32[]{:S(2)}) collective-permute-start(bf16[736,128]{1,0:T(8,128)(2,1)S(1)} %collective-permute-done.refs_2_.refs_6_), channel_id=1, source_target_pairs={{0,1},{1,0},{2,3},{3,2},{4,5},{5,4},{6,7},{7,6},{8,9},{9,8},{10,11... | collective-permute-start | bytes 565256 | tf_op jit(solution)/shard_map/ppermute | solution.py:86
  29.0 3.3 %collective-permute-start.4 = (bf16[1984,128]{1,0:T(8,128)(2,1)S(1)}, bf16[1984,128]{1,0:T(8,128)(2,1)S(1)}, u32[]{:S(2)}, u32[]{:S(2)}) collective-permute-start(bf16[1984,128]{1,0:T(8,128)(2,1)S(1)} %shard_map.130.refs_0_.refs_4_.refs_8_), channel_id=1, source_target_pairs={{0,32},{32,0},{1,33},{33,1},{2,34},{34,2},{3,35},{35,3},{4,36},{36... | collective-permute-start | bytes 1523720 | tf_op jit(solution)/shard_map/ppermute | solution.py:86
  32.3 2.5 %collective-permute-start.1 = (bf16[736,128]{1,0:T(8,128)(2,1)S(1)}, bf16[736,128]{1,0:T(8,128)(2,1)S(1)}, u32[]{:S(2)}, u32[]{:S(2)}) collective-permute-start(bf16[736,128]{1,0:T(8,128)(2,1)S(1)} %get-tuple-element.29.refs_0_.refs_4_), channel_id=1, source_target_pairs={{0,1},{1,0},{2,3},{3,2},{4,5},{5,4},{6,7},{7,6},{8,9},{9,8},{10,11... | collective-permute-start | bytes 565256 | tf_op jit(solution)/shard_map/ppermute | solution.py:86
  35.9 4.6 %all-to-all-done = bf16[32,16,128]{2,1,0:T(8,128)(2,1)S(1)} async-done(((bf16[32,16,128]{2,1,0:T(8,128)(2,1)}), bf16[32,16,128]{2,1,0:T(8,128)(2,1)S(1)}, u32[]{:S(2)}, u32[]{:S(2)}) %all-to-all-start) | async-done | bytes 131104 | tf_op jit(solution)/shard_map/all_to_all | solution.py:268
  40.5 2.0 %shard_map.128 = (bf16[32,2,16,128]{3,2,1,0:T(8,128)(2,1)}, f32[4,4,16,128]{3,2,1,0:T(8,128)S(1)}) custom-call(s32[2]{0:T(128)S(1)} %pad_add_fusion.place, bf16[16,2,16,128]{3,2,1,0:T(8,128)(2,1)S(1)} %bitcast.48, bf16[736,128]{1,0:T(8,128)(2,1)S(1)} %get-tuple-element.29.refs_0_.refs_4_, bf16[736,128]{1,0:T(8,128)(2,1)S(1)} %collective-permute-done.1.refs_1_.refs_5_, ...), custom_call_target="tpu_custom_call" | custom-call | tf_op jit(solution)/shard_map/pallas_call | solution.py:300
  42.5 6.8 %all-to-all-start.1 = ((bf16[16,2,2,16,128]{4,3,2,1,0:T(8,128)(2,1)}), bf16[16,2,2,16,128]{4,3,2,1,0:T(8,128)(2,1)S(1)}, u32[]{:S(2)}, u32[]{:S(2)}) async-start(bf16[16,2,2,16,128]{4,3,2,1,0:T(8,128)(2,1)} %bitcast.14), calls=%async_computation.1 | async-start | bytes 524288 | tf_op jit(solution)/shard_map/all_to_all | solution.py:206
  49.3 3.9 %collective-permute-start.3 = (bf16[1984,128]{1,0:T(8,128)(2,1)S(1)}, bf16[1984,128]{1,0:T(8,128)(2,1)S(1)}, u32[]{:S(2)}, u32[]{:S(2)}) collective-permute-start(bf16[1984,128]{1,0:T(8,128)(2,1)S(1)} %shard_map.130.refs_0_.refs_4_.refs_8_), channel_id=1, source_target_pairs={{0,1},{1,0},{2,3},{3,2},{4,5},{5,4},{6,7},{7,6},{8,9},{9,8},{10,11... | collective-permute-start | bytes 1523720 | tf_op jit(solution)/shard_map/ppermute | solution.py:86
  53.2 1.9 %collective-permute-start.5 = (bf16[1984,128]{1,0:T(8,128)(2,1)S(1)}, bf16[1984,128]{1,0:T(8,128)(2,1)S(1)}, u32[]{:S(2)}, u32[]{:S(2)}) collective-permute-start(bf16[1984,128]{1,0:T(8,128)(2,1)S(1)} %collective-permute-done.4.refs_2_.refs_6_.refs_10_), channel_id=1, source_target_pairs={{0,1},{1,0},{2,3},{3,2},{4,5},{5,4},{6,7},{7,6},{8,9},{9,8},{10,11... | collective-permute-start | bytes 1523720 | tf_op jit(solution)/shard_map/ppermute | solution.py:86
  55.1 1.5 all-to-all-done.1.got
  58.0 5.9 %all-to-all-start.2 = ((bf16[8,2,2,16,128]{4,3,2,1,0:T(8,128)(2,1)}), bf16[8,2,2,16,128]{4,3,2,1,0:T(8,128)(2,1)S(1)}, u32[]{:S(2)}, u32[]{:S(2)}) async-start(bf16[8,2,2,16,128]{4,3,2,1,0:T(8,128)(2,1)} %get-tuple-element.32), calls=%async_computation.2 | async-start | bytes 262144 | tf_op jit(solution)/shard_map/all_to_all | solution.py:210
  63.9 13.7 %all-to-all-done.2 = bf16[8,2,2,16,128]{4,3,2,1,0:T(8,128)(2,1)S(1)} async-done(((bf16[8,2,2,16,128]{4,3,2,1,0:T(8,128)(2,1)}), bf16[8,2,2,16,128]{4,3,2,1,0:T(8,128)(2,1)S(1)}, u32[]{:S(2)}, u32[]{:S(2)}) %all-to-all-start.2) | async-done | bytes 131104 | tf_op jit(solution)/shard_map/all_to_all | solution.py:210
  77.6 2.4 %shard_map.131 = (bf16[32,2,16,128]{3,2,1,0:T(8,128)(2,1)S(1)}, f32[4,4,16,128]{3,2,1,0:T(8,128)}) custom-call(s32[2]{0:T(128)S(1)} %pad_add_fusion.place, bf16[16,2,16,128]{3,2,1,0:T(8,128)(2,1)S(1)} %bitcast.49, bf16[1984,128]{1,0:T(8,128)(2,1)S(1)} %shard_map.130.refs_0_.refs_4_.refs_8_, ...), custom_call_target="tpu_custom_call" | custom-call | tf_op jit(solution)/shard_map/pallas_call | solution.py:300
  80.0 10.6 %all_to_all.40.got = bf16[16,2,2,16,128]{4,3,2,1,0:T(8,128)(2,1)S(1)} all-to-all(bf16[16,2,2,16,128]{4,3,2,1,0:T(8,128)(2,1)S(1)} %bitcast.55), channel_id=1, replica_groups=mesh['zh'=8,'zl'=2,'x'=4,'y'=4,'core'=2] {'x','y'}, dimensions={0} | all-to-all | bytes 524288 | tf_op jit(solution)/shard_map/all_to_all | solution.py:206
  91.5 16.5 %all_to_all.41 = bf16[8,2,2,16,128]{4,3,2,1,0:T(8,128)(2,1)S(1)} all-to-all(bf16[8,2,2,16,128]{4,3,2,1,0:T(8,128)(2,1)S(1)} %get-tuple-element.35), channel_id=1, replica_groups=mesh['zh'=8,'zl'=2,'x'=4,'y'=4,'core'=2] {'zh'}, dimensions={0} | all-to-all | bytes 262144 | tf_op jit(solution)/shard_map/all_to_all | solution.py:210
  109.3 10.7 %all_to_all.42.got = bf16[16,2,2,16,128]{4,3,2,1,0:T(8,128)(2,1)S(1)} all-to-all(bf16[16,2,2,16,128]{4,3,2,1,0:T(8,128)(2,1)S(1)} %bitcast.56), channel_id=1, replica_groups=mesh['zh'=8,'zl'=2,'x'=4,'y'=4,'core'=2] {'x','y'}, dimensions={0} | all-to-all | bytes 524288 | tf_op jit(solution)/shard_map/all_to_all | solution.py:206
  121.4 3.4 %all-to-all-start.6 = ((bf16[8,2,2,16,128]{4,3,2,1,0:T(8,128)(2,1)}), bf16[8,2,2,16,128]{4,3,2,1,0:T(8,128)(2,1)S(1)}, u32[]{:S(2)}, u32[]{:S(2)}) async-start(bf16[8,2,2,16,128]{4,3,2,1,0:T(8,128)(2,1)} %get-tuple-element.38), calls=%async_computation.6 | async-start | bytes 262144 | tf_op jit(solution)/shard_map/all_to_all | solution.py:210
  124.8 9.4 %collective-permute-start.8 = (bf16[2,16,128]{2,1,0:T(8,128)(2,1)S(1)}, bf16[2,16,128]{2,1,0:T(8,128)(2,1)S(1)}, u32[]{:S(2)}, u32[]{:S(2)}) collective-permute-start(bf16[2,16,128]{2,1,0:T(8,128)(2,1)S(1)} %get-tuple-element.49), channel_id=1, source_target_pairs={{0,33},{1,32},{32,1},{33,0},{2,35},{3,34},{34,3},{35,2},{4,37},{5,... | collective-permute-start | bytes 24584 | tf_op jit(solution)/shard_map/ppermute | solution.py:347
  134.2 1.9 %collective-permute-start.6 = (bf16[2,16,128]{2,1,0:T(8,128)(2,1)S(1)}, bf16[2,16,128]{2,1,0:T(8,128)(2,1)S(1)}, u32[]{:S(2)}, u32[]{:S(2)}) collective-permute-start(bf16[2,16,128]{2,1,0:T(8,128)(2,1)S(1)} %get-tuple-element.51), channel_id=1, source_target_pairs={{0,1},{1,0},{32,33},{33,32},{2,3},{3,2},{34,35},{35,34},{4,5},{5,4... | collective-permute-start | bytes 24584 | tf_op jit(solution)/shard_map/ppermute | solution.py:347
  136.1 2.8 %collective-permute-start.7 = (bf16[2,16,128]{2,1,0:T(8,128)(2,1)S(1)}, bf16[2,16,128]{2,1,0:T(8,128)(2,1)S(1)}, u32[]{:S(2)}, u32[]{:S(2)}) collective-permute-start(bf16[2,16,128]{2,1,0:T(8,128)(2,1)S(1)} %get-tuple-element.52), channel_id=1, source_target_pairs={{0,32},{1,33},{32,0},{33,1},{2,34},{3,35},{34,2},{35,3},{4,36},{5,... | collective-permute-start | bytes 24584 | tf_op jit(solution)/shard_map/ppermute | solution.py:347
  139.0 1.8 %collective-permute-done.7.home_2 = bf16[2,16,128]{2,1,0:T(8,128)(2,1)S(1)} collective-permute-done((bf16[2,16,128]{2,1,0:T(8,128)(2,1)S(1)}, bf16[2,16,128]{2,1,0:T(8,128)(2,1)S(1)}, u32[]{:S(2)}, u32[]{:S(2)}) %collective-permute-start.7) | collective-permute-done | bytes 8224 | tf_op jit(solution)/shard_map/ppermute | solution.py:347
  140.8 2.4 %shard_map.135 = (bf16[2,32,16,128]{3,2,1,0:T(8,128)(2,1)S(1)}, f32[4,4,16,128]{3,2,1,0:T(8,128)}) custom-call(s32[2]{0:T(128)S(1)} %pad_add_fusion.place, bf16[16,2,16,128]{3,2,1,0:T(8,128)(2,1)S(1)} %bitcast.47, bf16[1984,128]{1,0:T(8,128)(2,1)S(1)} %shard_map.130.refs_0_.refs_4_.refs_8_, ...), custom_call_target="tpu_custom_call" | custom-call | tf_op jit(solution)/shard_map/pallas_call | solution.py:300
  143.3 19.1 %all_to_all.43 = bf16[64,16,128]{2,1,0:T(8,128)(2,1)S(1)} all-to-all(bf16[64,16,128]{2,1,0:T(8,128)(2,1)S(1)} %bitcast.54), channel_id=1, replica_groups=mesh['zh'=8,'zl'=2,'x'=4,'y'=4,'core'=2] {'zl','x','y','core'}, dimensions={0} | all-to-all | bytes 524288 | tf_op jit(solution)/shard_map/all_to_all | solution.py:350
  (51 shorter events, 14.2 us)
Async XLA Ops:
  0.0 0.7 copy-start.12
  0.0 0.7 copy-start.10
  0.0 0.7 copy-start.14
  0.8 1.0 copy-start
  1.7 0.9 copy-start.2
  2.6 0.8 copy-start.5
  3.4 24.6 %copy-start.3 = (bf16[1,1,3,1,128,128]{5,4,3,2,1,0:T(8,128)(2,1)S(1)}, bf16[1,1,3,1,128,128]{5,4,3,2,1,0:T(8,128)(2,1)}, u32[]{:S(2)}) copy-start(bf16[1,1,3,1,128,128]{5,4,3,2,1,0:T(8,128)(2,1)} %param.14) | copy-start | bytes 294916
  3.4 24.6 %copy-start.4 = (bf16[1,1,3,1,128,128]{5,4,3,2,1,0:T(8,128)(2,1)S(1)}, bf16[1,1,3,1,128,128]{5,4,3,2,1,0:T(8,128)(2,1)}, u32[]{:S(2)}) copy-start(bf16[1,1,3,1,128,128]{5,4,3,2,1,0:T(8,128)(2,1)} %param.15) | copy-start | bytes 294916
  3.4 24.6 %copy-start.6 = (bf16[1,1,3,1,64,128]{5,4,3,2,1,0:T(8,128)(2,1)S(1)}, bf16[1,1,3,1,64,128]{5,4,3,2,1,0:T(8,128)(2,1)}, u32[]{:S(2)}) copy-start(bf16[1,1,3,1,64,128]{5,4,3,2,1,0:T(8,128)(2,1)} %param.13) | copy-start | bytes 147460
  3.4 24.6 %copy-start.7 = (bf16[1,1,2,4,128,128]{5,4,3,2,1,0:T(8,128)(2,1)S(1)}, bf16[1,1,2,4,128,128]{5,4,3,2,1,0:T(8,128)(2,1)}, u32[]{:S(2)}) copy-start(bf16[1,1,2,4,128,128]{5,4,3,2,1,0:T(8,128)(2,1)} %param.21) | copy-start | bytes 786436
  4.8 23.2 %copy-start.1 = (bf16[1,1,2,4,128,128]{5,4,3,2,1,0:T(8,128)(2,1)S(1)}, bf16[1,1,2,4,128,128]{5,4,3,2,1,0:T(8,128)(2,1)}, u32[]{:S(2)}) copy-start(bf16[1,1,2,4,128,128]{5,4,3,2,1,0:T(8,128)(2,1)} %param.16) | copy-start | bytes 786436
  4.8 19.8 %collective-permute-start = (bf16[736,128]{1,0:T(8,128)(2,1)S(1)}, bf16[736,128]{1,0:T(8,128)(2,1)S(1)}, u32[]{:S(2)}, u32[]{:S(2)}) collective-permute-start(bf16[736,128]{1,0:T(8,128)(2,1)S(1)} %get-tuple-element.29.refs_0_.refs_4_), channel_id=1, source_target_pairs={{0,32},{32,0},{1,33},{33,1},{2,34},{34,2},{3,35},{35,3},{4,36},{36... | collective-permute-start | bytes 565256 | tf_op jit(solution)/shard_map/ppermute | solution.py:86
  9.3 31.2 %all-to-all-start = ((bf16[32,16,128]{2,1,0:T(8,128)(2,1)}), bf16[32,16,128]{2,1,0:T(8,128)(2,1)S(1)}, u32[]{:S(2)}, u32[]{:S(2)}) async-start(bf16[32,16,128]{2,1,0:T(8,128)(2,1)} %bitcast.12), calls=%async_computation | async-start | bytes 262144 | tf_op jit(solution)/shard_map/all_to_all | solution.py:268
  24.7 3.3 %collective-permute-start.2 = (bf16[736,128]{1,0:T(8,128)(2,1)S(1)}, bf16[736,128]{1,0:T(8,128)(2,1)S(1)}, u32[]{:S(2)}, u32[]{:S(2)}) collective-permute-start(bf16[736,128]{1,0:T(8,128)(2,1)S(1)} %collective-permute-done.refs_2_.refs_6_), channel_id=1, source_target_pairs={{0,1},{1,0},{2,3},{3,2},{4,5},{5,4},{6,7},{7,6},{8,9},{9,8},{10,11... | collective-permute-start | bytes 565256 | tf_op jit(solution)/shard_map/ppermute | solution.py:86
  29.0 24.2 %collective-permute-start.4 = (bf16[1984,128]{1,0:T(8,128)(2,1)S(1)}, bf16[1984,128]{1,0:T(8,128)(2,1)S(1)}, u32[]{:S(2)}, u32[]{:S(2)}) collective-permute-start(bf16[1984,128]{1,0:T(8,128)(2,1)S(1)} %shard_map.130.refs_0_.refs_4_.refs_8_), channel_id=1, source_target_pairs={{0,32},{32,0},{1,33},{33,1},{2,34},{34,2},{3,35},{35,3},{4,36},{36... | collective-permute-start | bytes 1523720 | tf_op jit(solution)/shard_map/ppermute | solution.py:86
  32.3 3.6 %collective-permute-start.1 = (bf16[736,128]{1,0:T(8,128)(2,1)S(1)}, bf16[736,128]{1,0:T(8,128)(2,1)S(1)}, u32[]{:S(2)}, u32[]{:S(2)}) collective-permute-start(bf16[736,128]{1,0:T(8,128)(2,1)S(1)} %get-tuple-element.29.refs_0_.refs_4_), channel_id=1, source_target_pairs={{0,1},{1,0},{2,3},{3,2},{4,5},{5,4},{6,7},{7,6},{8,9},{9,8},{10,11... | collective-permute-start | bytes 565256 | tf_op jit(solution)/shard_map/ppermute | solution.py:86
  42.5 14.1 %all-to-all-start.1 = ((bf16[16,2,2,16,128]{4,3,2,1,0:T(8,128)(2,1)}), bf16[16,2,2,16,128]{4,3,2,1,0:T(8,128)(2,1)S(1)}, u32[]{:S(2)}, u32[]{:S(2)}) async-start(bf16[16,2,2,16,128]{4,3,2,1,0:T(8,128)(2,1)} %bitcast.14), calls=%async_computation.1 | async-start | bytes 524288 | tf_op jit(solution)/shard_map/all_to_all | solution.py:206
  49.3 14.6 %collective-permute-start.3 = (bf16[1984,128]{1,0:T(8,128)(2,1)S(1)}, bf16[1984,128]{1,0:T(8,128)(2,1)S(1)}, u32[]{:S(2)}, u32[]{:S(2)}) collective-permute-start(bf16[1984,128]{1,0:T(8,128)(2,1)S(1)} %shard_map.130.refs_0_.refs_4_.refs_8_), channel_id=1, source_target_pairs={{0,1},{1,0},{2,3},{3,2},{4,5},{5,4},{6,7},{7,6},{8,9},{9,8},{10,11... | collective-permute-start | bytes 1523720 | tf_op jit(solution)/shard_map/ppermute | solution.py:86
  53.2 24.4 %collective-permute-start.5 = (bf16[1984,128]{1,0:T(8,128)(2,1)S(1)}, bf16[1984,128]{1,0:T(8,128)(2,1)S(1)}, u32[]{:S(2)}, u32[]{:S(2)}) collective-permute-start(bf16[1984,128]{1,0:T(8,128)(2,1)S(1)} %collective-permute-done.4.refs_2_.refs_6_.refs_10_), channel_id=1, source_target_pairs={{0,1},{1,0},{2,3},{3,2},{4,5},{5,4},{6,7},{7,6},{8,9},{9,8},{10,11... | collective-permute-start | bytes 1523720 | tf_op jit(solution)/shard_map/ppermute | solution.py:86
  58.0 19.6 %all-to-all-start.2 = ((bf16[8,2,2,16,128]{4,3,2,1,0:T(8,128)(2,1)}), bf16[8,2,2,16,128]{4,3,2,1,0:T(8,128)(2,1)S(1)}, u32[]{:S(2)}, u32[]{:S(2)}) async-start(bf16[8,2,2,16,128]{4,3,2,1,0:T(8,128)(2,1)} %get-tuple-element.32), calls=%async_computation.2 | async-start | bytes 262144 | tf_op jit(solution)/shard_map/all_to_all | solution.py:210
  121.4 19.5 %all-to-all-start.6 = ((bf16[8,2,2,16,128]{4,3,2,1,0:T(8,128)(2,1)}), bf16[8,2,2,16,128]{4,3,2,1,0:T(8,128)(2,1)S(1)}, u32[]{:S(2)}, u32[]{:S(2)}) async-start(bf16[8,2,2,16,128]{4,3,2,1,0:T(8,128)(2,1)} %get-tuple-element.38), calls=%async_computation.6 | async-start | bytes 262144 | tf_op jit(solution)/shard_map/all_to_all | solution.py:210
  124.8 14.2 %collective-permute-start.8 = (bf16[2,16,128]{2,1,0:T(8,128)(2,1)S(1)}, bf16[2,16,128]{2,1,0:T(8,128)(2,1)S(1)}, u32[]{:S(2)}, u32[]{:S(2)}) collective-permute-start(bf16[2,16,128]{2,1,0:T(8,128)(2,1)S(1)} %get-tuple-element.49), channel_id=1, source_target_pairs={{0,33},{1,32},{32,1},{33,0},{2,35},{3,34},{34,3},{35,2},{4,37},{5,... | collective-permute-start | bytes 24584 | tf_op jit(solution)/shard_map/ppermute | solution.py:347
  134.2 4.8 %collective-permute-start.6 = (bf16[2,16,128]{2,1,0:T(8,128)(2,1)S(1)}, bf16[2,16,128]{2,1,0:T(8,128)(2,1)S(1)}, u32[]{:S(2)}, u32[]{:S(2)}) collective-permute-start(bf16[2,16,128]{2,1,0:T(8,128)(2,1)S(1)} %get-tuple-element.51), channel_id=1, source_target_pairs={{0,1},{1,0},{32,33},{33,32},{2,3},{3,2},{34,35},{35,34},{4,5},{5,4... | collective-permute-start | bytes 24584 | tf_op jit(solution)/shard_map/ppermute | solution.py:347
  136.1 4.7 %collective-permute-start.7 = (bf16[2,16,128]{2,1,0:T(8,128)(2,1)S(1)}, bf16[2,16,128]{2,1,0:T(8,128)(2,1)S(1)}, u32[]{:S(2)}, u32[]{:S(2)}) collective-permute-start(bf16[2,16,128]{2,1,0:T(8,128)(2,1)S(1)} %get-tuple-element.52), channel_id=1, source_target_pairs={{0,32},{1,33},{32,0},{33,1},{2,34},{3,35},{34,2},{35,3},{4,36},{5,... | collective-permute-start | bytes 24584 | tf_op jit(solution)/shard_map/ppermute | solution.py:347
  (5 other events, 3.5 us)

commit v5 on v4

--- a/solution.py
+++ b/solution.py
@@ -42,13 +42,14 @@
     return pl.BlockSpec(memory_space=pltpu.SMEM)
 
 
-def first_kernel(
-    sides_1, sides_2, inv_1, inv_2, tiles, rows, ls, lt, lc, us, ut, uc, packed, copies, forward, index
-):
-    solved = jnp.dot(sides_2[0], inv_2[0], preferred_element_type=F32).astype(BF16)
+def top_kernel(sides, inverse, copies, forward):
+    solved = jnp.dot(sides[0], inverse[0], preferred_element_type=F32).astype(BF16)
     forward[...] = solved
     for i in range(copies.shape[0]):
         copies[i] = solved
+
+
+def first_kernel(sides_1, inv_1, tiles, rows, ls, lt, lc, us, ut, uc, packed, index):
     blocks, extent = tiles.shape[1], tiles.shape[2]
     for b, table in enumerate(row_table(rows[0])):
         packed[b * extent : (b + 1) * extent] = moved_columns(tiles[0, b], table)
@@ -142,6 +143,38 @@
     lax.fori_loop(0, targets, one_target, 0, unroll=4)
 
 
+def scatter_kernel(group, level, by_target, after, place, table, column, *refs):
+    tiles, before = refs[:SPLIT], refs[SPLIT] if after else None
+    partial, terms, sums = (refs[-2], None, refs[-1]) if after else refs[-3:]
+    zl, core = place[0], place[1]
+    extent = column.shape[3]
+    blocks = tiles[0].shape[0] // extent
+    targets = partial.shape[1] if by_target else partial.shape[0]
+    sums[...] = jnp.zeros(sums.shape, F32)
+
+    def add(step, entry, row, term):
+        goal = table[step, entry] - level * targets
+        slot = jnp.where((goal >= 0) & (goal < targets), goal, targets)
+        at = (pl.ds(row, 1), pl.ds(slot, 1)) if by_target else (pl.ds(slot, 1), pl.ds(row, 1))
+        sums[at] = sums[at] + term[None, None]
+
+    for step, (dz, dc) in enumerate(offsets()):
+        half, row = lax.bitwise_xor(core, dc), lax.bitwise_xor(zl, dz)
+        for b in range(blocks):
+            source = jnp.clip(table[step, 2 * blocks * group + b], 0, column.shape[0] - 1)
+            term = jnp.dot(
+                column[pl.ds(source, 1), pl.ds(half, 1)][0, 0],
+                tiles[step][b * extent : (b + 1) * extent],
+                preferred_element_type=F32,
+            )
+            if not after:
+                terms[step, b] = term
+            add(step, 2 * blocks * group + blocks + b, row, term)
+            if after:
+                add(step, 2 * blocks * (group - 1) + blocks + b, row, before[step, b])
+    partial[...] = (sums[:, :targets] if by_target else sums[:targets]).astype(BF16)
+
+
 def full_product(operand, inverse):
     high = operand.astype(BF16)
     rest = operand - high.astype(F32)
@@ -241,37 +274,41 @@
     tile_rows = blocks * extent
 
     first_sizes = [tile_rows, extent, side_extent, 8 * blocks]
-    packed, copies, forward_2 = pl.pallas_call(
-        first_kernel,
+    copies, forward_2 = pl.pallas_call(
+        top_kernel,
         grid=(1,),
-        in_specs=[one_of(sides, 1), one_of(sides, 2), one_of(low_inv, 1), one_of(low_inv, 2)]
-        + [one_of(low_tiles, 0), one_of(low_rows, 0)]
-        + [scalars()] * 6,
+        in_specs=[one_of(sides, 2), one_of(low_inv, 2)],
         out_shape=[
-            jax.ShapeDtypeStruct((sum(first_sizes), extent), BF16),
             jax.ShapeDtypeStruct((high, side_extent, extent), BF16),
             jax.ShapeDtypeStruct((side_extent, extent), BF16),
         ],
         out_specs=[
-            pl.BlockSpec((sum(first_sizes), extent), lambda i: (0, 0)),
             pl.BlockSpec((high, side_extent, extent), lambda i: (0, 0, 0)),
             pl.BlockSpec((side_extent, extent), lambda i: (0, 0)),
         ],
+        compiler_params=pltpu.CompilerParams(vmem_limit_bytes=56 << 20),
+    )(sides, low_inv)
+    packed = pl.pallas_call(
+        first_kernel,
+        grid=(1,),
+        in_specs=[one_of(sides, 1), one_of(low_inv, 1), one_of(low_tiles, 0), one_of(low_rows, 0)]
+        + [scalars()] * 6,
+        out_shape=jax.ShapeDtypeStruct((sum(first_sizes), extent), BF16),
+        out_specs=pl.BlockSpec((sum(first_sizes), extent), lambda i: (0, 0)),
         scratch_shapes=[pltpu.VMEM((8 * blocks, extent), jnp.int32)],
         compiler_params=pltpu.CompilerParams(vmem_limit_bytes=16 << 20),
     )(
-        *(sides, sides, low_inv, low_inv, low_tiles, low_rows),
+        *(sides, low_inv, low_tiles, low_rows),
         *(low_source, low_target, low_count, up_source, up_target, up_count),
     )
     z_mate = swapped(packed, "zl")
     copies = copies.reshape(-1, rows, extent)
     column = lax.all_to_all(copies, ("zh", "zl", "core"), 0, 0, tiled=True)
     column = column.reshape(-1, cores, rows, extent)
-    packed, z_mate = lax.optimization_barrier((packed, z_mate))
     first = (packed, swapped(packed, "core"), z_mate, swapped(z_mate, "core"))
 
     later_sizes = [tile_rows] * 3 + [extent] * 3 + [side_extent]
-    start = first[3][:16]
+    start = packed[:16]
     packed = pl.pallas_call(
         later_kernel,
         grid=(1,),
@@ -292,22 +329,34 @@
 
     index_block = rows_of(first_sizes, 3)
 
+    table = jnp.stack([buffer[-8 * blocks :, 0] for buffer in first])
+    table = table.astype(F32).astype(jnp.int32)
+
     def edge(column, buffers, tile_block, group, level, before=None, by_target=False):
         shape = (row_group, pair) if not by_target else (pair, row_group)
         partial = jax.ShapeDtypeStruct(shape + (rows, extent), BF16)
         terms = jax.ShapeDtypeStruct((SPLIT, blocks, rows, extent), F32)
         extra = () if before is None else (before,)
+        extra_specs = [whole(array) for array in extra]
+        if group == 0:
+            kernel, scratch = spread_kernel, []
+            in_specs = [scalars(), whole(column)] + [tile_block] * SPLIT + [index_block] * SPLIT
+            arrays = (place, column, *buffers, *first)
+        else:
+            kernel = scatter_kernel
+            sums = (row_group + 1, pair) if not by_target else (pair, row_group + 1)
+            scratch = [pltpu.VMEM(sums + (rows, extent), F32)]
+            in_specs = [scalars(), scalars(), whole(column)] + [tile_block] * SPLIT
+            arrays = (place, table, column, *buffers)
         return pl.pallas_call(
-            functools.partial(spread_kernel, group, level, by_target, before is not None),
+            functools.partial(kernel, group, level, by_target, before is not None),
             grid=(1,),
-            in_specs=[scalars(), whole(column)]
-            + [tile_block] * SPLIT
-            + [index_block] * SPLIT
-            + [whole(array) for array in extra],
-            out_shape=[partial, terms],
-            out_specs=[whole(partial), whole(terms)],
+            in_specs=in_specs + extra_specs,
+            out_shape=[partial, terms] if before is None else [partial],
+            out_specs=[whole(partial), whole(terms)] if before is None else [whole(partial)],
+            scratch_shapes=scratch,
             compiler_params=pltpu.CompilerParams(vmem_limit_bytes=16 << 20),
-        )(place, column, *buffers, *first, *extra)
+        )(*arrays, *extra)
 
     def solve(kind, got, *pieces):
         solved = jax.ShapeDtypeStruct((SPLIT, rows, extent), BF16)
@@ -330,7 +379,7 @@
     inverse, side = rows_of(first_sizes, 1), rows_of(first_sizes, 2)
     forward_1, copies = solve(0, got, (first, inverse), (first, side))
     column = gather_column(copies)
-    partial, _ = edge(column, later, rows_of(later_sizes, 0), 1, 0, terms)
+    (partial,) = edge(column, later, rows_of(later_sizes, 0), 1, 0, terms)
     got = row_exchange(partial)
     inverse, upper, side = (rows_of(later_sizes, i) for i in (3, 4, 6))
     solution_0, copies = solve(1, got, (later, inverse), (later, side), (later, upper))
@@ -346,7 +395,7 @@
     for step in range(1, SPLIT):
         home.append(lax.ppermute(done[step], GROUP, [(i, i ^ step) for i in range(SPLIT)]))
     column, *home = lax.optimization_barrier((column, *home))
-    partial, _ = edge(column, later, rows_of(later_sizes, 2), 3, 1, terms, by_target=True)
+    (partial,) = edge(column, later, rows_of(later_sizes, 2), 3, 1, terms, by_target=True)
     got = lax.all_to_all(partial.reshape(-1, rows, extent), ("zl", "x", "y", "core"), 0, 0, tiled=True)
     got = got.reshape(pair, row_group // cores, cores, rows, extent)
     result = jax.ShapeDtypeStruct(sides.shape, BF16)

time: 165 us -> 160 us (0.970)
  waiting for transfers between devices: 23.8 us -> 18.9 us
  starting transfers between devices: 63.8 us -> 66.8 us
  Pallas kernels: 14.8 us -> 12.3 us
  local copies, waits for them, and re-layouts: 4.03 us -> 1.81 us
  blocking collectives: 56.9 us -> 58.7 us
    all_to_all x1, waiting for transfers between devices: 4.62 us -> 0.01 us  [body(): column = lax.all_to_all(copies, ('zh', 'zl', 'core'), 0, 0, tiled=True)]
    all_to_all x2, starting transfers between devices: 9.24 us -> 13.5 us  [gather_column(): got = lax.all_to_all(copies, 'zh', 0, 0, tiled=True)]
    unnamed x32 -> x28, local copies, waits for them, and re-layouts: 4.03 us -> 1.36 us
    pallas_call x4 -> x5, Pallas kernels: 8.15 us -> 6.23 us  [the longest x4 4.62 us: edge(): pl.pallas_call(functools.partial(kernel, group, level, by_target, before...]
  transfers between devices with their start and end apart: 13 -> 13, of which waited for: 6 -> 5; matrix products, arithmetic and copies ran while one was open for 0% -> 0% of each run, Pallas kernels for 2% -> 3%
where the time goes in v5:
time: 160 us; the launch traced here: 159 us
  starting transfers between devices  66.8 us (42%)
  blocking collectives  58.7 us (37%)
  waiting for transfers between devices  18.9 us (12%)
  Pallas kernels  12.3 us (8%)
  local copies, waits for them, and re-layouts  1.81 us (1%)
    all_to_all x2, blocking collectives, row_exchange(): return lax.all_to_all(chunks, ('x', 'y'), 0, 0, tiled=True)  21.8 us
    all_to_all x1, blocking collectives, body(): lax.all_to_all(partial.reshape(-1, rows, extent), ('zl', 'x', 'y', 'core'...  19.2 us
    all_to_all x1, blocking collectives, gather_column(): got = lax.all_to_all(copies, 'zh', 0, 0, tiled=True)  17.7 us
    all_to_all x1, starting transfers between devices, body(): column = lax.all_to_all(copies, ('zh', 'zl', 'core'), 0, 0, tiled=True)  16.9 us
    ppermute x6, starting transfers between devices, swapped(): return lax.ppermute(value, axis, [(0, 1), (1, 0)])  16.8 us
    all_to_all x2, starting transfers between devices, gather_column(): got = lax.all_to_all(copies, 'zh', 0, 0, tiled=True)  13.5 us
    all_to_all x2, waiting for transfers between devices, gather_column(): got = lax.all_to_all(copies, 'zh', 0, 0, tiled=True)  13.1 us
    ppermute x3, starting transfers between devices, body(): lax.ppermute(done[step], GROUP, [(i, i ^ step) for i in range(SPLIT)])  12.8 us
  transfers between devices with their start and end apart: 13, of which 5 were waited for; matrix products, arithmetic and copies ran while one was open for 0% of the time, Pallas kernels for 3%

profile of v5, /device:TPU:1, one launch (start us, length us, event | category | flops | bytes accessed | tf_op | source)
XLA Modules:
  0.0 158.9 jit_solution(15489695655173050471)
XLA Ops:
  0.0 1.6 %shard_map.128 = (bf16[8,64,128]{2,1,0:T(8,128)(2,1)}, bf16[64,128]{1,0:T(8,128)(2,1)}) custom-call(bf16[3,64,128]{2,1,0:T(8,128)(2,1)} %bitcast.57, bf16[3,128,128]{2,1,0:T(8,128)(2,1)} %bitcast.47), custom_call_target="tpu_custom_call" | custom-call | tf_op jit(solution)/shard_map/pallas_call | solution.py:277
  1.6 16.9 %all-to-all-start = ((bf16[32,16,128]{2,1,0:T(8,128)(2,1)}), bf16[32,16,128]{2,1,0:T(8,128)(2,1)S(1)}, u32[]{:S(2)}, u32[]{:S(2)}) async-start(bf16[32,16,128]{2,1,0:T(8,128)(2,1)} %bitcast.73), calls=%async_computation | async-start | bytes 262144 | tf_op jit(solution)/shard_map/all_to_all | solution.py:306
  20.1 3.3 %collective-permute-start.1 = (bf16[736,128]{1,0:T(8,128)(2,1)S(1)}, bf16[736,128]{1,0:T(8,128)(2,1)S(1)}, u32[]{:S(2)}, u32[]{:S(2)}) collective-permute-start(bf16[736,128]{1,0:T(8,128)(2,1)S(1)} %shard_map.127.refs_0_.refs_4_), channel_id=1, source_target_pairs={{0,32},{32,0},{1,33},{33,1},{2,34},{34,2},{3,35},{35,3},{4,36},{36... | collective-permute-start | bytes 565256 | tf_op jit(solution)/shard_map/ppermute | solution.py:87
  24.4 2.0 %collective-permute-start.4 = (bf16[1984,128]{1,0:T(8,128)(2,1)S(1)}, bf16[1984,128]{1,0:T(8,128)(2,1)S(1)}, u32[]{:S(2)}, u32[]{:S(2)}) collective-permute-start(bf16[1984,128]{1,0:T(8,128)(2,1)S(1)} %shard_map.131.refs_0_.refs_4_.refs_8_), channel_id=1, source_target_pairs={{0,32},{32,0},{1,33},{33,1},{2,34},{34,2},{3,35},{35,3},{4,36},{36... | collective-permute-start | bytes 1523720 | tf_op jit(solution)/shard_map/ppermute | solution.py:87
  26.4 2.7 %collective-permute-start = (bf16[736,128]{1,0:T(8,128)(2,1)S(1)}, bf16[736,128]{1,0:T(8,128)(2,1)S(1)}, u32[]{:S(2)}, u32[]{:S(2)}) collective-permute-start(bf16[736,128]{1,0:T(8,128)(2,1)S(1)} %shard_map.127.refs_0_.refs_4_), channel_id=1, source_target_pairs={{0,1},{1,0},{2,3},{3,2},{4,5},{5,4},{6,7},{7,6},{8,9},{9,8},{10,11... | collective-permute-start | bytes 565256 | tf_op jit(solution)/shard_map/ppermute | solution.py:87
  30.4 3.3 %collective-permute-start.2 = (bf16[736,128]{1,0:T(8,128)(2,1)S(1)}, bf16[736,128]{1,0:T(8,128)(2,1)S(1)}, u32[]{:S(2)}, u32[]{:S(2)}) collective-permute-start(bf16[736,128]{1,0:T(8,128)(2,1)S(1)} %collective-permute-done.1.refs_2_.refs_6_), channel_id=1, source_target_pairs={{0,1},{1,0},{2,3},{3,2},{4,5},{5,4},{6,7},{7,6},{8,9},{9,8},{10,11... | collective-permute-start | bytes 565256 | tf_op jit(solution)/shard_map/ppermute | solution.py:87
  34.7 2.0 %shard_map.129 = (bf16[32,2,16,128]{3,2,1,0:T(8,128)(2,1)}, f32[4,4,16,128]{3,2,1,0:T(8,128)S(1)}) custom-call(s32[2]{0:T(128)S(1)} %pad_add_fusion.place, bf16[16,2,16,128]{3,2,1,0:T(8,128)(2,1)S(1)} %bitcast.53, bf16[736,128]{1,0:T(8,128)(2,1)S(1)} %shard_map.127.refs_0_.refs_4_, bf16[736,128]{1,0:T(8,128)(2,1)S(1)} %collective-permute-done.refs_1_.refs_5_, ...), custom_call_target="tpu_custom_call" | custom-call | tf_op jit(solution)/shard_map/pallas_call | solution.py:351
  36.8 6.8 %all-to-all-start.1 = ((bf16[16,2,2,16,128]{4,3,2,1,0:T(8,128)(2,1)}), bf16[16,2,2,16,128]{4,3,2,1,0:T(8,128)(2,1)S(1)}, u32[]{:S(2)}, u32[]{:S(2)}) async-start(bf16[16,2,2,16,128]{4,3,2,1,0:T(8,128)(2,1)} %bitcast.14), calls=%async_computation.1 | async-start | bytes 524288 | tf_op jit(solution)/shard_map/all_to_all | solution.py:239
  43.5 3.6 %collective-permute-start.3 = (bf16[1984,128]{1,0:T(8,128)(2,1)S(1)}, bf16[1984,128]{1,0:T(8,128)(2,1)S(1)}, u32[]{:S(2)}, u32[]{:S(2)}) collective-permute-start(bf16[1984,128]{1,0:T(8,128)(2,1)S(1)} %shard_map.131.refs_0_.refs_4_.refs_8_), channel_id=1, source_target_pairs={{0,1},{1,0},{2,3},{3,2},{4,5},{5,4},{6,7},{7,6},{8,9},{9,8},{10,11... | collective-permute-start | bytes 1523720 | tf_op jit(solution)/shard_map/ppermute | solution.py:87
  47.1 1.9 %collective-permute-start.5 = (bf16[1984,128]{1,0:T(8,128)(2,1)S(1)}, bf16[1984,128]{1,0:T(8,128)(2,1)S(1)}, u32[]{:S(2)}, u32[]{:S(2)}) collective-permute-start(bf16[1984,128]{1,0:T(8,128)(2,1)S(1)} %collective-permute-done.4.refs_2_.refs_6_.refs_10_), channel_id=1, source_target_pairs={{0,1},{1,0},{2,3},{3,2},{4,5},{5,4},{6,7},{7,6},{8,9},{9,8},{10,11... | collective-permute-start | bytes 1523720 | tf_op jit(solution)/shard_map/ppermute | solution.py:87
  49.1 1.8 %all-to-all-done.1.got = bf16[16,2,2,16,128]{4,3,2,1,0:T(8,128)(2,1)S(1)} async-done(((bf16[16,2,2,16,128]{4,3,2,1,0:T(8,128)(2,1)}), bf16[16,2,2,16,128]{4,3,2,1,0:T(8,128)(2,1)S(1)}, u32[]{:S(2)}, u32[]{:S(2)}) %all-to-all-start.1) | async-done | bytes 262176 | tf_op jit(solution)/shard_map/all_to_all | solution.py:239
  50.8 1.4 shard_map.130
  52.2 10.2 %all-to-all-start.2 = ((bf16[8,2,2,16,128]{4,3,2,1,0:T(8,128)(2,1)}), bf16[8,2,2,16,128]{4,3,2,1,0:T(8,128)(2,1)S(1)}, u32[]{:S(2)}, u32[]{:S(2)}) async-start(bf16[8,2,2,16,128]{4,3,2,1,0:T(8,128)(2,1)} %get-tuple-element.24), calls=%async_computation.2 | async-start | bytes 262144 | tf_op jit(solution)/shard_map/all_to_all | solution.py:243
  62.9 13.1 %all-to-all-done.2 = bf16[8,2,2,16,128]{4,3,2,1,0:T(8,128)(2,1)S(1)} async-done(((bf16[8,2,2,16,128]{4,3,2,1,0:T(8,128)(2,1)}), bf16[8,2,2,16,128]{4,3,2,1,0:T(8,128)(2,1)S(1)}, u32[]{:S(2)}, u32[]{:S(2)}) %all-to-all-start.2) | async-done | bytes 131104 | tf_op jit(solution)/shard_map/all_to_all | solution.py:243
  76.9 10.9 %all_to_all.40.got = bf16[16,2,2,16,128]{4,3,2,1,0:T(8,128)(2,1)S(1)} all-to-all(bf16[16,2,2,16,128]{4,3,2,1,0:T(8,128)(2,1)S(1)} %bitcast.43), channel_id=1, replica_groups=mesh['zh'=8,'zl'=2,'x'=4,'y'=4,'core'=2] {'x','y'}, dimensions={0} | all-to-all | bytes 524288 | tf_op jit(solution)/shard_map/all_to_all | solution.py:239
  88.7 17.7 %all_to_all.41 = bf16[8,2,2,16,128]{4,3,2,1,0:T(8,128)(2,1)S(1)} all-to-all(bf16[8,2,2,16,128]{4,3,2,1,0:T(8,128)(2,1)S(1)} %get-tuple-element.26), channel_id=1, replica_groups=mesh['zh'=8,'zl'=2,'x'=4,'y'=4,'core'=2] {'zh'}, dimensions={0} | all-to-all | bytes 262144 | tf_op jit(solution)/shard_map/all_to_all | solution.py:243
  107.2 10.8 %all_to_all.42.got = bf16[16,2,2,16,128]{4,3,2,1,0:T(8,128)(2,1)S(1)} all-to-all(bf16[16,2,2,16,128]{4,3,2,1,0:T(8,128)(2,1)S(1)} %bitcast.60), channel_id=1, replica_groups=mesh['zh'=8,'zl'=2,'x'=4,'y'=4,'core'=2] {'x','y'}, dimensions={0} | all-to-all | bytes 524288 | tf_op jit(solution)/shard_map/all_to_all | solution.py:239
  118.0 1.4 shard_map.135
  119.4 3.4 %all-to-all-start.6 = ((bf16[8,2,2,16,128]{4,3,2,1,0:T(8,128)(2,1)}), bf16[8,2,2,16,128]{4,3,2,1,0:T(8,128)(2,1)S(1)}, u32[]{:S(2)}, u32[]{:S(2)}) async-start(bf16[8,2,2,16,128]{4,3,2,1,0:T(8,128)(2,1)} %get-tuple-element.29), calls=%async_computation.6 | async-start | bytes 262144 | tf_op jit(solution)/shard_map/all_to_all | solution.py:243
  122.8 7.8 %collective-permute-start.8 = (bf16[2,16,128]{2,1,0:T(8,128)(2,1)S(1)}, bf16[2,16,128]{2,1,0:T(8,128)(2,1)S(1)}, u32[]{:S(2)}, u32[]{:S(2)}) collective-permute-start(bf16[2,16,128]{2,1,0:T(8,128)(2,1)S(1)} %get-tuple-element.39), channel_id=1, source_target_pairs={{0,33},{1,32},{32,1},{33,0},{2,35},{3,34},{34,3},{35,2},{4,37},{5,... | collective-permute-start | bytes 24584 | tf_op jit(solution)/shard_map/ppermute | solution.py:396
  130.6 1.9 %collective-permute-start.6 = (bf16[2,16,128]{2,1,0:T(8,128)(2,1)S(1)}, bf16[2,16,128]{2,1,0:T(8,128)(2,1)S(1)}, u32[]{:S(2)}, u32[]{:S(2)}) collective-permute-start(bf16[2,16,128]{2,1,0:T(8,128)(2,1)S(1)} %get-tuple-element.41), channel_id=1, source_target_pairs={{0,1},{1,0},{32,33},{33,32},{2,3},{3,2},{34,35},{35,34},{4,5},{5,4... | collective-permute-start | bytes 24584 | tf_op jit(solution)/shard_map/ppermute | solution.py:396
  132.5 3.1 %collective-permute-start.7 = (bf16[2,16,128]{2,1,0:T(8,128)(2,1)S(1)}, bf16[2,16,128]{2,1,0:T(8,128)(2,1)S(1)}, u32[]{:S(2)}, u32[]{:S(2)}) collective-permute-start(bf16[2,16,128]{2,1,0:T(8,128)(2,1)S(1)} %get-tuple-element.42), channel_id=1, source_target_pairs={{0,32},{1,33},{32,0},{33,1},{2,34},{3,35},{34,2},{35,3},{4,36},{5,... | collective-permute-start | bytes 24584 | tf_op jit(solution)/shard_map/ppermute | solution.py:396
  135.7 1.8 %collective-permute-done.7.home_2 = bf16[2,16,128]{2,1,0:T(8,128)(2,1)S(1)} collective-permute-done((bf16[2,16,128]{2,1,0:T(8,128)(2,1)S(1)}, bf16[2,16,128]{2,1,0:T(8,128)(2,1)S(1)}, u32[]{:S(2)}, u32[]{:S(2)}) %collective-permute-start.7) | collective-permute-done | bytes 8224 | tf_op jit(solution)/shard_map/ppermute | solution.py:396
  138.3 19.2 %all_to_all.43 = bf16[64,16,128]{2,1,0:T(8,128)(2,1)S(1)} all-to-all(bf16[64,16,128]{2,1,0:T(8,128)(2,1)S(1)} %bitcast.42), channel_id=1, replica_groups=mesh['zh'=8,'zl'=2,'x'=4,'y'=4,'core'=2] {'zl','x','y','core'}, dimensions={0} | all-to-all | bytes 524288 | tf_op jit(solution)/shard_map/all_to_all | solution.py:399
  (53 shorter events, 10.0 us)
Async XLA Ops:
  0.0 18.6 %copy-start = (bf16[1,1,2,4,128,128]{5,4,3,2,1,0:T(8,128)(2,1)S(1)}, bf16[1,1,2,4,128,128]{5,4,3,2,1,0:T(8,128)(2,1)}, u32[]{:S(2)}) copy-start(bf16[1,1,2,4,128,128]{5,4,3,2,1,0:T(8,128)(2,1)} %param.16) | copy-start | bytes 786436
  1.6 17.0 %copy-start.1 = (bf16[1,1,3,1,128,128]{5,4,3,2,1,0:T(8,128)(2,1)S(1)}, bf16[1,1,3,1,128,128]{5,4,3,2,1,0:T(8,128)(2,1)}, u32[]{:S(2)}) copy-start(bf16[1,1,3,1,128,128]{5,4,3,2,1,0:T(8,128)(2,1)} %param.14) | copy-start | bytes 294916
  1.6 17.0 %copy-start.3 = (bf16[1,1,3,1,64,128]{5,4,3,2,1,0:T(8,128)(2,1)S(1)}, bf16[1,1,3,1,64,128]{5,4,3,2,1,0:T(8,128)(2,1)}, u32[]{:S(2)}) copy-start(bf16[1,1,3,1,64,128]{5,4,3,2,1,0:T(8,128)(2,1)} %param.13) | copy-start | bytes 147460
  1.6 33.1 %all-to-all-start = ((bf16[32,16,128]{2,1,0:T(8,128)(2,1)}), bf16[32,16,128]{2,1,0:T(8,128)(2,1)S(1)}, u32[]{:S(2)}, u32[]{:S(2)}) async-start(bf16[32,16,128]{2,1,0:T(8,128)(2,1)} %bitcast.73), calls=%async_computation | async-start | bytes 262144 | tf_op jit(solution)/shard_map/all_to_all | solution.py:306
  18.5 0.7 copy-start.5
  18.5 0.7 copy-start.9
  18.6 0.7 copy-start.10
  18.6 0.7 copy-start.8
  18.6 0.7 copy-start.12
  19.3 4.2 %copy-start.2 = (bf16[1,1,3,1,128,128]{5,4,3,2,1,0:T(8,128)(2,1)S(1)}, bf16[1,1,3,1,128,128]{5,4,3,2,1,0:T(8,128)(2,1)}, u32[]{:S(2)}) copy-start(bf16[1,1,3,1,128,128]{5,4,3,2,1,0:T(8,128)(2,1)} %param.15) | copy-start | bytes 294916
  19.3 4.2 %copy-start.4 = (bf16[1,1,2,4,128,128]{5,4,3,2,1,0:T(8,128)(2,1)S(1)}, bf16[1,1,2,4,128,128]{5,4,3,2,1,0:T(8,128)(2,1)}, u32[]{:S(2)}) copy-start(bf16[1,1,2,4,128,128]{5,4,3,2,1,0:T(8,128)(2,1)} %param.21) | copy-start | bytes 786436
  20.1 10.3 %collective-permute-start.1 = (bf16[736,128]{1,0:T(8,128)(2,1)S(1)}, bf16[736,128]{1,0:T(8,128)(2,1)S(1)}, u32[]{:S(2)}, u32[]{:S(2)}) collective-permute-start(bf16[736,128]{1,0:T(8,128)(2,1)S(1)} %shard_map.127.refs_0_.refs_4_), channel_id=1, source_target_pairs={{0,32},{32,0},{1,33},{33,1},{2,34},{34,2},{3,35},{35,3},{4,36},{36... | collective-permute-start | bytes 565256 | tf_op jit(solution)/shard_map/ppermute | solution.py:87
  24.4 22.7 %collective-permute-start.4 = (bf16[1984,128]{1,0:T(8,128)(2,1)S(1)}, bf16[1984,128]{1,0:T(8,128)(2,1)S(1)}, u32[]{:S(2)}, u32[]{:S(2)}) collective-permute-start(bf16[1984,128]{1,0:T(8,128)(2,1)S(1)} %shard_map.131.refs_0_.refs_4_.refs_8_), channel_id=1, source_target_pairs={{0,32},{32,0},{1,33},{33,1},{2,34},{34,2},{3,35},{35,3},{4,36},{36... | collective-permute-start | bytes 1523720 | tf_op jit(solution)/shard_map/ppermute | solution.py:87
  26.4 7.3 %collective-permute-start = (bf16[736,128]{1,0:T(8,128)(2,1)S(1)}, bf16[736,128]{1,0:T(8,128)(2,1)S(1)}, u32[]{:S(2)}, u32[]{:S(2)}) collective-permute-start(bf16[736,128]{1,0:T(8,128)(2,1)S(1)} %shard_map.127.refs_0_.refs_4_), channel_id=1, source_target_pairs={{0,1},{1,0},{2,3},{3,2},{4,5},{5,4},{6,7},{7,6},{8,9},{9,8},{10,11... | collective-permute-start | bytes 565256 | tf_op jit(solution)/shard_map/ppermute | solution.py:87
  30.4 4.3 %collective-permute-start.2 = (bf16[736,128]{1,0:T(8,128)(2,1)S(1)}, bf16[736,128]{1,0:T(8,128)(2,1)S(1)}, u32[]{:S(2)}, u32[]{:S(2)}) collective-permute-start(bf16[736,128]{1,0:T(8,128)(2,1)S(1)} %collective-permute-done.1.refs_2_.refs_6_), channel_id=1, source_target_pairs={{0,1},{1,0},{2,3},{3,2},{4,5},{5,4},{6,7},{7,6},{8,9},{9,8},{10,11... | collective-permute-start | bytes 565256 | tf_op jit(solution)/shard_map/ppermute | solution.py:87
  36.8 14.1 %all-to-all-start.1 = ((bf16[16,2,2,16,128]{4,3,2,1,0:T(8,128)(2,1)}), bf16[16,2,2,16,128]{4,3,2,1,0:T(8,128)(2,1)S(1)}, u32[]{:S(2)}, u32[]{:S(2)}) async-start(bf16[16,2,2,16,128]{4,3,2,1,0:T(8,128)(2,1)} %bitcast.14), calls=%async_computation.1 | async-start | bytes 524288 | tf_op jit(solution)/shard_map/all_to_all | solution.py:239
  43.5 19.4 %collective-permute-start.3 = (bf16[1984,128]{1,0:T(8,128)(2,1)S(1)}, bf16[1984,128]{1,0:T(8,128)(2,1)S(1)}, u32[]{:S(2)}, u32[]{:S(2)}) collective-permute-start(bf16[1984,128]{1,0:T(8,128)(2,1)S(1)} %shard_map.131.refs_0_.refs_4_.refs_8_), channel_id=1, source_target_pairs={{0,1},{1,0},{2,3},{3,2},{4,5},{5,4},{6,7},{7,6},{8,9},{9,8},{10,11... | collective-permute-start | bytes 1523720 | tf_op jit(solution)/shard_map/ppermute | solution.py:87
  47.1 15.7 %collective-permute-start.5 = (bf16[1984,128]{1,0:T(8,128)(2,1)S(1)}, bf16[1984,128]{1,0:T(8,128)(2,1)S(1)}, u32[]{:S(2)}, u32[]{:S(2)}) collective-permute-start(bf16[1984,128]{1,0:T(8,128)(2,1)S(1)} %collective-permute-done.4.refs_2_.refs_6_.refs_10_), channel_id=1, source_target_pairs={{0,1},{1,0},{2,3},{3,2},{4,5},{5,4},{6,7},{7,6},{8,9},{9,8},{10,11... | collective-permute-start | bytes 1523720 | tf_op jit(solution)/shard_map/ppermute | solution.py:87
  52.2 23.8 %all-to-all-start.2 = ((bf16[8,2,2,16,128]{4,3,2,1,0:T(8,128)(2,1)}), bf16[8,2,2,16,128]{4,3,2,1,0:T(8,128)(2,1)S(1)}, u32[]{:S(2)}, u32[]{:S(2)}) async-start(bf16[8,2,2,16,128]{4,3,2,1,0:T(8,128)(2,1)} %get-tuple-element.24), calls=%async_computation.2 | async-start | bytes 262144 | tf_op jit(solution)/shard_map/all_to_all | solution.py:243
  119.4 18.0 %all-to-all-start.6 = ((bf16[8,2,2,16,128]{4,3,2,1,0:T(8,128)(2,1)}), bf16[8,2,2,16,128]{4,3,2,1,0:T(8,128)(2,1)S(1)}, u32[]{:S(2)}, u32[]{:S(2)}) async-start(bf16[8,2,2,16,128]{4,3,2,1,0:T(8,128)(2,1)} %get-tuple-element.29), calls=%async_computation.6 | async-start | bytes 262144 | tf_op jit(solution)/shard_map/all_to_all | solution.py:243
  122.8 12.8 %collective-permute-start.8 = (bf16[2,16,128]{2,1,0:T(8,128)(2,1)S(1)}, bf16[2,16,128]{2,1,0:T(8,128)(2,1)S(1)}, u32[]{:S(2)}, u32[]{:S(2)}) collective-permute-start(bf16[2,16,128]{2,1,0:T(8,128)(2,1)S(1)} %get-tuple-element.39), channel_id=1, source_target_pairs={{0,33},{1,32},{32,1},{33,0},{2,35},{3,34},{34,3},{35,2},{4,37},{5,... | collective-permute-start | bytes 24584 | tf_op jit(solution)/shard_map/ppermute | solution.py:396
  130.6 5.1 %collective-permute-start.6 = (bf16[2,16,128]{2,1,0:T(8,128)(2,1)S(1)}, bf16[2,16,128]{2,1,0:T(8,128)(2,1)S(1)}, u32[]{:S(2)}, u32[]{:S(2)}) collective-permute-start(bf16[2,16,128]{2,1,0:T(8,128)(2,1)S(1)} %get-tuple-element.41), channel_id=1, source_target_pairs={{0,1},{1,0},{32,33},{33,32},{2,3},{3,2},{34,35},{35,34},{4,5},{5,4... | collective-permute-start | bytes 24584 | tf_op jit(solution)/shard_map/ppermute | solution.py:396
  132.5 4.9 %collective-permute-start.7 = (bf16[2,16,128]{2,1,0:T(8,128)(2,1)S(1)}, bf16[2,16,128]{2,1,0:T(8,128)(2,1)S(1)}, u32[]{:S(2)}, u32[]{:S(2)}) collective-permute-start(bf16[2,16,128]{2,1,0:T(8,128)(2,1)S(1)} %get-tuple-element.42), channel_id=1, source_target_pairs={{0,32},{1,33},{32,0},{33,1},{2,34},{3,35},{34,2},{35,3},{4,36},{5,... | collective-permute-start | bytes 24584 | tf_op jit(solution)/shard_map/ppermute | solution.py:396
  138.3 19.2 %copy-start.6 = (bf16[64,128]{1,0:T(8,128)(2,1)S(1)}, bf16[64,128]{1,0:T(8,128)(2,1)}, u32[]{:S(2)}) copy-start(bf16[64,128]{1,0:T(8,128)(2,1)} %get-tuple-element.34.forward) | copy-start | bytes 49156
  (3 other events, 2.0 us)

commit v6 on v4

--- a/solution.py
+++ b/solution.py
@@ -90,56 +90,36 @@
     return [(step // 2, step % 2) for step in range(SPLIT)]
 
 
-def spread_kernel(group, level, by_target, after, place, column, *refs):
-    tiles, indices, refs = refs[:SPLIT], refs[SPLIT : 2 * SPLIT], refs[2 * SPLIT :]
-    before = refs[0] if after else None
-    partial, terms = refs[-2:]
+def scatter_kernel(group, level, by_target, after, place, table, column, *refs):
+    tiles, before = refs[:SPLIT], refs[SPLIT] if after else None
+    partial, terms, sums = (refs[-2], None, refs[-1]) if after else refs[-3:]
     zl, core = place[0], place[1]
     extent = column.shape[3]
-    rows, blocks = column.shape[2], tiles[0].shape[0] // extent
-    goals = []
+    blocks = tiles[0].shape[0] // extent
+    targets = partial.shape[1] if by_target else partial.shape[0]
+    sums[...] = jnp.zeros(sums.shape, F32)
+
+    def add(step, entry, row, term):
+        goal = table[step, entry] - level * targets
+        slot = jnp.where((goal >= 0) & (goal < targets), goal, targets)
+        at = (pl.ds(row, 1), pl.ds(slot, 1)) if by_target else (pl.ds(slot, 1), pl.ds(row, 1))
+        sums[at] = sums[at] + term[None, None]
+
     for step, (dz, dc) in enumerate(offsets()):
-        index = indices[step][...].astype(F32)
-        half = lax.bitwise_xor(core, dc)
-        held = [column[j, pl.ds(half, 1)][0].astype(F32) for j in range(column.shape[0])]
-        first = 2 * blocks * group
-        goals.append([index[first + blocks + b : first + blocks + b + 1] for b in range(blocks)])
-        if after:
-            first = first - 2 * blocks
-            goals[-1] += [index[first + blocks + b : first + blocks + b + 1] for b in range(blocks)]
-        first = 2 * blocks * group
+        half, row = lax.bitwise_xor(core, dc), lax.bitwise_xor(zl, dz)
         for b in range(blocks):
-            source = index[first + b : first + b + 1]
-            picked = jnp.zeros((rows, extent), F32)
-            for j, tile in enumerate(held):
-                picked = jnp.where(source == float(j), tile, picked)
-            terms[step, b] = jnp.dot(
-                picked.astype(BF16),
+            source = jnp.clip(table[step, 2 * blocks * group + b], 0, column.shape[0] - 1)
+            term = jnp.dot(
+                column[pl.ds(source, 1), pl.ds(half, 1)][0, 0],
                 tiles[step][b * extent : (b + 1) * extent],
                 preferred_element_type=F32,
             )
-
-    targets = partial.shape[1] if by_target else partial.shape[0]
-
-    def one_target(t, carry):
-        slot = (t + level * targets).astype(F32)
-        for dz in range(2):
-            total = jnp.zeros((rows, extent), F32)
-            for dc in range(2):
-                step = 2 * dz + dc
-                for b in range(blocks):
-                    total = total + jnp.where(goals[step][b] == slot, terms[step, b], 0.0)
-                    if after:
-                        hit = goals[step][blocks + b] == slot
-                        total = total + jnp.where(hit, before[step, b], 0.0)
-            row = lax.bitwise_xor(zl, dz)
-            if by_target:
-                partial[pl.ds(row, 1), pl.ds(t, 1)] = total.astype(BF16)[None, None]
-            else:
-                partial[pl.ds(t, 1), pl.ds(row, 1)] = total.astype(BF16)[None, None]
-        return carry
-
-    lax.fori_loop(0, targets, one_target, 0, unroll=4)
+            if not after:
+                terms[step, b] = term
+            add(step, 2 * blocks * group + blocks + b, row, term)
+            if after:
+                add(step, 2 * blocks * (group - 1) + blocks + b, row, before[step, b])
+    partial[...] = (sums[:, :targets] if by_target else sums[:targets]).astype(BF16)
 
 
 def full_product(operand, inverse):
@@ -258,7 +238,7 @@
             pl.BlockSpec((side_extent, extent), lambda i: (0, 0)),
         ],
         scratch_shapes=[pltpu.VMEM((8 * blocks, extent), jnp.int32)],
-        compiler_params=pltpu.CompilerParams(vmem_limit_bytes=16 << 20),
+        compiler_params=pltpu.CompilerParams(vmem_limit_bytes=56 << 20),
     )(
         *(sides, sides, low_inv, low_inv, low_tiles, low_rows),
         *(low_source, low_target, low_count, up_source, up_target, up_count),
@@ -290,24 +270,25 @@
         start, size = sum(sizes[:number]), sizes[number]
         return pl.BlockSpec((size, extent), lambda i: (start // size, 0))
 
-    index_block = rows_of(first_sizes, 3)
+    table = jnp.stack([buffer[-8 * blocks :, 0] for buffer in first])
+    table = table.astype(F32).astype(jnp.int32)
 
     def edge(column, buffers, tile_block, group, level, before=None, by_target=False):
         shape = (row_group, pair) if not by_target else (pair, row_group)
         partial = jax.ShapeDtypeStruct(shape + (rows, extent), BF16)
         terms = jax.ShapeDtypeStruct((SPLIT, blocks, rows, extent), F32)
         extra = () if before is None else (before,)
+        extra_specs = [whole(array) for array in extra]
+        sums = (row_group + 1, pair) if not by_target else (pair, row_group + 1)
         return pl.pallas_call(
-            functools.partial(spread_kernel, group, level, by_target, before is not None),
+            functools.partial(scatter_kernel, group, level, by_target, before is not None),
             grid=(1,),
-            in_specs=[scalars(), whole(column)]
-            + [tile_block] * SPLIT
-            + [index_block] * SPLIT
-            + [whole(array) for array in extra],
-            out_shape=[partial, terms],
-            out_specs=[whole(partial), whole(terms)],
+            in_specs=[scalars(), scalars(), whole(column)] + [tile_block] * SPLIT + extra_specs,
+            out_shape=[partial, terms] if before is None else [partial],
+            out_specs=[whole(partial), whole(terms)] if before is None else [whole(partial)],
+            scratch_shapes=[pltpu.VMEM(sums + (rows, extent), F32)],
             compiler_params=pltpu.CompilerParams(vmem_limit_bytes=16 << 20),
-        )(place, column, *buffers, *first, *extra)
+        )(place, table, column, *buffers, *extra)
 
     def solve(kind, got, *pieces):
         solved = jax.ShapeDtypeStruct((SPLIT, rows, extent), BF16)
@@ -330,7 +311,7 @@
     inverse, side = rows_of(first_sizes, 1), rows_of(first_sizes, 2)
     forward_1, copies = solve(0, got, (first, inverse), (first, side))
     column = gather_column(copies)
-    partial, _ = edge(column, later, rows_of(later_sizes, 0), 1, 0, terms)
+    (partial,) = edge(column, later, rows_of(later_sizes, 0), 1, 0, terms)
     got = row_exchange(partial)
     inverse, upper, side = (rows_of(later_sizes, i) for i in (3, 4, 6))
     solution_0, copies = solve(1, got, (later, inverse), (later, side), (later, upper))
@@ -346,7 +327,7 @@
     for step in range(1, SPLIT):
         home.append(lax.ppermute(done[step], GROUP, [(i, i ^ step) for i in range(SPLIT)]))
     column, *home = lax.optimization_barrier((column, *home))
-    partial, _ = edge(column, later, rows_of(later_sizes, 2), 3, 1, terms, by_target=True)
+    (partial,) = edge(column, later, rows_of(later_sizes, 2), 3, 1, terms, by_target=True)
     got = lax.all_to_all(partial.reshape(-1, rows, extent), ("zl", "x", "y", "core"), 0, 0, tiled=True)
     got = got.reshape(pair, row_group // cores, cores, rows, extent)
     result = jax.ShapeDtypeStruct(sides.shape, BF16)

time: 165 us -> 159 us (0.964)
  blocking collectives: 56.9 us -> 60.6 us
  starting transfers between devices: 63.8 us -> 60.1 us
  Pallas kernels: 14.8 us -> 11.3 us
  local copies, waits for them, and re-layouts: 4.03 us -> 1.96 us
    pallas_call x4, Pallas kernels: 8.15 us -> 4.14 us  [edge(): pl.pallas_call(functools.partial(scatter_kernel, group, level, by_target,...]
    all_to_all x2, blocking collectives: 21.4 us -> 24.8 us  [row_exchange(): return lax.all_to_all(chunks, ('x', 'y'), 0, 0, tiled=True)]
    unnamed x32 -> x18, local copies, waits for them, and re-layouts: 4.03 us -> 1.62 us
    ppermute x3, starting transfers between devices: 14.2 us -> 12 us  [body(): lax.ppermute(done[step], GROUP, [(i, i ^ step) for i in range(SPLIT)])]
    ppermute x6, waiting for transfers between devices: 2.14 us -> 0.02 us  [swapped(): return lax.ppermute(value, axis, [(0, 1), (1, 0)])]
  transfers between devices with their start and end apart: 13 -> 13, of which waited for: 6 -> 4; matrix products, arithmetic and copies ran while one was open for 0% -> 0% of each run, Pallas kernels for 2% -> 2%
where the time goes in v6:
time: 159 us; the launch traced here: 158 us
  blocking collectives  60.6 us (38%)
  starting transfers between devices  60.1 us (38%)
  waiting for transfers between devices  23.1 us (15%)
  Pallas kernels  11.3 us (7%)
  local copies, waits for them, and re-layouts  1.96 us (1%)
    all_to_all x2, blocking collectives, row_exchange(): return lax.all_to_all(chunks, ('x', 'y'), 0, 0, tiled=True)  24.8 us
    all_to_all x1, blocking collectives, body(): lax.all_to_all(partial.reshape(-1, rows, extent), ('zl', 'x', 'y', 'core'...  19 us
    ppermute x6, starting transfers between devices, swapped(): return lax.ppermute(value, axis, [(0, 1), (1, 0)])  17.9 us
    all_to_all x1, blocking collectives, gather_column(): got = lax.all_to_all(copies, 'zh', 0, 0, tiled=True)  16.7 us
    all_to_all x1, starting transfers between devices, body(): column = lax.all_to_all(copies, ('zh', 'zl', 'core'), 0, 0, tiled=True)  15.4 us
    all_to_all x2, waiting for transfers between devices, gather_column(): got = lax.all_to_all(copies, 'zh', 0, 0, tiled=True)  13.8 us
    ppermute x3, starting transfers between devices, body(): lax.ppermute(done[step], GROUP, [(i, i ^ step) for i in range(SPLIT)])  12 us
    all_to_all x2, starting transfers between devices, gather_column(): got = lax.all_to_all(copies, 'zh', 0, 0, tiled=True)  8.01 us
  transfers between devices with their start and end apart: 13, of which 4 were waited for; matrix products, arithmetic and copies ran while one was open for 0% of the time, Pallas kernels for 2%

profile of v6, /device:TPU:1, one launch (start us, length us, event | category | flops | bytes accessed | tf_op | source)
XLA Modules:
  0.0 157.5 jit_solution(5505967135496332192)
XLA Ops:
  0.0 1.9 %shard_map.127 = (bf16[736,128]{1,0:T(8,128)(2,1)}, bf16[8,64,128]{2,1,0:T(8,128)(2,1)}, bf16[64,128]{1,0:T(8,128)(2,1)}) custom-call(bf16[3,64,128]{2,1,0:T(8,128)(2,1)} %bitcast.57, bf16[3,64,128]{2,1,0:T(8,128)(2,1)} %bitcast.58, bf16[3,128,128]{2,1,0:T(8,128)(2,1)} %bitcast.47, bf16[3,128,128]{2,1,0:T(8,128)(2,1)} %bitcast.48, ...), custom_call_target="tpu_custom_call" | custom-call | tf_op jit(solution)/shard_map/pallas_call | solution.py:224
  2.0 4.5 %collective-permute-start = (bf16[736,128]{1,0:T(8,128)(2,1)}, bf16[736,128]{1,0:T(8,128)(2,1)S(1)}, u32[]{:S(2)}, u32[]{:S(2)}) collective-permute-start(bf16[736,128]{1,0:T(8,128)(2,1)} %get-tuple-element.26.refs_0_.refs_4_), channel_id=1, source_target_pairs={{0,32},{32,0},{1,33},{33,1},{2,34},{34,2},{3,35},{35,3},{4,36},{36... | collective-permute-start | bytes 565256 | tf_op jit(solution)/shard_map/ppermute | solution.py:86
  6.5 15.4 %all-to-all-start = ((bf16[32,16,128]{2,1,0:T(8,128)(2,1)}), bf16[32,16,128]{2,1,0:T(8,128)(2,1)S(1)}, u32[]{:S(2)}, u32[]{:S(2)}) async-start(bf16[32,16,128]{2,1,0:T(8,128)(2,1)} %bitcast.67), calls=%async_computation | async-start | bytes 262144 | tf_op jit(solution)/shard_map/all_to_all | solution.py:248
  21.9 2.1 %collective-permute-start.2 = (bf16[736,128]{1,0:T(8,128)(2,1)S(1)}, bf16[736,128]{1,0:T(8,128)(2,1)S(1)}, u32[]{:S(2)}, u32[]{:S(2)}) collective-permute-start(bf16[736,128]{1,0:T(8,128)(2,1)S(1)} %collective-permute-done.refs_2_.refs_6_), channel_id=1, source_target_pairs={{0,1},{1,0},{2,3},{3,2},{4,5},{5,4},{6,7},{7,6},{8,9},{9,8},{10,11... | collective-permute-start | bytes 565256 | tf_op jit(solution)/shard_map/ppermute | solution.py:86
  24.2 2.2 %collective-permute-start.1 = (bf16[736,128]{1,0:T(8,128)(2,1)S(1)}, bf16[736,128]{1,0:T(8,128)(2,1)S(1)}, u32[]{:S(2)}, u32[]{:S(2)}) collective-permute-start(bf16[736,128]{1,0:T(8,128)(2,1)S(1)} %copy-done), channel_id=1, source_target_pairs={{0,1},{1,0},{2,3},{3,2},{4,5},{5,4},{6,7},{7,6},{8,9},{9,8},{10,11... | collective-permute-start | bytes 565256 | tf_op jit(solution)/shard_map/ppermute | solution.py:86
  28.4 3.3 %collective-permute-start.4 = (bf16[1984,128]{1,0:T(8,128)(2,1)S(1)}, bf16[1984,128]{1,0:T(8,128)(2,1)S(1)}, u32[]{:S(2)}, u32[]{:S(2)}) collective-permute-start(bf16[1984,128]{1,0:T(8,128)(2,1)S(1)} %shard_map.130.refs_0_.refs_4_.refs_8_), channel_id=1, source_target_pairs={{0,32},{32,0},{1,33},{33,1},{2,34},{34,2},{3,35},{35,3},{4,36},{36... | collective-permute-start | bytes 1523720 | tf_op jit(solution)/shard_map/ppermute | solution.py:86
  32.0 5.8 %all-to-all-done = bf16[32,16,128]{2,1,0:T(8,128)(2,1)S(1)} async-done(((bf16[32,16,128]{2,1,0:T(8,128)(2,1)}), bf16[32,16,128]{2,1,0:T(8,128)(2,1)S(1)}, u32[]{:S(2)}, u32[]{:S(2)}) %all-to-all-start) | async-done | bytes 131104 | tf_op jit(solution)/shard_map/all_to_all | solution.py:248
  37.8 1.6 shard_map.128
  39.3 6.7 %all-to-all-start.1 = ((bf16[16,2,2,16,128]{4,3,2,1,0:T(8,128)(2,1)}), bf16[16,2,2,16,128]{4,3,2,1,0:T(8,128)(2,1)S(1)}, u32[]{:S(2)}, u32[]{:S(2)}) async-start(bf16[16,2,2,16,128]{4,3,2,1,0:T(8,128)(2,1)} %bitcast.14), calls=%async_computation.1 | async-start | bytes 524288 | tf_op jit(solution)/shard_map/all_to_all | solution.py:186
  46.1 3.9 %collective-permute-start.3 = (bf16[1984,128]{1,0:T(8,128)(2,1)S(1)}, bf16[1984,128]{1,0:T(8,128)(2,1)S(1)}, u32[]{:S(2)}, u32[]{:S(2)}) collective-permute-start(bf16[1984,128]{1,0:T(8,128)(2,1)S(1)} %shard_map.130.refs_0_.refs_4_.refs_8_), channel_id=1, source_target_pairs={{0,1},{1,0},{2,3},{3,2},{4,5},{5,4},{6,7},{7,6},{8,9},{9,8},{10,11... | collective-permute-start | bytes 1523720 | tf_op jit(solution)/shard_map/ppermute | solution.py:86
  50.0 1.9 %collective-permute-start.5 = (bf16[1984,128]{1,0:T(8,128)(2,1)S(1)}, bf16[1984,128]{1,0:T(8,128)(2,1)S(1)}, u32[]{:S(2)}, u32[]{:S(2)}) collective-permute-start(bf16[1984,128]{1,0:T(8,128)(2,1)S(1)} %collective-permute-done.4.refs_2_.refs_6_.refs_10_), channel_id=1, source_target_pairs={{0,1},{1,0},{2,3},{3,2},{4,5},{5,4},{6,7},{7,6},{8,9},{9,8},{10,11... | collective-permute-start | bytes 1523720 | tf_op jit(solution)/shard_map/ppermute | solution.py:86
  51.9 1.5 all-to-all-done.1.got
  53.4 1.4 shard_map.129
  54.8 4.6 %all-to-all-start.2 = ((bf16[8,2,2,16,128]{4,3,2,1,0:T(8,128)(2,1)}), bf16[8,2,2,16,128]{4,3,2,1,0:T(8,128)(2,1)S(1)}, u32[]{:S(2)}, u32[]{:S(2)}) async-start(bf16[8,2,2,16,128]{4,3,2,1,0:T(8,128)(2,1)} %get-tuple-element.30), calls=%async_computation.2 | async-start | bytes 262144 | tf_op jit(solution)/shard_map/all_to_all | solution.py:190
  59.5 13.8 %all-to-all-done.2 = bf16[8,2,2,16,128]{4,3,2,1,0:T(8,128)(2,1)S(1)} async-done(((bf16[8,2,2,16,128]{4,3,2,1,0:T(8,128)(2,1)}), bf16[8,2,2,16,128]{4,3,2,1,0:T(8,128)(2,1)S(1)}, u32[]{:S(2)}, u32[]{:S(2)}) %all-to-all-start.2) | async-done | bytes 131104 | tf_op jit(solution)/shard_map/all_to_all | solution.py:190
  74.1 14.2 %all_to_all.40.got = bf16[16,2,2,16,128]{4,3,2,1,0:T(8,128)(2,1)S(1)} all-to-all(bf16[16,2,2,16,128]{4,3,2,1,0:T(8,128)(2,1)S(1)} %bitcast.43), channel_id=1, replica_groups=mesh['zh'=8,'zl'=2,'x'=4,'y'=4,'core'=2] {'x','y'}, dimensions={0} | all-to-all | bytes 524288 | tf_op jit(solution)/shard_map/all_to_all | solution.py:186
  89.2 16.7 %all_to_all.41 = bf16[8,2,2,16,128]{4,3,2,1,0:T(8,128)(2,1)S(1)} all-to-all(bf16[8,2,2,16,128]{4,3,2,1,0:T(8,128)(2,1)S(1)} %get-tuple-element.32), channel_id=1, replica_groups=mesh['zh'=8,'zl'=2,'x'=4,'y'=4,'core'=2] {'zh'}, dimensions={0} | all-to-all | bytes 262144 | tf_op jit(solution)/shard_map/all_to_all | solution.py:190
  106.8 10.6 %all_to_all.42.got = bf16[16,2,2,16,128]{4,3,2,1,0:T(8,128)(2,1)S(1)} all-to-all(bf16[16,2,2,16,128]{4,3,2,1,0:T(8,128)(2,1)S(1)} %bitcast.60), channel_id=1, replica_groups=mesh['zh'=8,'zl'=2,'x'=4,'y'=4,'core'=2] {'x','y'}, dimensions={0} | all-to-all | bytes 524288 | tf_op jit(solution)/shard_map/all_to_all | solution.py:186
  118.8 3.4 %all-to-all-start.6 = ((bf16[8,2,2,16,128]{4,3,2,1,0:T(8,128)(2,1)}), bf16[8,2,2,16,128]{4,3,2,1,0:T(8,128)(2,1)S(1)}, u32[]{:S(2)}, u32[]{:S(2)}) async-start(bf16[8,2,2,16,128]{4,3,2,1,0:T(8,128)(2,1)} %get-tuple-element.35), calls=%async_computation.6 | async-start | bytes 262144 | tf_op jit(solution)/shard_map/all_to_all | solution.py:190
  122.2 7.2 %collective-permute-start.8 = (bf16[2,16,128]{2,1,0:T(8,128)(2,1)S(1)}, bf16[2,16,128]{2,1,0:T(8,128)(2,1)S(1)}, u32[]{:S(2)}, u32[]{:S(2)}) collective-permute-start(bf16[2,16,128]{2,1,0:T(8,128)(2,1)S(1)} %get-tuple-element.45), channel_id=1, source_target_pairs={{0,33},{1,32},{32,1},{33,0},{2,35},{3,34},{34,3},{35,2},{4,37},{5,... | collective-permute-start | bytes 24584 | tf_op jit(solution)/shard_map/ppermute | solution.py:328
  129.4 1.9 %collective-permute-start.6 = (bf16[2,16,128]{2,1,0:T(8,128)(2,1)S(1)}, bf16[2,16,128]{2,1,0:T(8,128)(2,1)S(1)}, u32[]{:S(2)}, u32[]{:S(2)}) collective-permute-start(bf16[2,16,128]{2,1,0:T(8,128)(2,1)S(1)} %get-tuple-element.47), channel_id=1, source_target_pairs={{0,1},{1,0},{32,33},{33,32},{2,3},{3,2},{34,35},{35,34},{4,5},{5,4... | collective-permute-start | bytes 24584 | tf_op jit(solution)/shard_map/ppermute | solution.py:328
  131.4 2.9 %collective-permute-start.7 = (bf16[2,16,128]{2,1,0:T(8,128)(2,1)S(1)}, bf16[2,16,128]{2,1,0:T(8,128)(2,1)S(1)}, u32[]{:S(2)}, u32[]{:S(2)}) collective-permute-start(bf16[2,16,128]{2,1,0:T(8,128)(2,1)S(1)} %get-tuple-element.48), channel_id=1, source_target_pairs={{0,32},{1,33},{32,0},{33,1},{2,34},{3,35},{34,2},{35,3},{4,36},{5,... | collective-permute-start | bytes 24584 | tf_op jit(solution)/shard_map/ppermute | solution.py:328
  134.3 2.0 %collective-permute-done.7.home_2 = bf16[2,16,128]{2,1,0:T(8,128)(2,1)S(1)} collective-permute-done((bf16[2,16,128]{2,1,0:T(8,128)(2,1)S(1)}, bf16[2,16,128]{2,1,0:T(8,128)(2,1)S(1)}, u32[]{:S(2)}, u32[]{:S(2)}) %collective-permute-start.7) | collective-permute-done | bytes 8224 | tf_op jit(solution)/shard_map/ppermute | solution.py:328
  137.1 19.0 %all_to_all.43 = bf16[64,16,128]{2,1,0:T(8,128)(2,1)S(1)} all-to-all(bf16[64,16,128]{2,1,0:T(8,128)(2,1)S(1)} %bitcast.42), channel_id=1, replica_groups=mesh['zh'=8,'zl'=2,'x'=4,'y'=4,'core'=2] {'zl','x','y','core'}, dimensions={0} | all-to-all | bytes 524288 | tf_op jit(solution)/shard_map/all_to_all | solution.py:331
  (41 shorter events, 8.5 us)
Async XLA Ops:
  0.0 26.5 %copy-start.1 = (bf16[1,1,2,4,128,128]{5,4,3,2,1,0:T(8,128)(2,1)S(1)}, bf16[1,1,2,4,128,128]{5,4,3,2,1,0:T(8,128)(2,1)}, u32[]{:S(2)}) copy-start(bf16[1,1,2,4,128,128]{5,4,3,2,1,0:T(8,128)(2,1)} %param.16) | copy-start | bytes 786436
  0.0 26.5 %copy-start.3 = (bf16[1,1,3,1,128,128]{5,4,3,2,1,0:T(8,128)(2,1)S(1)}, bf16[1,1,3,1,128,128]{5,4,3,2,1,0:T(8,128)(2,1)}, u32[]{:S(2)}) copy-start(bf16[1,1,3,1,128,128]{5,4,3,2,1,0:T(8,128)(2,1)} %param.15) | copy-start | bytes 294916
  0.0 26.5 %copy-start.4 = (bf16[1,1,3,1,64,128]{5,4,3,2,1,0:T(8,128)(2,1)S(1)}, bf16[1,1,3,1,64,128]{5,4,3,2,1,0:T(8,128)(2,1)}, u32[]{:S(2)}) copy-start(bf16[1,1,3,1,64,128]{5,4,3,2,1,0:T(8,128)(2,1)} %param.13) | copy-start | bytes 147460
  2.0 22.2 %copy-start = (bf16[736,128]{1,0:T(8,128)(2,1)S(1)}, bf16[736,128]{1,0:T(8,128)(2,1)}, u32[]{:S(2)}) copy-start(bf16[736,128]{1,0:T(8,128)(2,1)} %get-tuple-element.26.refs_0_.refs_4_) | copy-start | bytes 565252
  2.0 20.0 %collective-permute-start = (bf16[736,128]{1,0:T(8,128)(2,1)}, bf16[736,128]{1,0:T(8,128)(2,1)S(1)}, u32[]{:S(2)}, u32[]{:S(2)}) collective-permute-start(bf16[736,128]{1,0:T(8,128)(2,1)} %get-tuple-element.26.refs_0_.refs_4_), channel_id=1, source_target_pairs={{0,32},{32,0},{1,33},{33,1},{2,34},{34,2},{3,35},{35,3},{4,36},{36... | collective-permute-start | bytes 565256 | tf_op jit(solution)/shard_map/ppermute | solution.py:86
  6.5 20.1 %copy-start.2 = (bf16[1,1,3,1,128,128]{5,4,3,2,1,0:T(8,128)(2,1)S(1)}, bf16[1,1,3,1,128,128]{5,4,3,2,1,0:T(8,128)(2,1)}, u32[]{:S(2)}) copy-start(bf16[1,1,3,1,128,128]{5,4,3,2,1,0:T(8,128)(2,1)} %param.14) | copy-start | bytes 294916
  6.5 31.3 %all-to-all-start = ((bf16[32,16,128]{2,1,0:T(8,128)(2,1)}), bf16[32,16,128]{2,1,0:T(8,128)(2,1)S(1)}, u32[]{:S(2)}, u32[]{:S(2)}) async-start(bf16[32,16,128]{2,1,0:T(8,128)(2,1)} %bitcast.67), calls=%async_computation | async-start | bytes 262144 | tf_op jit(solution)/shard_map/all_to_all | solution.py:248
  21.9 4.5 %collective-permute-start.2 = (bf16[736,128]{1,0:T(8,128)(2,1)S(1)}, bf16[736,128]{1,0:T(8,128)(2,1)S(1)}, u32[]{:S(2)}, u32[]{:S(2)}) collective-permute-start(bf16[736,128]{1,0:T(8,128)(2,1)S(1)} %collective-permute-done.refs_2_.refs_6_), channel_id=1, source_target_pairs={{0,1},{1,0},{2,3},{3,2},{4,5},{5,4},{6,7},{7,6},{8,9},{9,8},{10,11... | collective-permute-start | bytes 565256 | tf_op jit(solution)/shard_map/ppermute | solution.py:86
  24.2 7.7 %collective-permute-start.1 = (bf16[736,128]{1,0:T(8,128)(2,1)S(1)}, bf16[736,128]{1,0:T(8,128)(2,1)S(1)}, u32[]{:S(2)}, u32[]{:S(2)}) collective-permute-start(bf16[736,128]{1,0:T(8,128)(2,1)S(1)} %copy-done), channel_id=1, source_target_pairs={{0,1},{1,0},{2,3},{3,2},{4,5},{5,4},{6,7},{7,6},{8,9},{9,8},{10,11... | collective-permute-start | bytes 565256 | tf_op jit(solution)/shard_map/ppermute | solution.py:86
  26.5 0.7 copy-start.8
  26.5 0.7 copy-start.6
  27.2 0.9 copy-start.5
  28.4 21.6 %collective-permute-start.4 = (bf16[1984,128]{1,0:T(8,128)(2,1)S(1)}, bf16[1984,128]{1,0:T(8,128)(2,1)S(1)}, u32[]{:S(2)}, u32[]{:S(2)}) collective-permute-start(bf16[1984,128]{1,0:T(8,128)(2,1)S(1)} %shard_map.130.refs_0_.refs_4_.refs_8_), channel_id=1, source_target_pairs={{0,32},{32,0},{1,33},{33,1},{2,34},{34,2},{3,35},{35,3},{4,36},{36... | collective-permute-start | bytes 1523720 | tf_op jit(solution)/shard_map/ppermute | solution.py:86
  39.3 14.1 %all-to-all-start.1 = ((bf16[16,2,2,16,128]{4,3,2,1,0:T(8,128)(2,1)}), bf16[16,2,2,16,128]{4,3,2,1,0:T(8,128)(2,1)S(1)}, u32[]{:S(2)}, u32[]{:S(2)}) async-start(bf16[16,2,2,16,128]{4,3,2,1,0:T(8,128)(2,1)} %bitcast.14), calls=%async_computation.1 | async-start | bytes 524288 | tf_op jit(solution)/shard_map/all_to_all | solution.py:186
  46.1 13.4 %collective-permute-start.3 = (bf16[1984,128]{1,0:T(8,128)(2,1)S(1)}, bf16[1984,128]{1,0:T(8,128)(2,1)S(1)}, u32[]{:S(2)}, u32[]{:S(2)}) collective-permute-start(bf16[1984,128]{1,0:T(8,128)(2,1)S(1)} %shard_map.130.refs_0_.refs_4_.refs_8_), channel_id=1, source_target_pairs={{0,1},{1,0},{2,3},{3,2},{4,5},{5,4},{6,7},{7,6},{8,9},{9,8},{10,11... | collective-permute-start | bytes 1523720 | tf_op jit(solution)/shard_map/ppermute | solution.py:86
  50.0 23.3 %collective-permute-start.5 = (bf16[1984,128]{1,0:T(8,128)(2,1)S(1)}, bf16[1984,128]{1,0:T(8,128)(2,1)S(1)}, u32[]{:S(2)}, u32[]{:S(2)}) collective-permute-start(bf16[1984,128]{1,0:T(8,128)(2,1)S(1)} %collective-permute-done.4.refs_2_.refs_6_.refs_10_), channel_id=1, source_target_pairs={{0,1},{1,0},{2,3},{3,2},{4,5},{5,4},{6,7},{7,6},{8,9},{9,8},{10,11... | collective-permute-start | bytes 1523720 | tf_op jit(solution)/shard_map/ppermute | solution.py:86
  54.8 18.4 %all-to-all-start.2 = ((bf16[8,2,2,16,128]{4,3,2,1,0:T(8,128)(2,1)}), bf16[8,2,2,16,128]{4,3,2,1,0:T(8,128)(2,1)S(1)}, u32[]{:S(2)}, u32[]{:S(2)}) async-start(bf16[8,2,2,16,128]{4,3,2,1,0:T(8,128)(2,1)} %get-tuple-element.30), calls=%async_computation.2 | async-start | bytes 262144 | tf_op jit(solution)/shard_map/all_to_all | solution.py:190
  118.8 17.4 %all-to-all-start.6 = ((bf16[8,2,2,16,128]{4,3,2,1,0:T(8,128)(2,1)}), bf16[8,2,2,16,128]{4,3,2,1,0:T(8,128)(2,1)S(1)}, u32[]{:S(2)}, u32[]{:S(2)}) async-start(bf16[8,2,2,16,128]{4,3,2,1,0:T(8,128)(2,1)} %get-tuple-element.35), calls=%async_computation.6 | async-start | bytes 262144 | tf_op jit(solution)/shard_map/all_to_all | solution.py:190
  122.2 12.0 %collective-permute-start.8 = (bf16[2,16,128]{2,1,0:T(8,128)(2,1)S(1)}, bf16[2,16,128]{2,1,0:T(8,128)(2,1)S(1)}, u32[]{:S(2)}, u32[]{:S(2)}) collective-permute-start(bf16[2,16,128]{2,1,0:T(8,128)(2,1)S(1)} %get-tuple-element.45), channel_id=1, source_target_pairs={{0,33},{1,32},{32,1},{33,0},{2,35},{3,34},{34,3},{35,2},{4,37},{5,... | collective-permute-start | bytes 24584 | tf_op jit(solution)/shard_map/ppermute | solution.py:328
  129.4 4.8 %collective-permute-start.6 = (bf16[2,16,128]{2,1,0:T(8,128)(2,1)S(1)}, bf16[2,16,128]{2,1,0:T(8,128)(2,1)S(1)}, u32[]{:S(2)}, u32[]{:S(2)}) collective-permute-start(bf16[2,16,128]{2,1,0:T(8,128)(2,1)S(1)} %get-tuple-element.47), channel_id=1, source_target_pairs={{0,1},{1,0},{32,33},{33,32},{2,3},{3,2},{34,35},{35,34},{4,5},{5,4... | collective-permute-start | bytes 24584 | tf_op jit(solution)/shard_map/ppermute | solution.py:328
  131.4 4.9 %collective-permute-start.7 = (bf16[2,16,128]{2,1,0:T(8,128)(2,1)S(1)}, bf16[2,16,128]{2,1,0:T(8,128)(2,1)S(1)}, u32[]{:S(2)}, u32[]{:S(2)}) collective-permute-start(bf16[2,16,128]{2,1,0:T(8,128)(2,1)S(1)} %get-tuple-element.48), channel_id=1, source_target_pairs={{0,32},{1,33},{32,0},{33,1},{2,34},{3,35},{34,2},{35,3},{4,36},{5,... | collective-permute-start | bytes 24584 | tf_op jit(solution)/shard_map/ppermute | solution.py:328
  137.1 19.1 %copy-start.7 = (bf16[64,128]{1,0:T(8,128)(2,1)S(1)}, bf16[64,128]{1,0:T(8,128)(2,1)}, u32[]{:S(2)}) copy-start(bf16[64,128]{1,0:T(8,128)(2,1)} %get-tuple-element.40.forward) | copy-start | bytes 49156

commit v7 on v6

--- a/solution.py
+++ b/solution.py
@@ -105,21 +105,37 @@
         at = (pl.ds(row, 1), pl.ds(slot, 1)) if by_target else (pl.ds(slot, 1), pl.ds(row, 1))
         sums[at] = sums[at] + term[None, None]
 
+    products = []
     for step, (dz, dc) in enumerate(offsets()):
-        half, row = lax.bitwise_xor(core, dc), lax.bitwise_xor(zl, dz)
+        half = lax.bitwise_xor(core, dc)
         for b in range(blocks):
             source = jnp.clip(table[step, 2 * blocks * group + b], 0, column.shape[0] - 1)
-            term = jnp.dot(
-                column[pl.ds(source, 1), pl.ds(half, 1)][0, 0],
-                tiles[step][b * extent : (b + 1) * extent],
-                preferred_element_type=F32,
+            products.append(
+                jnp.dot(
+                    column[pl.ds(source, 1), pl.ds(half, 1)][0, 0],
+                    tiles[step][b * extent : (b + 1) * extent],
+                    preferred_element_type=F32,
+                )
             )
-            if not after:
-                terms[step, b] = term
-            add(step, 2 * blocks * group + blocks + b, row, term)
+    for step, (dz, dc) in enumerate(offsets()):
+        row = lax.bitwise_xor(zl, dz)
+        for b in range(blocks):
             if after:
                 add(step, 2 * blocks * (group - 1) + blocks + b, row, before[step, b])
+            else:
+                terms[step, b] = products[step * blocks + b]
+    for step, (dz, dc) in enumerate(offsets()):
+        row = lax.bitwise_xor(zl, dz)
+        for b in range(blocks):
+            add(step, 2 * blocks * group + blocks + b, row, products[step * blocks + b])
     partial[...] = (sums[:, :targets] if by_target else sums[:targets]).astype(BF16)
+
+
+def tree_sum(values):
+    while len(values) > 1:
+        pairs = [values[i] + values[i + 1] for i in range(0, len(values) - 1, 2)]
+        values = pairs + values[len(values) - len(values) % 2 :]
+    return values[0]
 
 
 def full_product(operand, inverse):
@@ -133,9 +149,9 @@
     return product[:rows] + (product[rows : 2 * rows] + product[2 * rows :])
 
 
-def solve_kernel(kind, place, got, *refs):
+def solve_kernel(kind, got, *refs):
     inverses, refs = refs[:SPLIT], refs[SPLIT:]
-    zl, core = place[0], place[1]
+    zl, core = lax.axis_index("zl"), lax.axis_index("core")
     rows = got.shape[3]
     me = 2 * zl + core
     if kind == 2:
@@ -144,40 +160,43 @@
         sides, uppers, (solved, copies) = refs[:SPLIT], refs[SPLIT : 2 * SPLIT], refs[2 * SPLIT :]
     else:
         sides, (solved, copies) = refs[:SPLIT], refs[SPLIT:]
-    for step, (dz, dc) in enumerate(offsets()):
-        row, col = lax.bitwise_xor(zl, dz), lax.bitwise_xor(core, dc)
-        total = jnp.zeros(got.shape[3:], F32)
-        for i in range(got.shape[0]):
-            total = total + got[i, pl.ds(col, 1), pl.ds(row, 1)][0, 0].astype(F32)
+    places = [(lax.bitwise_xor(zl, dz), lax.bitwise_xor(core, dc)) for dz, dc in offsets()]
+    operands = []
+    for step, (row, col) in enumerate(places):
+        pieces = [got[i, pl.ds(col, 1), pl.ds(row, 1)][0, 0].astype(F32) for i in range(got.shape[0])]
         if kind == 2:
-            operand = held[step].astype(F32) - total
+            mine = held[step]
         else:
             mine = sides[step][pl.ds(pl.multiple_of(me * rows, rows), rows)]
-            operand = mine.astype(F32) - total
-        result = full_product(operand, inverses[step][...]).astype(BF16)
-        if kind == 1:
-            result = jnp.dot(result, uppers[step][...], preferred_element_type=F32).astype(BF16)
-        solved[step] = result
+        operands.append(mine.astype(F32) - tree_sum(pieces))
+    results = [full_product(operands[step], inverses[step][...]) for step in range(SPLIT)]
+    results = [result.astype(BF16) for result in results]
+    if kind == 1:
+        results = [
+            jnp.dot(results[step], uppers[step][...], preferred_element_type=F32).astype(BF16)
+            for step in range(SPLIT)
+        ]
+    for step, (row, col) in enumerate(places):
+        solved[step] = results[step]
         for i in range(copies.shape[0]):
-            copies[i, pl.ds(row, 1), pl.ds(col, 1)] = result[None, None]
-
-
-def last_kernel(place, got, forward, inverse, home_0, home_1, home_2, home_3, out):
-    zl, core = place[0], place[1]
+            copies[i, pl.ds(row, 1), pl.ds(col, 1)] = results[step][None, None]
+
+
+def last_kernel(got, forward, inverse, home_0, home_1, home_2, home_3, out):
+    zl, core = lax.axis_index("zl"), lax.axis_index("core")
     rows = got.shape[3]
     me = 2 * zl + core
     for step, home in enumerate((home_0, home_1, home_2, home_3)):
         at = pl.multiple_of(lax.bitwise_xor(me, step) * rows, rows)
         for level in range(2):
             out[level, pl.ds(at, rows)] = home[level]
-    for pair in range(got.shape[0]):
-        for core_at in range(got.shape[2]):
-            total = jnp.zeros(got.shape[3:], F32)
-            for i in range(got.shape[1]):
-                total = total + got[pair, i, core_at].astype(F32)
-            at = (2 * pair + core_at) * rows
-            operand = forward[at : at + rows].astype(F32) - total
-            out[2, at : at + rows] = full_product(operand, inverse[0]).astype(BF16)
+    totals = [
+        tree_sum([got[pair, i, col].astype(F32) for i in range(got.shape[1])])
+        for pair in range(got.shape[0])
+        for col in range(got.shape[2])
+    ]
+    operand = forward[...].astype(F32) - jnp.concatenate(totals, axis=0)
+    out[2] = full_product(operand, inverse[0]).astype(BF16)
 
 
 def row_exchange(partial):
@@ -264,11 +283,11 @@
     z_mate = swapped(packed, "zl")
     later = (packed, swapped(packed, "core"), z_mate, swapped(z_mate, "core"))
 
-    place = jnp.stack([lax.axis_index("zl"), lax.axis_index("core")]).astype(jnp.int32)
-
     def rows_of(sizes, number):
         start, size = sum(sizes[:number]), sizes[number]
         return pl.BlockSpec((size, extent), lambda i: (start // size, 0))
+
+    place = jnp.stack([lax.axis_index("zl"), lax.axis_index("core")]).astype(jnp.int32)
 
     table = jnp.stack([buffer[-8 * blocks :, 0] for buffer in first])
     table = table.astype(F32).astype(jnp.int32)
@@ -300,11 +319,11 @@
         return pl.pallas_call(
             functools.partial(solve_kernel, kind),
             grid=(1,),
-            in_specs=[scalars(), whole(got)] + specs,
+            in_specs=[whole(got)] + specs,
             out_shape=[solved, copies],
             out_specs=[whole(solved), whole(copies)],
             compiler_params=pltpu.CompilerParams(vmem_limit_bytes=16 << 20),
-        )(place, got, *arrays)
+        )(got, *arrays)
 
     partial, terms = edge(column, first, rows_of(first_sizes, 0), 0, 1)
     got = row_exchange(partial)
@@ -334,12 +353,12 @@
     result = pl.pallas_call(
         last_kernel,
         grid=(1,),
-        in_specs=[scalars(), whole(got), whole(forward_2), one_of(up_inv, 2)]
+        in_specs=[whole(got), whole(forward_2), one_of(up_inv, 2)]
         + [whole(piece) for piece in home],
         out_shape=result,
         out_specs=whole(result),
         compiler_params=pltpu.CompilerParams(vmem_limit_bytes=16 << 20),
-    )(place, got, forward_2, up_inv, *home)
+    )(got, forward_2, up_inv, *home)
     return result[None, None, :, None]
 
 

time: 159 us -> 156 us (0.981)
  Pallas kernels: 11.3 us -> 9.12 us
    pallas_call x3, Pallas kernels: 3.62 us -> 1.99 us  [solve(): pl.pallas_call(functools.partial(solve_kernel, kind), grid=(1,), in_specs...]
where the time goes in v7:
time: 156 us; the launch traced here: 155 us
  blocking collectives  60.7 us (39%)
  starting transfers between devices  60.2 us (39%)
  waiting for transfers between devices  22.5 us (14%)
  Pallas kernels  9.12 us (6%)
  local copies, waits for them, and re-layouts  1.96 us (1%)
    all_to_all x2, blocking collectives, row_exchange(): return lax.all_to_all(chunks, ('x', 'y'), 0, 0, tiled=True)  25 us
    all_to_all x1, blocking collectives, body(): lax.all_to_all(partial.reshape(-1, rows, extent), ('zl', 'x', 'y', 'core'...  19.1 us
    ppermute x6, starting transfers between devices, swapped(): return lax.ppermute(value, axis, [(0, 1), (1, 0)])  17.9 us
    all_to_all x1, blocking collectives, gather_column(): got = lax.all_to_all(copies, 'zh', 0, 0, tiled=True)  16.6 us
    all_to_all x1, starting transfers between devices, body(): column = lax.all_to_all(copies, ('zh', 'zl', 'core'), 0, 0, tiled=True)  15.4 us
    all_to_all x2, waiting for transfers between devices, gather_column(): got = lax.all_to_all(copies, 'zh', 0, 0, tiled=True)  13.8 us
    ppermute x3, starting transfers between devices, body(): lax.ppermute(done[step], GROUP, [(i, i ^ step) for i in range(SPLIT)])  12 us
    all_to_all x2, starting transfers between devices, gather_column(): got = lax.all_to_all(copies, 'zh', 0, 0, tiled=True)  8 us
  transfers between devices with their start and end apart: 13, of which 4 were waited for; matrix products, arithmetic and copies ran while one was open for 0% of the time, Pallas kernels for 2%

profile of v7, /device:TPU:1, one launch (start us, length us, event | category | flops | bytes accessed | tf_op | source)
XLA Modules:
  0.0 154.9 jit_solution(428279103130843121)
XLA Ops:
  0.0 1.9 %shard_map.127 = (bf16[736,128]{1,0:T(8,128)(2,1)}, bf16[8,64,128]{2,1,0:T(8,128)(2,1)}, bf16[64,128]{1,0:T(8,128)(2,1)}) custom-call(bf16[3,64,128]{2,1,0:T(8,128)(2,1)} %bitcast.57, bf16[3,64,128]{2,1,0:T(8,128)(2,1)} %bitcast.58, bf16[3,128,128]{2,1,0:T(8,128)(2,1)} %bitcast.47, bf16[3,128,128]{2,1,0:T(8,128)(2,1)} %bitcast.48, ...), custom_call_target="tpu_custom_call" | custom-call | tf_op jit(solution)/shard_map/pallas_call | solution.py:243
  2.0 4.5 %collective-permute-start = (bf16[736,128]{1,0:T(8,128)(2,1)}, bf16[736,128]{1,0:T(8,128)(2,1)S(1)}, u32[]{:S(2)}, u32[]{:S(2)}) collective-permute-start(bf16[736,128]{1,0:T(8,128)(2,1)} %get-tuple-element.26.refs_0_.refs_4_), channel_id=1, source_target_pairs={{0,32},{32,0},{1,33},{33,1},{2,34},{34,2},{3,35},{35,3},{4,36},{36... | collective-permute-start | bytes 565256 | tf_op jit(solution)/shard_map/ppermute | solution.py:86
  6.5 15.4 %all-to-all-start = ((bf16[32,16,128]{2,1,0:T(8,128)(2,1)}), bf16[32,16,128]{2,1,0:T(8,128)(2,1)S(1)}, u32[]{:S(2)}, u32[]{:S(2)}) async-start(bf16[32,16,128]{2,1,0:T(8,128)(2,1)} %bitcast.67), calls=%async_computation | async-start | bytes 262144 | tf_op jit(solution)/shard_map/all_to_all | solution.py:267
  21.9 2.1 %collective-permute-start.2 = (bf16[736,128]{1,0:T(8,128)(2,1)S(1)}, bf16[736,128]{1,0:T(8,128)(2,1)S(1)}, u32[]{:S(2)}, u32[]{:S(2)}) collective-permute-start(bf16[736,128]{1,0:T(8,128)(2,1)S(1)} %collective-permute-done.refs_2_.refs_6_), channel_id=1, source_target_pairs={{0,1},{1,0},{2,3},{3,2},{4,5},{5,4},{6,7},{7,6},{8,9},{9,8},{10,11... | collective-permute-start | bytes 565256 | tf_op jit(solution)/shard_map/ppermute | solution.py:86
  24.2 2.2 %collective-permute-start.1 = (bf16[736,128]{1,0:T(8,128)(2,1)S(1)}, bf16[736,128]{1,0:T(8,128)(2,1)S(1)}, u32[]{:S(2)}, u32[]{:S(2)}) collective-permute-start(bf16[736,128]{1,0:T(8,128)(2,1)S(1)} %copy-done), channel_id=1, source_target_pairs={{0,1},{1,0},{2,3},{3,2},{4,5},{5,4},{6,7},{7,6},{8,9},{9,8},{10,11... | collective-permute-start | bytes 565256 | tf_op jit(solution)/shard_map/ppermute | solution.py:86
  27.2 0.9 copy-done.5
  28.4 3.3 %collective-permute-start.4 = (bf16[1984,128]{1,0:T(8,128)(2,1)S(1)}, bf16[1984,128]{1,0:T(8,128)(2,1)S(1)}, u32[]{:S(2)}, u32[]{:S(2)}) collective-permute-start(bf16[1984,128]{1,0:T(8,128)(2,1)S(1)} %shard_map.130.refs_0_.refs_4_.refs_8_), channel_id=1, source_target_pairs={{0,32},{32,0},{1,33},{33,1},{2,34},{34,2},{3,35},{35,3},{4,36},{36... | collective-permute-start | bytes 1523720 | tf_op jit(solution)/shard_map/ppermute | solution.py:86
  32.0 5.8 %all-to-all-done = bf16[32,16,128]{2,1,0:T(8,128)(2,1)S(1)} async-done(((bf16[32,16,128]{2,1,0:T(8,128)(2,1)}), bf16[32,16,128]{2,1,0:T(8,128)(2,1)S(1)}, u32[]{:S(2)}, u32[]{:S(2)}) %all-to-all-start) | async-done | bytes 131104 | tf_op jit(solution)/shard_map/all_to_all | solution.py:267
  37.8 1.5 shard_map.128
  39.3 6.8 %all-to-all-start.1 = ((bf16[16,2,2,16,128]{4,3,2,1,0:T(8,128)(2,1)}), bf16[16,2,2,16,128]{4,3,2,1,0:T(8,128)(2,1)S(1)}, u32[]{:S(2)}, u32[]{:S(2)}) async-start(bf16[16,2,2,16,128]{4,3,2,1,0:T(8,128)(2,1)} %bitcast.14), calls=%async_computation.1 | async-start | bytes 524288 | tf_op jit(solution)/shard_map/all_to_all | solution.py:205
  46.1 3.9 %collective-permute-start.3 = (bf16[1984,128]{1,0:T(8,128)(2,1)S(1)}, bf16[1984,128]{1,0:T(8,128)(2,1)S(1)}, u32[]{:S(2)}, u32[]{:S(2)}) collective-permute-start(bf16[1984,128]{1,0:T(8,128)(2,1)S(1)} %shard_map.130.refs_0_.refs_4_.refs_8_), channel_id=1, source_target_pairs={{0,1},{1,0},{2,3},{3,2},{4,5},{5,4},{6,7},{7,6},{8,9},{9,8},{10,11... | collective-permute-start | bytes 1523720 | tf_op jit(solution)/shard_map/ppermute | solution.py:86
  50.0 1.9 %collective-permute-start.5 = (bf16[1984,128]{1,0:T(8,128)(2,1)S(1)}, bf16[1984,128]{1,0:T(8,128)(2,1)S(1)}, u32[]{:S(2)}, u32[]{:S(2)}) collective-permute-start(bf16[1984,128]{1,0:T(8,128)(2,1)S(1)} %collective-permute-done.4.refs_2_.refs_6_.refs_10_), channel_id=1, source_target_pairs={{0,1},{1,0},{2,3},{3,2},{4,5},{5,4},{6,7},{7,6},{8,9},{9,8},{10,11... | collective-permute-start | bytes 1523720 | tf_op jit(solution)/shard_map/ppermute | solution.py:86
  51.9 1.5 all-to-all-done.1.got
  54.3 4.6 %all-to-all-start.2 = ((bf16[8,2,2,16,128]{4,3,2,1,0:T(8,128)(2,1)}), bf16[8,2,2,16,128]{4,3,2,1,0:T(8,128)(2,1)S(1)}, u32[]{:S(2)}, u32[]{:S(2)}) async-start(bf16[8,2,2,16,128]{4,3,2,1,0:T(8,128)(2,1)} %get-tuple-element.30), calls=%async_computation.2 | async-start | bytes 262144 | tf_op jit(solution)/shard_map/all_to_all | solution.py:209
  58.9 13.8 %all-to-all-done.2 = bf16[8,2,2,16,128]{4,3,2,1,0:T(8,128)(2,1)S(1)} async-done(((bf16[8,2,2,16,128]{4,3,2,1,0:T(8,128)(2,1)}), bf16[8,2,2,16,128]{4,3,2,1,0:T(8,128)(2,1)S(1)}, u32[]{:S(2)}, u32[]{:S(2)}) %all-to-all-start.2) | async-done | bytes 131104 | tf_op jit(solution)/shard_map/all_to_all | solution.py:209
  73.6 14.2 %all_to_all.40.got = bf16[16,2,2,16,128]{4,3,2,1,0:T(8,128)(2,1)S(1)} all-to-all(bf16[16,2,2,16,128]{4,3,2,1,0:T(8,128)(2,1)S(1)} %bitcast.43), channel_id=1, replica_groups=mesh['zh'=8,'zl'=2,'x'=4,'y'=4,'core'=2] {'x','y'}, dimensions={0} | all-to-all | bytes 524288 | tf_op jit(solution)/shard_map/all_to_all | solution.py:205
  88.1 16.6 %all_to_all.41 = bf16[8,2,2,16,128]{4,3,2,1,0:T(8,128)(2,1)S(1)} all-to-all(bf16[8,2,2,16,128]{4,3,2,1,0:T(8,128)(2,1)S(1)} %get-tuple-element.32), channel_id=1, replica_groups=mesh['zh'=8,'zl'=2,'x'=4,'y'=4,'core'=2] {'zh'}, dimensions={0} | all-to-all | bytes 262144 | tf_op jit(solution)/shard_map/all_to_all | solution.py:209
  105.6 10.7 %all_to_all.42.got = bf16[16,2,2,16,128]{4,3,2,1,0:T(8,128)(2,1)S(1)} all-to-all(bf16[16,2,2,16,128]{4,3,2,1,0:T(8,128)(2,1)S(1)} %bitcast.60), channel_id=1, replica_groups=mesh['zh'=8,'zl'=2,'x'=4,'y'=4,'core'=2] {'x','y'}, dimensions={0} | all-to-all | bytes 524288 | tf_op jit(solution)/shard_map/all_to_all | solution.py:205
  117.1 3.4 %all-to-all-start.6 = ((bf16[8,2,2,16,128]{4,3,2,1,0:T(8,128)(2,1)}), bf16[8,2,2,16,128]{4,3,2,1,0:T(8,128)(2,1)S(1)}, u32[]{:S(2)}, u32[]{:S(2)}) async-start(bf16[8,2,2,16,128]{4,3,2,1,0:T(8,128)(2,1)} %get-tuple-element.35), calls=%async_computation.6 | async-start | bytes 262144 | tf_op jit(solution)/shard_map/all_to_all | solution.py:209
  120.5 6.9 %collective-permute-start.8 = (bf16[2,16,128]{2,1,0:T(8,128)(2,1)S(1)}, bf16[2,16,128]{2,1,0:T(8,128)(2,1)S(1)}, u32[]{:S(2)}, u32[]{:S(2)}) collective-permute-start(bf16[2,16,128]{2,1,0:T(8,128)(2,1)S(1)} %get-tuple-element.45), channel_id=1, source_target_pairs={{0,33},{1,32},{32,1},{33,0},{2,35},{3,34},{34,3},{35,2},{4,37},{5,... | collective-permute-start | bytes 24584 | tf_op jit(solution)/shard_map/ppermute | solution.py:347
  127.4 1.9 %collective-permute-start.6 = (bf16[2,16,128]{2,1,0:T(8,128)(2,1)S(1)}, bf16[2,16,128]{2,1,0:T(8,128)(2,1)S(1)}, u32[]{:S(2)}, u32[]{:S(2)}) collective-permute-start(bf16[2,16,128]{2,1,0:T(8,128)(2,1)S(1)} %get-tuple-element.47), channel_id=1, source_target_pairs={{0,1},{1,0},{32,33},{33,32},{2,3},{3,2},{34,35},{35,34},{4,5},{5,4... | collective-permute-start | bytes 24584 | tf_op jit(solution)/shard_map/ppermute | solution.py:347
  129.3 3.2 %collective-permute-start.7 = (bf16[2,16,128]{2,1,0:T(8,128)(2,1)S(1)}, bf16[2,16,128]{2,1,0:T(8,128)(2,1)S(1)}, u32[]{:S(2)}, u32[]{:S(2)}) collective-permute-start(bf16[2,16,128]{2,1,0:T(8,128)(2,1)S(1)} %get-tuple-element.48), channel_id=1, source_target_pairs={{0,32},{1,33},{32,0},{33,1},{2,34},{3,35},{34,2},{35,3},{4,36},{5,... | collective-permute-start | bytes 24584 | tf_op jit(solution)/shard_map/ppermute | solution.py:347
  132.6 1.4 collective-permute-done.7.home_2
  134.9 19.1 %all_to_all.43 = bf16[64,16,128]{2,1,0:T(8,128)(2,1)S(1)} all-to-all(bf16[64,16,128]{2,1,0:T(8,128)(2,1)S(1)} %bitcast.42), channel_id=1, replica_groups=mesh['zh'=8,'zl'=2,'x'=4,'y'=4,'core'=2] {'zl','x','y','core'}, dimensions={0} | all-to-all | bytes 524288 | tf_op jit(solution)/shard_map/all_to_all | solution.py:350
  (41 shorter events, 6.8 us)
Async XLA Ops:
  0.0 26.5 %copy-start.1 = (bf16[1,1,2,4,128,128]{5,4,3,2,1,0:T(8,128)(2,1)S(1)}, bf16[1,1,2,4,128,128]{5,4,3,2,1,0:T(8,128)(2,1)}, u32[]{:S(2)}) copy-start(bf16[1,1,2,4,128,128]{5,4,3,2,1,0:T(8,128)(2,1)} %param.16) | copy-start | bytes 786436
  0.0 26.5 %copy-start.3 = (bf16[1,1,3,1,128,128]{5,4,3,2,1,0:T(8,128)(2,1)S(1)}, bf16[1,1,3,1,128,128]{5,4,3,2,1,0:T(8,128)(2,1)}, u32[]{:S(2)}) copy-start(bf16[1,1,3,1,128,128]{5,4,3,2,1,0:T(8,128)(2,1)} %param.15) | copy-start | bytes 294916
  0.0 26.5 %copy-start.4 = (bf16[1,1,3,1,64,128]{5,4,3,2,1,0:T(8,128)(2,1)S(1)}, bf16[1,1,3,1,64,128]{5,4,3,2,1,0:T(8,128)(2,1)}, u32[]{:S(2)}) copy-start(bf16[1,1,3,1,64,128]{5,4,3,2,1,0:T(8,128)(2,1)} %param.13) | copy-start | bytes 147460
  2.0 22.2 %copy-start = (bf16[736,128]{1,0:T(8,128)(2,1)S(1)}, bf16[736,128]{1,0:T(8,128)(2,1)}, u32[]{:S(2)}) copy-start(bf16[736,128]{1,0:T(8,128)(2,1)} %get-tuple-element.26.refs_0_.refs_4_) | copy-start | bytes 565252
  2.0 20.0 %collective-permute-start = (bf16[736,128]{1,0:T(8,128)(2,1)}, bf16[736,128]{1,0:T(8,128)(2,1)S(1)}, u32[]{:S(2)}, u32[]{:S(2)}) collective-permute-start(bf16[736,128]{1,0:T(8,128)(2,1)} %get-tuple-element.26.refs_0_.refs_4_), channel_id=1, source_target_pairs={{0,32},{32,0},{1,33},{33,1},{2,34},{34,2},{3,35},{35,3},{4,36},{36... | collective-permute-start | bytes 565256 | tf_op jit(solution)/shard_map/ppermute | solution.py:86
  6.5 20.1 %copy-start.2 = (bf16[1,1,3,1,128,128]{5,4,3,2,1,0:T(8,128)(2,1)S(1)}, bf16[1,1,3,1,128,128]{5,4,3,2,1,0:T(8,128)(2,1)}, u32[]{:S(2)}) copy-start(bf16[1,1,3,1,128,128]{5,4,3,2,1,0:T(8,128)(2,1)} %param.14) | copy-start | bytes 294916
  6.5 31.3 %all-to-all-start = ((bf16[32,16,128]{2,1,0:T(8,128)(2,1)}), bf16[32,16,128]{2,1,0:T(8,128)(2,1)S(1)}, u32[]{:S(2)}, u32[]{:S(2)}) async-start(bf16[32,16,128]{2,1,0:T(8,128)(2,1)} %bitcast.67), calls=%async_computation | async-start | bytes 262144 | tf_op jit(solution)/shard_map/all_to_all | solution.py:267
  21.9 4.5 %collective-permute-start.2 = (bf16[736,128]{1,0:T(8,128)(2,1)S(1)}, bf16[736,128]{1,0:T(8,128)(2,1)S(1)}, u32[]{:S(2)}, u32[]{:S(2)}) collective-permute-start(bf16[736,128]{1,0:T(8,128)(2,1)S(1)} %collective-permute-done.refs_2_.refs_6_), channel_id=1, source_target_pairs={{0,1},{1,0},{2,3},{3,2},{4,5},{5,4},{6,7},{7,6},{8,9},{9,8},{10,11... | collective-permute-start | bytes 565256 | tf_op jit(solution)/shard_map/ppermute | solution.py:86
  24.2 7.7 %collective-permute-start.1 = (bf16[736,128]{1,0:T(8,128)(2,1)S(1)}, bf16[736,128]{1,0:T(8,128)(2,1)S(1)}, u32[]{:S(2)}, u32[]{:S(2)}) collective-permute-start(bf16[736,128]{1,0:T(8,128)(2,1)S(1)} %copy-done), channel_id=1, source_target_pairs={{0,1},{1,0},{2,3},{3,2},{4,5},{5,4},{6,7},{7,6},{8,9},{9,8},{10,11... | collective-permute-start | bytes 565256 | tf_op jit(solution)/shard_map/ppermute | solution.py:86
  26.5 0.7 copy-start.8
  26.5 0.7 copy-start.6
  27.2 0.9 copy-start.5
  28.4 21.6 %collective-permute-start.4 = (bf16[1984,128]{1,0:T(8,128)(2,1)S(1)}, bf16[1984,128]{1,0:T(8,128)(2,1)S(1)}, u32[]{:S(2)}, u32[]{:S(2)}) collective-permute-start(bf16[1984,128]{1,0:T(8,128)(2,1)S(1)} %shard_map.130.refs_0_.refs_4_.refs_8_), channel_id=1, source_target_pairs={{0,32},{32,0},{1,33},{33,1},{2,34},{34,2},{3,35},{35,3},{4,36},{36... | collective-permute-start | bytes 1523720 | tf_op jit(solution)/shard_map/ppermute | solution.py:86
  39.3 14.1 %all-to-all-start.1 = ((bf16[16,2,2,16,128]{4,3,2,1,0:T(8,128)(2,1)}), bf16[16,2,2,16,128]{4,3,2,1,0:T(8,128)(2,1)S(1)}, u32[]{:S(2)}, u32[]{:S(2)}) async-start(bf16[16,2,2,16,128]{4,3,2,1,0:T(8,128)(2,1)} %bitcast.14), calls=%async_computation.1 | async-start | bytes 524288 | tf_op jit(solution)/shard_map/all_to_all | solution.py:205
  46.1 12.8 %collective-permute-start.3 = (bf16[1984,128]{1,0:T(8,128)(2,1)S(1)}, bf16[1984,128]{1,0:T(8,128)(2,1)S(1)}, u32[]{:S(2)}, u32[]{:S(2)}) collective-permute-start(bf16[1984,128]{1,0:T(8,128)(2,1)S(1)} %shard_map.130.refs_0_.refs_4_.refs_8_), channel_id=1, source_target_pairs={{0,1},{1,0},{2,3},{3,2},{4,5},{5,4},{6,7},{7,6},{8,9},{9,8},{10,11... | collective-permute-start | bytes 1523720 | tf_op jit(solution)/shard_map/ppermute | solution.py:86
  50.0 22.7 %collective-permute-start.5 = (bf16[1984,128]{1,0:T(8,128)(2,1)S(1)}, bf16[1984,128]{1,0:T(8,128)(2,1)S(1)}, u32[]{:S(2)}, u32[]{:S(2)}) collective-permute-start(bf16[1984,128]{1,0:T(8,128)(2,1)S(1)} %collective-permute-done.4.refs_2_.refs_6_.refs_10_), channel_id=1, source_target_pairs={{0,1},{1,0},{2,3},{3,2},{4,5},{5,4},{6,7},{7,6},{8,9},{9,8},{10,11... | collective-permute-start | bytes 1523720 | tf_op jit(solution)/shard_map/ppermute | solution.py:86
  54.3 18.4 %all-to-all-start.2 = ((bf16[8,2,2,16,128]{4,3,2,1,0:T(8,128)(2,1)}), bf16[8,2,2,16,128]{4,3,2,1,0:T(8,128)(2,1)S(1)}, u32[]{:S(2)}, u32[]{:S(2)}) async-start(bf16[8,2,2,16,128]{4,3,2,1,0:T(8,128)(2,1)} %get-tuple-element.30), calls=%async_computation.2 | async-start | bytes 262144 | tf_op jit(solution)/shard_map/all_to_all | solution.py:209
  117.1 16.9 %all-to-all-start.6 = ((bf16[8,2,2,16,128]{4,3,2,1,0:T(8,128)(2,1)}), bf16[8,2,2,16,128]{4,3,2,1,0:T(8,128)(2,1)S(1)}, u32[]{:S(2)}, u32[]{:S(2)}) async-start(bf16[8,2,2,16,128]{4,3,2,1,0:T(8,128)(2,1)} %get-tuple-element.35), calls=%async_computation.6 | async-start | bytes 262144 | tf_op jit(solution)/shard_map/all_to_all | solution.py:209
  120.5 12.1 %collective-permute-start.8 = (bf16[2,16,128]{2,1,0:T(8,128)(2,1)S(1)}, bf16[2,16,128]{2,1,0:T(8,128)(2,1)S(1)}, u32[]{:S(2)}, u32[]{:S(2)}) collective-permute-start(bf16[2,16,128]{2,1,0:T(8,128)(2,1)S(1)} %get-tuple-element.45), channel_id=1, source_target_pairs={{0,33},{1,32},{32,1},{33,0},{2,35},{3,34},{34,3},{35,2},{4,37},{5,... | collective-permute-start | bytes 24584 | tf_op jit(solution)/shard_map/ppermute | solution.py:347
  127.4 5.2 %collective-permute-start.6 = (bf16[2,16,128]{2,1,0:T(8,128)(2,1)S(1)}, bf16[2,16,128]{2,1,0:T(8,128)(2,1)S(1)}, u32[]{:S(2)}, u32[]{:S(2)}) collective-permute-start(bf16[2,16,128]{2,1,0:T(8,128)(2,1)S(1)} %get-tuple-element.47), channel_id=1, source_target_pairs={{0,1},{1,0},{32,33},{33,32},{2,3},{3,2},{34,35},{35,34},{4,5},{5,4... | collective-permute-start | bytes 24584 | tf_op jit(solution)/shard_map/ppermute | solution.py:347
  129.3 4.7 %collective-permute-start.7 = (bf16[2,16,128]{2,1,0:T(8,128)(2,1)S(1)}, bf16[2,16,128]{2,1,0:T(8,128)(2,1)S(1)}, u32[]{:S(2)}, u32[]{:S(2)}) collective-permute-start(bf16[2,16,128]{2,1,0:T(8,128)(2,1)S(1)} %get-tuple-element.48), channel_id=1, source_target_pairs={{0,32},{1,33},{32,0},{33,1},{2,34},{3,35},{34,2},{35,3},{4,36},{5,... | collective-permute-start | bytes 24584 | tf_op jit(solution)/shard_map/ppermute | solution.py:347
  134.9 19.2 %copy-start.7 = (bf16[64,128]{1,0:T(8,128)(2,1)S(1)}, bf16[64,128]{1,0:T(8,128)(2,1)}, u32[]{:S(2)}) copy-start(bf16[64,128]{1,0:T(8,128)(2,1)} %get-tuple-element.40.forward) | copy-start | bytes 49156

commit v8 on v7

--- a/solution.py
+++ b/solution.py
@@ -93,14 +93,15 @@
 def scatter_kernel(group, level, by_target, after, place, table, column, *refs):
     tiles, before = refs[:SPLIT], refs[SPLIT] if after else None
     partial, terms, sums = (refs[-2], None, refs[-1]) if after else refs[-3:]
-    zl, core = place[0], place[1]
+    zl, core = lax.axis_index("zl"), lax.axis_index("core")
+    entries = table[...]
     extent = column.shape[3]
     blocks = tiles[0].shape[0] // extent
     targets = partial.shape[1] if by_target else partial.shape[0]
     sums[...] = jnp.zeros(sums.shape, F32)
 
     def add(step, entry, row, term):
-        goal = table[step, entry] - level * targets
+        goal = entries[step, entry] - level * targets
         slot = jnp.where((goal >= 0) & (goal < targets), goal, targets)
         at = (pl.ds(row, 1), pl.ds(slot, 1)) if by_target else (pl.ds(slot, 1), pl.ds(row, 1))
         sums[at] = sums[at] + term[None, None]
@@ -109,7 +110,7 @@
     for step, (dz, dc) in enumerate(offsets()):
         half = lax.bitwise_xor(core, dc)
         for b in range(blocks):
-            source = jnp.clip(table[step, 2 * blocks * group + b], 0, column.shape[0] - 1)
+            source = jnp.clip(entries[step, 2 * blocks * group + b], 0, column.shape[0] - 1)
             products.append(
                 jnp.dot(
                     column[pl.ds(source, 1), pl.ds(half, 1)][0, 0],
@@ -302,7 +303,7 @@
         return pl.pallas_call(
             functools.partial(scatter_kernel, group, level, by_target, before is not None),
             grid=(1,),
-            in_specs=[scalars(), scalars(), whole(column)] + [tile_block] * SPLIT + extra_specs,
+            in_specs=[whole(place), whole(table), whole(column)] + [tile_block] * SPLIT + extra_specs,
             out_shape=[partial, terms] if before is None else [partial],
             out_specs=[whole(partial), whole(terms)] if before is None else [whole(partial)],
             scratch_shapes=[pltpu.VMEM(sums + (rows, extent), F32)],

time: 156 us -> 155 us (level)
  Pallas kernels: 9.12 us -> 7.22 us
    pallas_call x4, Pallas kernels: 4.09 us -> 2.2 us  [edge(): pl.pallas_call(functools.partial(scatter_kernel, group, level, by_target,...]
  transfers between devices with their start and end apart: 13 -> 13, of which waited for: 4 -> 4; matrix products, arithmetic and copies ran while one was open for 0% -> 0% of each run, Pallas kernels for 2% -> 1%
where the time goes in v8:
time: 155 us; the launch traced here: 154 us
  blocking collectives  61 us (39%)
  starting transfers between devices  60.2 us (39%)
  waiting for transfers between devices  23 us (15%)
  Pallas kernels  7.22 us (5%)
  local copies, waits for them, and re-layouts  1.96 us (1%)
    all_to_all x2, blocking collectives, row_exchange(): return lax.all_to_all(chunks, ('x', 'y'), 0, 0, tiled=True)  25.3 us
    all_to_all x1, blocking collectives, body(): lax.all_to_all(partial.reshape(-1, rows, extent), ('zl', 'x', 'y', 'core'...  19.2 us
    ppermute x6, starting transfers between devices, swapped(): return lax.ppermute(value, axis, [(0, 1), (1, 0)])  17.9 us
    all_to_all x1, blocking collectives, gather_column(): got = lax.all_to_all(copies, 'zh', 0, 0, tiled=True)  16.6 us
    all_to_all x1, starting transfers between devices, body(): column = lax.all_to_all(copies, ('zh', 'zl', 'core'), 0, 0, tiled=True)  15.4 us
    all_to_all x2, waiting for transfers between devices, gather_column(): got = lax.all_to_all(copies, 'zh', 0, 0, tiled=True)  13.9 us
    ppermute x3, starting transfers between devices, body(): lax.ppermute(done[step], GROUP, [(i, i ^ step) for i in range(SPLIT)])  12 us
    all_to_all x2, starting transfers between devices, gather_column(): got = lax.all_to_all(copies, 'zh', 0, 0, tiled=True)  8.03 us
  transfers between devices with their start and end apart: 13, of which 4 were waited for; matrix products, arithmetic and copies ran while one was open for 0% of the time, Pallas kernels for 1%

profile of v8, /device:TPU:1, one launch (start us, length us, event | category | flops | bytes accessed | tf_op | source)
XLA Modules:
  0.0 153.8 jit_solution(7041442025388110175)
XLA Ops:
  0.0 1.9 %shard_map.127 = (bf16[736,128]{1,0:T(8,128)(2,1)}, bf16[8,64,128]{2,1,0:T(8,128)(2,1)}, bf16[64,128]{1,0:T(8,128)(2,1)}) custom-call(bf16[3,64,128]{2,1,0:T(8,128)(2,1)} %bitcast.57, bf16[3,64,128]{2,1,0:T(8,128)(2,1)} %bitcast.58, bf16[3,128,128]{2,1,0:T(8,128)(2,1)} %bitcast.47, bf16[3,128,128]{2,1,0:T(8,128)(2,1)} %bitcast.48, ...), custom_call_target="tpu_custom_call" | custom-call | tf_op jit(solution)/shard_map/pallas_call | solution.py:244
  2.0 4.5 %collective-permute-start = (bf16[736,128]{1,0:T(8,128)(2,1)}, bf16[736,128]{1,0:T(8,128)(2,1)S(1)}, u32[]{:S(2)}, u32[]{:S(2)}) collective-permute-start(bf16[736,128]{1,0:T(8,128)(2,1)} %get-tuple-element.26.refs_0_.refs_4_), channel_id=1, source_target_pairs={{0,32},{32,0},{1,33},{33,1},{2,34},{34,2},{3,35},{35,3},{4,36},{36... | collective-permute-start | bytes 565256 | tf_op jit(solution)/shard_map/ppermute | solution.py:86
  6.5 15.4 %all-to-all-start = ((bf16[32,16,128]{2,1,0:T(8,128)(2,1)}), bf16[32,16,128]{2,1,0:T(8,128)(2,1)S(1)}, u32[]{:S(2)}, u32[]{:S(2)}) async-start(bf16[32,16,128]{2,1,0:T(8,128)(2,1)} %bitcast.67), calls=%async_computation | async-start | bytes 262144 | tf_op jit(solution)/shard_map/all_to_all | solution.py:268
  21.9 2.1 %collective-permute-start.2 = (bf16[736,128]{1,0:T(8,128)(2,1)S(1)}, bf16[736,128]{1,0:T(8,128)(2,1)S(1)}, u32[]{:S(2)}, u32[]{:S(2)}) collective-permute-start(bf16[736,128]{1,0:T(8,128)(2,1)S(1)} %collective-permute-done.refs_2_.refs_6_), channel_id=1, source_target_pairs={{0,1},{1,0},{2,3},{3,2},{4,5},{5,4},{6,7},{7,6},{8,9},{9,8},{10,11... | collective-permute-start | bytes 565256 | tf_op jit(solution)/shard_map/ppermute | solution.py:86
  24.2 2.2 %collective-permute-start.1 = (bf16[736,128]{1,0:T(8,128)(2,1)S(1)}, bf16[736,128]{1,0:T(8,128)(2,1)S(1)}, u32[]{:S(2)}, u32[]{:S(2)}) collective-permute-start(bf16[736,128]{1,0:T(8,128)(2,1)S(1)} %copy-done), channel_id=1, source_target_pairs={{0,1},{1,0},{2,3},{3,2},{4,5},{5,4},{6,7},{7,6},{8,9},{9,8},{10,11... | collective-permute-start | bytes 565256 | tf_op jit(solution)/shard_map/ppermute | solution.py:86
  27.2 0.9 copy-done.5
  28.4 3.3 %collective-permute-start.4 = (bf16[1984,128]{1,0:T(8,128)(2,1)S(1)}, bf16[1984,128]{1,0:T(8,128)(2,1)S(1)}, u32[]{:S(2)}, u32[]{:S(2)}) collective-permute-start(bf16[1984,128]{1,0:T(8,128)(2,1)S(1)} %shard_map.130.refs_0_.refs_4_.refs_8_), channel_id=1, source_target_pairs={{0,32},{32,0},{1,33},{33,1},{2,34},{34,2},{3,35},{35,3},{4,36},{36... | collective-permute-start | bytes 1523720 | tf_op jit(solution)/shard_map/ppermute | solution.py:86
  32.0 5.8 %all-to-all-done = bf16[32,16,128]{2,1,0:T(8,128)(2,1)S(1)} async-done(((bf16[32,16,128]{2,1,0:T(8,128)(2,1)}), bf16[32,16,128]{2,1,0:T(8,128)(2,1)S(1)}, u32[]{:S(2)}, u32[]{:S(2)}) %all-to-all-start) | async-done | bytes 131104 | tf_op jit(solution)/shard_map/all_to_all | solution.py:268
  37.8 1.1 shard_map.128
  38.9 6.8 %all-to-all-start.1 = ((bf16[16,2,2,16,128]{4,3,2,1,0:T(8,128)(2,1)}), bf16[16,2,2,16,128]{4,3,2,1,0:T(8,128)(2,1)S(1)}, u32[]{:S(2)}, u32[]{:S(2)}) async-start(bf16[16,2,2,16,128]{4,3,2,1,0:T(8,128)(2,1)} %bitcast.14), calls=%async_computation.1 | async-start | bytes 524288 | tf_op jit(solution)/shard_map/all_to_all | solution.py:206
  45.6 3.9 %collective-permute-start.3 = (bf16[1984,128]{1,0:T(8,128)(2,1)S(1)}, bf16[1984,128]{1,0:T(8,128)(2,1)S(1)}, u32[]{:S(2)}, u32[]{:S(2)}) collective-permute-start(bf16[1984,128]{1,0:T(8,128)(2,1)S(1)} %shard_map.130.refs_0_.refs_4_.refs_8_), channel_id=1, source_target_pairs={{0,1},{1,0},{2,3},{3,2},{4,5},{5,4},{6,7},{7,6},{8,9},{9,8},{10,11... | collective-permute-start | bytes 1523720 | tf_op jit(solution)/shard_map/ppermute | solution.py:86
  49.5 1.9 %collective-permute-start.5 = (bf16[1984,128]{1,0:T(8,128)(2,1)S(1)}, bf16[1984,128]{1,0:T(8,128)(2,1)S(1)}, u32[]{:S(2)}, u32[]{:S(2)}) collective-permute-start(bf16[1984,128]{1,0:T(8,128)(2,1)S(1)} %collective-permute-done.4.refs_2_.refs_6_.refs_10_), channel_id=1, source_target_pairs={{0,1},{1,0},{2,3},{3,2},{4,5},{5,4},{6,7},{7,6},{8,9},{9,8},{10,11... | collective-permute-start | bytes 1523720 | tf_op jit(solution)/shard_map/ppermute | solution.py:86
  51.5 1.5 all-to-all-done.1.got
  53.8 4.7 %all-to-all-start.2 = ((bf16[8,2,2,16,128]{4,3,2,1,0:T(8,128)(2,1)}), bf16[8,2,2,16,128]{4,3,2,1,0:T(8,128)(2,1)S(1)}, u32[]{:S(2)}, u32[]{:S(2)}) async-start(bf16[8,2,2,16,128]{4,3,2,1,0:T(8,128)(2,1)} %get-tuple-element.30), calls=%async_computation.2 | async-start | bytes 262144 | tf_op jit(solution)/shard_map/all_to_all | solution.py:210
  58.5 13.9 %all-to-all-done.2 = bf16[8,2,2,16,128]{4,3,2,1,0:T(8,128)(2,1)S(1)} async-done(((bf16[8,2,2,16,128]{4,3,2,1,0:T(8,128)(2,1)}), bf16[8,2,2,16,128]{4,3,2,1,0:T(8,128)(2,1)S(1)}, u32[]{:S(2)}, u32[]{:S(2)}) %all-to-all-start.2) | async-done | bytes 131104 | tf_op jit(solution)/shard_map/all_to_all | solution.py:210
  72.7 14.6 %all_to_all.40.got = bf16[16,2,2,16,128]{4,3,2,1,0:T(8,128)(2,1)S(1)} all-to-all(bf16[16,2,2,16,128]{4,3,2,1,0:T(8,128)(2,1)S(1)} %bitcast.43), channel_id=1, replica_groups=mesh['zh'=8,'zl'=2,'x'=4,'y'=4,'core'=2] {'x','y'}, dimensions={0} | all-to-all | bytes 524288 | tf_op jit(solution)/shard_map/all_to_all | solution.py:206
  87.6 16.6 %all_to_all.41 = bf16[8,2,2,16,128]{4,3,2,1,0:T(8,128)(2,1)S(1)} all-to-all(bf16[8,2,2,16,128]{4,3,2,1,0:T(8,128)(2,1)S(1)} %get-tuple-element.32), channel_id=1, replica_groups=mesh['zh'=8,'zl'=2,'x'=4,'y'=4,'core'=2] {'zh'}, dimensions={0} | all-to-all | bytes 262144 | tf_op jit(solution)/shard_map/all_to_all | solution.py:210
  104.6 10.7 %all_to_all.42.got = bf16[16,2,2,16,128]{4,3,2,1,0:T(8,128)(2,1)S(1)} all-to-all(bf16[16,2,2,16,128]{4,3,2,1,0:T(8,128)(2,1)S(1)} %bitcast.60), channel_id=1, replica_groups=mesh['zh'=8,'zl'=2,'x'=4,'y'=4,'core'=2] {'x','y'}, dimensions={0} | all-to-all | bytes 524288 | tf_op jit(solution)/shard_map/all_to_all | solution.py:206
  116.2 3.4 %all-to-all-start.6 = ((bf16[8,2,2,16,128]{4,3,2,1,0:T(8,128)(2,1)}), bf16[8,2,2,16,128]{4,3,2,1,0:T(8,128)(2,1)S(1)}, u32[]{:S(2)}, u32[]{:S(2)}) async-start(bf16[8,2,2,16,128]{4,3,2,1,0:T(8,128)(2,1)} %get-tuple-element.35), calls=%async_computation.6 | async-start | bytes 262144 | tf_op jit(solution)/shard_map/all_to_all | solution.py:210
  119.5 6.9 %collective-permute-start.8 = (bf16[2,16,128]{2,1,0:T(8,128)(2,1)S(1)}, bf16[2,16,128]{2,1,0:T(8,128)(2,1)S(1)}, u32[]{:S(2)}, u32[]{:S(2)}) collective-permute-start(bf16[2,16,128]{2,1,0:T(8,128)(2,1)S(1)} %get-tuple-element.45), channel_id=1, source_target_pairs={{0,33},{1,32},{32,1},{33,0},{2,35},{3,34},{34,3},{35,2},{4,37},{5,... | collective-permute-start | bytes 24584 | tf_op jit(solution)/shard_map/ppermute | solution.py:348
  126.4 1.9 %collective-permute-start.6 = (bf16[2,16,128]{2,1,0:T(8,128)(2,1)S(1)}, bf16[2,16,128]{2,1,0:T(8,128)(2,1)S(1)}, u32[]{:S(2)}, u32[]{:S(2)}) collective-permute-start(bf16[2,16,128]{2,1,0:T(8,128)(2,1)S(1)} %get-tuple-element.47), channel_id=1, source_target_pairs={{0,1},{1,0},{32,33},{33,32},{2,3},{3,2},{34,35},{35,34},{4,5},{5,4... | collective-permute-start | bytes 24584 | tf_op jit(solution)/shard_map/ppermute | solution.py:348
  128.4 3.2 %collective-permute-start.7 = (bf16[2,16,128]{2,1,0:T(8,128)(2,1)S(1)}, bf16[2,16,128]{2,1,0:T(8,128)(2,1)S(1)}, u32[]{:S(2)}, u32[]{:S(2)}) collective-permute-start(bf16[2,16,128]{2,1,0:T(8,128)(2,1)S(1)} %get-tuple-element.48), channel_id=1, source_target_pairs={{0,32},{1,33},{32,0},{33,1},{2,34},{3,35},{34,2},{35,3},{4,36},{5,... | collective-permute-start | bytes 24584 | tf_op jit(solution)/shard_map/ppermute | solution.py:348
  131.6 1.8 %collective-permute-done.7.home_2 = bf16[2,16,128]{2,1,0:T(8,128)(2,1)S(1)} collective-permute-done((bf16[2,16,128]{2,1,0:T(8,128)(2,1)S(1)}, bf16[2,16,128]{2,1,0:T(8,128)(2,1)S(1)}, u32[]{:S(2)}, u32[]{:S(2)}) %collective-permute-start.7) | collective-permute-done | bytes 8224 | tf_op jit(solution)/shard_map/ppermute | solution.py:348
  133.9 19.2 %all_to_all.43 = bf16[64,16,128]{2,1,0:T(8,128)(2,1)S(1)} all-to-all(bf16[64,16,128]{2,1,0:T(8,128)(2,1)S(1)} %bitcast.42), channel_id=1, replica_groups=mesh['zh'=8,'zl'=2,'x'=4,'y'=4,'core'=2] {'zl','x','y','core'}, dimensions={0} | all-to-all | bytes 524288 | tf_op jit(solution)/shard_map/all_to_all | solution.py:351
  (41 shorter events, 5.3 us)
Async XLA Ops:
  0.0 26.5 %copy-start.1 = (bf16[1,1,2,4,128,128]{5,4,3,2,1,0:T(8,128)(2,1)S(1)}, bf16[1,1,2,4,128,128]{5,4,3,2,1,0:T(8,128)(2,1)}, u32[]{:S(2)}) copy-start(bf16[1,1,2,4,128,128]{5,4,3,2,1,0:T(8,128)(2,1)} %param.16) | copy-start | bytes 786436
  0.0 26.5 %copy-start.3 = (bf16[1,1,3,1,128,128]{5,4,3,2,1,0:T(8,128)(2,1)S(1)}, bf16[1,1,3,1,128,128]{5,4,3,2,1,0:T(8,128)(2,1)}, u32[]{:S(2)}) copy-start(bf16[1,1,3,1,128,128]{5,4,3,2,1,0:T(8,128)(2,1)} %param.15) | copy-start | bytes 294916
  0.0 26.5 %copy-start.4 = (bf16[1,1,3,1,64,128]{5,4,3,2,1,0:T(8,128)(2,1)S(1)}, bf16[1,1,3,1,64,128]{5,4,3,2,1,0:T(8,128)(2,1)}, u32[]{:S(2)}) copy-start(bf16[1,1,3,1,64,128]{5,4,3,2,1,0:T(8,128)(2,1)} %param.13) | copy-start | bytes 147460
  2.0 22.2 %copy-start = (bf16[736,128]{1,0:T(8,128)(2,1)S(1)}, bf16[736,128]{1,0:T(8,128)(2,1)}, u32[]{:S(2)}) copy-start(bf16[736,128]{1,0:T(8,128)(2,1)} %get-tuple-element.26.refs_0_.refs_4_) | copy-start | bytes 565252
  2.0 20.0 %collective-permute-start = (bf16[736,128]{1,0:T(8,128)(2,1)}, bf16[736,128]{1,0:T(8,128)(2,1)S(1)}, u32[]{:S(2)}, u32[]{:S(2)}) collective-permute-start(bf16[736,128]{1,0:T(8,128)(2,1)} %get-tuple-element.26.refs_0_.refs_4_), channel_id=1, source_target_pairs={{0,32},{32,0},{1,33},{33,1},{2,34},{34,2},{3,35},{35,3},{4,36},{36... | collective-permute-start | bytes 565256 | tf_op jit(solution)/shard_map/ppermute | solution.py:86
  6.5 20.1 %copy-start.2 = (bf16[1,1,3,1,128,128]{5,4,3,2,1,0:T(8,128)(2,1)S(1)}, bf16[1,1,3,1,128,128]{5,4,3,2,1,0:T(8,128)(2,1)}, u32[]{:S(2)}) copy-start(bf16[1,1,3,1,128,128]{5,4,3,2,1,0:T(8,128)(2,1)} %param.14) | copy-start | bytes 294916
  6.5 31.3 %all-to-all-start = ((bf16[32,16,128]{2,1,0:T(8,128)(2,1)}), bf16[32,16,128]{2,1,0:T(8,128)(2,1)S(1)}, u32[]{:S(2)}, u32[]{:S(2)}) async-start(bf16[32,16,128]{2,1,0:T(8,128)(2,1)} %bitcast.67), calls=%async_computation | async-start | bytes 262144 | tf_op jit(solution)/shard_map/all_to_all | solution.py:268
  21.9 4.5 %collective-permute-start.2 = (bf16[736,128]{1,0:T(8,128)(2,1)S(1)}, bf16[736,128]{1,0:T(8,128)(2,1)S(1)}, u32[]{:S(2)}, u32[]{:S(2)}) collective-permute-start(bf16[736,128]{1,0:T(8,128)(2,1)S(1)} %collective-permute-done.refs_2_.refs_6_), channel_id=1, source_target_pairs={{0,1},{1,0},{2,3},{3,2},{4,5},{5,4},{6,7},{7,6},{8,9},{9,8},{10,11... | collective-permute-start | bytes 565256 | tf_op jit(solution)/shard_map/ppermute | solution.py:86
  24.2 7.7 %collective-permute-start.1 = (bf16[736,128]{1,0:T(8,128)(2,1)S(1)}, bf16[736,128]{1,0:T(8,128)(2,1)S(1)}, u32[]{:S(2)}, u32[]{:S(2)}) collective-permute-start(bf16[736,128]{1,0:T(8,128)(2,1)S(1)} %copy-done), channel_id=1, source_target_pairs={{0,1},{1,0},{2,3},{3,2},{4,5},{5,4},{6,7},{7,6},{8,9},{9,8},{10,11... | collective-permute-start | bytes 565256 | tf_op jit(solution)/shard_map/ppermute | solution.py:86
  26.5 0.7 copy-start.8
  26.5 0.7 copy-start.6
  27.2 0.9 copy-start.5
  28.4 21.1 %collective-permute-start.4 = (bf16[1984,128]{1,0:T(8,128)(2,1)S(1)}, bf16[1984,128]{1,0:T(8,128)(2,1)S(1)}, u32[]{:S(2)}, u32[]{:S(2)}) collective-permute-start(bf16[1984,128]{1,0:T(8,128)(2,1)S(1)} %shard_map.130.refs_0_.refs_4_.refs_8_), channel_id=1, source_target_pairs={{0,32},{32,0},{1,33},{33,1},{2,34},{34,2},{3,35},{35,3},{4,36},{36... | collective-permute-start | bytes 1523720 | tf_op jit(solution)/shard_map/ppermute | solution.py:86
  38.9 14.1 %all-to-all-start.1 = ((bf16[16,2,2,16,128]{4,3,2,1,0:T(8,128)(2,1)}), bf16[16,2,2,16,128]{4,3,2,1,0:T(8,128)(2,1)S(1)}, u32[]{:S(2)}, u32[]{:S(2)}) async-start(bf16[16,2,2,16,128]{4,3,2,1,0:T(8,128)(2,1)} %bitcast.14), calls=%async_computation.1 | async-start | bytes 524288 | tf_op jit(solution)/shard_map/all_to_all | solution.py:206
  45.6 12.9 %collective-permute-start.3 = (bf16[1984,128]{1,0:T(8,128)(2,1)S(1)}, bf16[1984,128]{1,0:T(8,128)(2,1)S(1)}, u32[]{:S(2)}, u32[]{:S(2)}) collective-permute-start(bf16[1984,128]{1,0:T(8,128)(2,1)S(1)} %shard_map.130.refs_0_.refs_4_.refs_8_), channel_id=1, source_target_pairs={{0,1},{1,0},{2,3},{3,2},{4,5},{5,4},{6,7},{7,6},{8,9},{9,8},{10,11... | collective-permute-start | bytes 1523720 | tf_op jit(solution)/shard_map/ppermute | solution.py:86
  49.5 22.8 %collective-permute-start.5 = (bf16[1984,128]{1,0:T(8,128)(2,1)S(1)}, bf16[1984,128]{1,0:T(8,128)(2,1)S(1)}, u32[]{:S(2)}, u32[]{:S(2)}) collective-permute-start(bf16[1984,128]{1,0:T(8,128)(2,1)S(1)} %collective-permute-done.4.refs_2_.refs_6_.refs_10_), channel_id=1, source_target_pairs={{0,1},{1,0},{2,3},{3,2},{4,5},{5,4},{6,7},{7,6},{8,9},{9,8},{10,11... | collective-permute-start | bytes 1523720 | tf_op jit(solution)/shard_map/ppermute | solution.py:86
  53.8 18.5 %all-to-all-start.2 = ((bf16[8,2,2,16,128]{4,3,2,1,0:T(8,128)(2,1)}), bf16[8,2,2,16,128]{4,3,2,1,0:T(8,128)(2,1)S(1)}, u32[]{:S(2)}, u32[]{:S(2)}) async-start(bf16[8,2,2,16,128]{4,3,2,1,0:T(8,128)(2,1)} %get-tuple-element.30), calls=%async_computation.2 | async-start | bytes 262144 | tf_op jit(solution)/shard_map/all_to_all | solution.py:210
  116.2 17.3 %all-to-all-start.6 = ((bf16[8,2,2,16,128]{4,3,2,1,0:T(8,128)(2,1)}), bf16[8,2,2,16,128]{4,3,2,1,0:T(8,128)(2,1)S(1)}, u32[]{:S(2)}, u32[]{:S(2)}) async-start(bf16[8,2,2,16,128]{4,3,2,1,0:T(8,128)(2,1)} %get-tuple-element.35), calls=%async_computation.6 | async-start | bytes 262144 | tf_op jit(solution)/shard_map/all_to_all | solution.py:210
  119.5 12.1 %collective-permute-start.8 = (bf16[2,16,128]{2,1,0:T(8,128)(2,1)S(1)}, bf16[2,16,128]{2,1,0:T(8,128)(2,1)S(1)}, u32[]{:S(2)}, u32[]{:S(2)}) collective-permute-start(bf16[2,16,128]{2,1,0:T(8,128)(2,1)S(1)} %get-tuple-element.45), channel_id=1, source_target_pairs={{0,33},{1,32},{32,1},{33,0},{2,35},{3,34},{34,3},{35,2},{4,37},{5,... | collective-permute-start | bytes 24584 | tf_op jit(solution)/shard_map/ppermute | solution.py:348
  126.4 5.2 %collective-permute-start.6 = (bf16[2,16,128]{2,1,0:T(8,128)(2,1)S(1)}, bf16[2,16,128]{2,1,0:T(8,128)(2,1)S(1)}, u32[]{:S(2)}, u32[]{:S(2)}) collective-permute-start(bf16[2,16,128]{2,1,0:T(8,128)(2,1)S(1)} %get-tuple-element.47), channel_id=1, source_target_pairs={{0,1},{1,0},{32,33},{33,32},{2,3},{3,2},{34,35},{35,34},{4,5},{5,4... | collective-permute-start | bytes 24584 | tf_op jit(solution)/shard_map/ppermute | solution.py:348
  128.4 5.1 %collective-permute-start.7 = (bf16[2,16,128]{2,1,0:T(8,128)(2,1)S(1)}, bf16[2,16,128]{2,1,0:T(8,128)(2,1)S(1)}, u32[]{:S(2)}, u32[]{:S(2)}) collective-permute-start(bf16[2,16,128]{2,1,0:T(8,128)(2,1)S(1)} %get-tuple-element.48), channel_id=1, source_target_pairs={{0,32},{1,33},{32,0},{33,1},{2,34},{3,35},{34,2},{35,3},{4,36},{5,... | collective-permute-start | bytes 24584 | tf_op jit(solution)/shard_map/ppermute | solution.py:348
  133.8 19.2 %copy-start.7 = (bf16[64,128]{1,0:T(8,128)(2,1)S(1)}, bf16[64,128]{1,0:T(8,128)(2,1)}, u32[]{:S(2)}) copy-start(bf16[64,128]{1,0:T(8,128)(2,1)} %get-tuple-element.40.forward) | copy-start | bytes 49156

commit v9 on v8

--- a/solution.py
+++ b/solution.py
@@ -271,7 +271,7 @@
     first = (packed, swapped(packed, "core"), z_mate, swapped(z_mate, "core"))
 
     later_sizes = [tile_rows] * 3 + [extent] * 3 + [side_extent]
-    start = first[3][:16]
+    start = z_mate[:16]
     packed = pl.pallas_call(
         later_kernel,
         grid=(1,),

time: 155 us -> 154 us (level)
  no operation moved by 1% of the time
where the time goes in v9:
time: 154 us; the launch traced here: 153 us
  blocking collectives  61 us (40%)
  starting transfers between devices  59.8 us (39%)
  waiting for transfers between devices  23.1 us (15%)
  Pallas kernels  7.22 us (5%)
    all_to_all x2, blocking collectives, row_exchange(): return lax.all_to_all(chunks, ('x', 'y'), 0, 0, tiled=True)  25.3 us
    all_to_all x1, blocking collectives, body(): lax.all_to_all(partial.reshape(-1, rows, extent), ('zl', 'x', 'y', 'core'...  19.1 us
    ppermute x6, starting transfers between devices, swapped(): return lax.ppermute(value, axis, [(0, 1), (1, 0)])  18.1 us
    all_to_all x1, blocking collectives, gather_column(): got = lax.all_to_all(copies, 'zh', 0, 0, tiled=True)  16.6 us
    all_to_all x1, starting transfers between devices, body(): column = lax.all_to_all(copies, ('zh', 'zl', 'core'), 0, 0, tiled=True)  15.4 us
    all_to_all x2, waiting for transfers between devices, gather_column(): got = lax.all_to_all(copies, 'zh', 0, 0, tiled=True)  13.8 us
    ppermute x3, starting transfers between devices, body(): lax.ppermute(done[step], GROUP, [(i, i ^ step) for i in range(SPLIT)])  12 us
    all_to_all x2, starting transfers between devices, gather_column(): got = lax.all_to_all(copies, 'zh', 0, 0, tiled=True)  7.5 us
  transfers between devices with their start and end apart: 13, of which 4 were waited for; matrix products, arithmetic and copies ran while one was open for 0% of the time, Pallas kernels for 1%

profile of v9, /device:TPU:1, one launch (start us, length us, event | category | flops | bytes accessed | tf_op | source)
XLA Modules:
  0.0 152.8 jit_solution(16793673630518225074)
XLA Ops:
  0.0 1.9 %shard_map.127 = (bf16[736,128]{1,0:T(8,128)(2,1)}, bf16[8,64,128]{2,1,0:T(8,128)(2,1)}, bf16[64,128]{1,0:T(8,128)(2,1)}) custom-call(bf16[3,64,128]{2,1,0:T(8,128)(2,1)} %bitcast.57, bf16[3,64,128]{2,1,0:T(8,128)(2,1)} %bitcast.58, bf16[3,128,128]{2,1,0:T(8,128)(2,1)} %bitcast.47, bf16[3,128,128]{2,1,0:T(8,128)(2,1)} %bitcast.48, ...), custom_call_target="tpu_custom_call" | custom-call | tf_op jit(solution)/shard_map/pallas_call | solution.py:244
  2.0 4.5 %collective-permute-start = (bf16[736,128]{1,0:T(8,128)(2,1)}, bf16[736,128]{1,0:T(8,128)(2,1)S(1)}, u32[]{:S(2)}, u32[]{:S(2)}) collective-permute-start(bf16[736,128]{1,0:T(8,128)(2,1)} %get-tuple-element.26.refs_0_.refs_4_), channel_id=1, source_target_pairs={{0,32},{32,0},{1,33},{33,1},{2,34},{34,2},{3,35},{35,3},{4,36},{36... | collective-permute-start | bytes 565256 | tf_op jit(solution)/shard_map/ppermute | solution.py:86
  6.5 15.4 %all-to-all-start = ((bf16[32,16,128]{2,1,0:T(8,128)(2,1)}), bf16[32,16,128]{2,1,0:T(8,128)(2,1)S(1)}, u32[]{:S(2)}, u32[]{:S(2)}) async-start(bf16[32,16,128]{2,1,0:T(8,128)(2,1)} %bitcast.67), calls=%async_computation | async-start | bytes 262144 | tf_op jit(solution)/shard_map/all_to_all | solution.py:268
  22.0 2.1 %collective-permute-start.1 = (bf16[736,128]{1,0:T(8,128)(2,1)S(1)}, bf16[736,128]{1,0:T(8,128)(2,1)S(1)}, u32[]{:S(2)}, u32[]{:S(2)}) collective-permute-start(bf16[736,128]{1,0:T(8,128)(2,1)S(1)} %copy-done), channel_id=1, source_target_pairs={{0,1},{1,0},{2,3},{3,2},{4,5},{5,4},{6,7},{7,6},{8,9},{9,8},{10,11... | collective-permute-start | bytes 565256 | tf_op jit(solution)/shard_map/ppermute | solution.py:86
  24.2 2.3 %collective-permute-start.2 = (bf16[736,128]{1,0:T(8,128)(2,1)S(1)}, bf16[736,128]{1,0:T(8,128)(2,1)S(1)}, u32[]{:S(2)}, u32[]{:S(2)}) collective-permute-start(bf16[736,128]{1,0:T(8,128)(2,1)S(1)} %collective-permute-done.refs_2_.refs_6_), channel_id=1, source_target_pairs={{0,1},{1,0},{2,3},{3,2},{4,5},{5,4},{6,7},{7,6},{8,9},{9,8},{10,11... | collective-permute-start | bytes 565256 | tf_op jit(solution)/shard_map/ppermute | solution.py:86
  26.6 0.9 copy-done.5
  27.8 3.3 %collective-permute-start.4 = (bf16[1984,128]{1,0:T(8,128)(2,1)S(1)}, bf16[1984,128]{1,0:T(8,128)(2,1)S(1)}, u32[]{:S(2)}, u32[]{:S(2)}) collective-permute-start(bf16[1984,128]{1,0:T(8,128)(2,1)S(1)} %shard_map.130.refs_0_.refs_4_.refs_8_), channel_id=1, source_target_pairs={{0,32},{32,0},{1,33},{33,1},{2,34},{34,2},{3,35},{35,3},{4,36},{36... | collective-permute-start | bytes 1523720 | tf_op jit(solution)/shard_map/ppermute | solution.py:86
  31.5 6.3 %all-to-all-done = bf16[32,16,128]{2,1,0:T(8,128)(2,1)S(1)} async-done(((bf16[32,16,128]{2,1,0:T(8,128)(2,1)}), bf16[32,16,128]{2,1,0:T(8,128)(2,1)S(1)}, u32[]{:S(2)}, u32[]{:S(2)}) %all-to-all-start) | async-done | bytes 131104 | tf_op jit(solution)/shard_map/all_to_all | solution.py:268
  37.8 1.1 shard_map.128
  38.8 6.8 %all-to-all-start.1 = ((bf16[16,2,2,16,128]{4,3,2,1,0:T(8,128)(2,1)}), bf16[16,2,2,16,128]{4,3,2,1,0:T(8,128)(2,1)S(1)}, u32[]{:S(2)}, u32[]{:S(2)}) async-start(bf16[16,2,2,16,128]{4,3,2,1,0:T(8,128)(2,1)} %bitcast.14), calls=%async_computation.1 | async-start | bytes 524288 | tf_op jit(solution)/shard_map/all_to_all | solution.py:206
  45.6 3.9 %collective-permute-start.3 = (bf16[1984,128]{1,0:T(8,128)(2,1)S(1)}, bf16[1984,128]{1,0:T(8,128)(2,1)S(1)}, u32[]{:S(2)}, u32[]{:S(2)}) collective-permute-start(bf16[1984,128]{1,0:T(8,128)(2,1)S(1)} %shard_map.130.refs_0_.refs_4_.refs_8_), channel_id=1, source_target_pairs={{0,1},{1,0},{2,3},{3,2},{4,5},{5,4},{6,7},{7,6},{8,9},{9,8},{10,11... | collective-permute-start | bytes 1523720 | tf_op jit(solution)/shard_map/ppermute | solution.py:86
  49.5 1.9 %collective-permute-start.5 = (bf16[1984,128]{1,0:T(8,128)(2,1)S(1)}, bf16[1984,128]{1,0:T(8,128)(2,1)S(1)}, u32[]{:S(2)}, u32[]{:S(2)}) collective-permute-start(bf16[1984,128]{1,0:T(8,128)(2,1)S(1)} %collective-permute-done.4.refs_2_.refs_6_.refs_10_), channel_id=1, source_target_pairs={{0,1},{1,0},{2,3},{3,2},{4,5},{5,4},{6,7},{7,6},{8,9},{9,8},{10,11... | collective-permute-start | bytes 1523720 | tf_op jit(solution)/shard_map/ppermute | solution.py:86
  51.5 1.5 all-to-all-done.1.got
  53.8 4.1 %all-to-all-start.2 = ((bf16[8,2,2,16,128]{4,3,2,1,0:T(8,128)(2,1)}), bf16[8,2,2,16,128]{4,3,2,1,0:T(8,128)(2,1)S(1)}, u32[]{:S(2)}, u32[]{:S(2)}) async-start(bf16[8,2,2,16,128]{4,3,2,1,0:T(8,128)(2,1)} %get-tuple-element.30), calls=%async_computation.2 | async-start | bytes 262144 | tf_op jit(solution)/shard_map/all_to_all | solution.py:210
  58.0 13.8 %all-to-all-done.2 = bf16[8,2,2,16,128]{4,3,2,1,0:T(8,128)(2,1)S(1)} async-done(((bf16[8,2,2,16,128]{4,3,2,1,0:T(8,128)(2,1)}), bf16[8,2,2,16,128]{4,3,2,1,0:T(8,128)(2,1)S(1)}, u32[]{:S(2)}, u32[]{:S(2)}) %all-to-all-start.2) | async-done | bytes 131104 | tf_op jit(solution)/shard_map/all_to_all | solution.py:210
  72.1 14.6 %all_to_all.40.got = bf16[16,2,2,16,128]{4,3,2,1,0:T(8,128)(2,1)S(1)} all-to-all(bf16[16,2,2,16,128]{4,3,2,1,0:T(8,128)(2,1)S(1)} %bitcast.43), channel_id=1, replica_groups=mesh['zh'=8,'zl'=2,'x'=4,'y'=4,'core'=2] {'x','y'}, dimensions={0} | all-to-all | bytes 524288 | tf_op jit(solution)/shard_map/all_to_all | solution.py:206
  87.0 16.6 %all_to_all.41 = bf16[8,2,2,16,128]{4,3,2,1,0:T(8,128)(2,1)S(1)} all-to-all(bf16[8,2,2,16,128]{4,3,2,1,0:T(8,128)(2,1)S(1)} %get-tuple-element.32), channel_id=1, replica_groups=mesh['zh'=8,'zl'=2,'x'=4,'y'=4,'core'=2] {'zh'}, dimensions={0} | all-to-all | bytes 262144 | tf_op jit(solution)/shard_map/all_to_all | solution.py:210
  104.0 10.7 %all_to_all.42.got = bf16[16,2,2,16,128]{4,3,2,1,0:T(8,128)(2,1)S(1)} all-to-all(bf16[16,2,2,16,128]{4,3,2,1,0:T(8,128)(2,1)S(1)} %bitcast.60), channel_id=1, replica_groups=mesh['zh'=8,'zl'=2,'x'=4,'y'=4,'core'=2] {'x','y'}, dimensions={0} | all-to-all | bytes 524288 | tf_op jit(solution)/shard_map/all_to_all | solution.py:206
  115.5 3.4 %all-to-all-start.6 = ((bf16[8,2,2,16,128]{4,3,2,1,0:T(8,128)(2,1)}), bf16[8,2,2,16,128]{4,3,2,1,0:T(8,128)(2,1)S(1)}, u32[]{:S(2)}, u32[]{:S(2)}) async-start(bf16[8,2,2,16,128]{4,3,2,1,0:T(8,128)(2,1)} %get-tuple-element.35), calls=%async_computation.6 | async-start | bytes 262144 | tf_op jit(solution)/shard_map/all_to_all | solution.py:210
  118.9 6.9 %collective-permute-start.8 = (bf16[2,16,128]{2,1,0:T(8,128)(2,1)S(1)}, bf16[2,16,128]{2,1,0:T(8,128)(2,1)S(1)}, u32[]{:S(2)}, u32[]{:S(2)}) collective-permute-start(bf16[2,16,128]{2,1,0:T(8,128)(2,1)S(1)} %get-tuple-element.45), channel_id=1, source_target_pairs={{0,33},{1,32},{32,1},{33,0},{2,35},{3,34},{34,3},{35,2},{4,37},{5,... | collective-permute-start | bytes 24584 | tf_op jit(solution)/shard_map/ppermute | solution.py:348
  125.8 1.9 %collective-permute-start.6 = (bf16[2,16,128]{2,1,0:T(8,128)(2,1)S(1)}, bf16[2,16,128]{2,1,0:T(8,128)(2,1)S(1)}, u32[]{:S(2)}, u32[]{:S(2)}) collective-permute-start(bf16[2,16,128]{2,1,0:T(8,128)(2,1)S(1)} %get-tuple-element.47), channel_id=1, source_target_pairs={{0,1},{1,0},{32,33},{33,32},{2,3},{3,2},{34,35},{35,34},{4,5},{5,4... | collective-permute-start | bytes 24584 | tf_op jit(solution)/shard_map/ppermute | solution.py:348
  127.7 3.2 %collective-permute-start.7 = (bf16[2,16,128]{2,1,0:T(8,128)(2,1)S(1)}, bf16[2,16,128]{2,1,0:T(8,128)(2,1)S(1)}, u32[]{:S(2)}, u32[]{:S(2)}) collective-permute-start(bf16[2,16,128]{2,1,0:T(8,128)(2,1)S(1)} %get-tuple-element.48), channel_id=1, source_target_pairs={{0,32},{1,33},{32,0},{33,1},{2,34},{3,35},{34,2},{35,3},{4,36},{5,... | collective-permute-start | bytes 24584 | tf_op jit(solution)/shard_map/ppermute | solution.py:348
  131.0 1.4 collective-permute-done.7.home_2
  132.8 19.1 %all_to_all.43 = bf16[64,16,128]{2,1,0:T(8,128)(2,1)S(1)} all-to-all(bf16[64,16,128]{2,1,0:T(8,128)(2,1)S(1)} %bitcast.42), channel_id=1, replica_groups=mesh['zh'=8,'zl'=2,'x'=4,'y'=4,'core'=2] {'zl','x','y','core'}, dimensions={0} | all-to-all | bytes 524288 | tf_op jit(solution)/shard_map/all_to_all | solution.py:351
  (41 shorter events, 4.7 us)
Async XLA Ops:
  0.0 26.5 %copy-start.1 = (bf16[1,1,2,4,128,128]{5,4,3,2,1,0:T(8,128)(2,1)S(1)}, bf16[1,1,2,4,128,128]{5,4,3,2,1,0:T(8,128)(2,1)}, u32[]{:S(2)}) copy-start(bf16[1,1,2,4,128,128]{5,4,3,2,1,0:T(8,128)(2,1)} %param.16) | copy-start | bytes 786436
  0.0 26.5 %copy-start.3 = (bf16[1,1,3,1,128,128]{5,4,3,2,1,0:T(8,128)(2,1)S(1)}, bf16[1,1,3,1,128,128]{5,4,3,2,1,0:T(8,128)(2,1)}, u32[]{:S(2)}) copy-start(bf16[1,1,3,1,128,128]{5,4,3,2,1,0:T(8,128)(2,1)} %param.15) | copy-start | bytes 294916
  0.0 26.5 %copy-start.4 = (bf16[1,1,3,1,64,128]{5,4,3,2,1,0:T(8,128)(2,1)S(1)}, bf16[1,1,3,1,64,128]{5,4,3,2,1,0:T(8,128)(2,1)}, u32[]{:S(2)}) copy-start(bf16[1,1,3,1,64,128]{5,4,3,2,1,0:T(8,128)(2,1)} %param.13) | copy-start | bytes 147460
  2.0 20.0 %copy-start = (bf16[736,128]{1,0:T(8,128)(2,1)S(1)}, bf16[736,128]{1,0:T(8,128)(2,1)}, u32[]{:S(2)}) copy-start(bf16[736,128]{1,0:T(8,128)(2,1)} %get-tuple-element.26.refs_0_.refs_4_) | copy-start | bytes 565252
  2.0 20.0 %collective-permute-start = (bf16[736,128]{1,0:T(8,128)(2,1)}, bf16[736,128]{1,0:T(8,128)(2,1)S(1)}, u32[]{:S(2)}, u32[]{:S(2)}) collective-permute-start(bf16[736,128]{1,0:T(8,128)(2,1)} %get-tuple-element.26.refs_0_.refs_4_), channel_id=1, source_target_pairs={{0,32},{32,0},{1,33},{33,1},{2,34},{34,2},{3,35},{35,3},{4,36},{36... | collective-permute-start | bytes 565256 | tf_op jit(solution)/shard_map/ppermute | solution.py:86
  6.5 20.1 %copy-start.2 = (bf16[1,1,3,1,128,128]{5,4,3,2,1,0:T(8,128)(2,1)S(1)}, bf16[1,1,3,1,128,128]{5,4,3,2,1,0:T(8,128)(2,1)}, u32[]{:S(2)}) copy-start(bf16[1,1,3,1,128,128]{5,4,3,2,1,0:T(8,128)(2,1)} %param.14) | copy-start | bytes 294916
  6.5 31.3 %all-to-all-start = ((bf16[32,16,128]{2,1,0:T(8,128)(2,1)}), bf16[32,16,128]{2,1,0:T(8,128)(2,1)S(1)}, u32[]{:S(2)}, u32[]{:S(2)}) async-start(bf16[32,16,128]{2,1,0:T(8,128)(2,1)} %bitcast.67), calls=%async_computation | async-start | bytes 262144 | tf_op jit(solution)/shard_map/all_to_all | solution.py:268
  22.0 9.3 %collective-permute-start.1 = (bf16[736,128]{1,0:T(8,128)(2,1)S(1)}, bf16[736,128]{1,0:T(8,128)(2,1)S(1)}, u32[]{:S(2)}, u32[]{:S(2)}) collective-permute-start(bf16[736,128]{1,0:T(8,128)(2,1)S(1)} %copy-done), channel_id=1, source_target_pairs={{0,1},{1,0},{2,3},{3,2},{4,5},{5,4},{6,7},{7,6},{8,9},{9,8},{10,11... | collective-permute-start | bytes 565256 | tf_op jit(solution)/shard_map/ppermute | solution.py:86
  24.2 2.4 %copy-start.8 = (s32[1,1,2,4,128]{4,3,2,1,0:T(4,128)S(1)}, s32[1,1,2,4,128]{4,3,2,1,0:T(4,128)}, u32[]{:S(2)}) copy-start(s32[1,1,2,4,128]{4,3,2,1,0:T(4,128)} %param.24) | copy-start | bytes 12292
  24.2 2.4 %copy-start.6 = (s32[1,1,2,4,128]{4,3,2,1,0:T(4,128)S(1)}, s32[1,1,2,4,128]{4,3,2,1,0:T(4,128)}, u32[]{:S(2)}) copy-start(s32[1,1,2,4,128]{4,3,2,1,0:T(4,128)} %param.19) | copy-start | bytes 12292
  24.2 7.2 %collective-permute-start.2 = (bf16[736,128]{1,0:T(8,128)(2,1)S(1)}, bf16[736,128]{1,0:T(8,128)(2,1)S(1)}, u32[]{:S(2)}, u32[]{:S(2)}) collective-permute-start(bf16[736,128]{1,0:T(8,128)(2,1)S(1)} %collective-permute-done.refs_2_.refs_6_), channel_id=1, source_target_pairs={{0,1},{1,0},{2,3},{3,2},{4,5},{5,4},{6,7},{7,6},{8,9},{9,8},{10,11... | collective-permute-start | bytes 565256 | tf_op jit(solution)/shard_map/ppermute | solution.py:86
  26.6 1.0 copy-start.5
  27.8 21.7 %collective-permute-start.4 = (bf16[1984,128]{1,0:T(8,128)(2,1)S(1)}, bf16[1984,128]{1,0:T(8,128)(2,1)S(1)}, u32[]{:S(2)}, u32[]{:S(2)}) collective-permute-start(bf16[1984,128]{1,0:T(8,128)(2,1)S(1)} %shard_map.130.refs_0_.refs_4_.refs_8_), channel_id=1, source_target_pairs={{0,32},{32,0},{1,33},{33,1},{2,34},{34,2},{3,35},{35,3},{4,36},{36... | collective-permute-start | bytes 1523720 | tf_op jit(solution)/shard_map/ppermute | solution.py:86
  38.8 14.1 %all-to-all-start.1 = ((bf16[16,2,2,16,128]{4,3,2,1,0:T(8,128)(2,1)}), bf16[16,2,2,16,128]{4,3,2,1,0:T(8,128)(2,1)S(1)}, u32[]{:S(2)}, u32[]{:S(2)}) async-start(bf16[16,2,2,16,128]{4,3,2,1,0:T(8,128)(2,1)} %bitcast.14), calls=%async_computation.1 | async-start | bytes 524288 | tf_op jit(solution)/shard_map/all_to_all | solution.py:206
  45.6 12.3 %collective-permute-start.3 = (bf16[1984,128]{1,0:T(8,128)(2,1)S(1)}, bf16[1984,128]{1,0:T(8,128)(2,1)S(1)}, u32[]{:S(2)}, u32[]{:S(2)}) collective-permute-start(bf16[1984,128]{1,0:T(8,128)(2,1)S(1)} %shard_map.130.refs_0_.refs_4_.refs_8_), channel_id=1, source_target_pairs={{0,1},{1,0},{2,3},{3,2},{4,5},{5,4},{6,7},{7,6},{8,9},{9,8},{10,11... | collective-permute-start | bytes 1523720 | tf_op jit(solution)/shard_map/ppermute | solution.py:86
  49.5 8.4 %collective-permute-start.5 = (bf16[1984,128]{1,0:T(8,128)(2,1)S(1)}, bf16[1984,128]{1,0:T(8,128)(2,1)S(1)}, u32[]{:S(2)}, u32[]{:S(2)}) collective-permute-start(bf16[1984,128]{1,0:T(8,128)(2,1)S(1)} %collective-permute-done.4.refs_2_.refs_6_.refs_10_), channel_id=1, source_target_pairs={{0,1},{1,0},{2,3},{3,2},{4,5},{5,4},{6,7},{7,6},{8,9},{9,8},{10,11... | collective-permute-start | bytes 1523720 | tf_op jit(solution)/shard_map/ppermute | solution.py:86
  53.8 18.0 %all-to-all-start.2 = ((bf16[8,2,2,16,128]{4,3,2,1,0:T(8,128)(2,1)}), bf16[8,2,2,16,128]{4,3,2,1,0:T(8,128)(2,1)S(1)}, u32[]{:S(2)}, u32[]{:S(2)}) async-start(bf16[8,2,2,16,128]{4,3,2,1,0:T(8,128)(2,1)} %get-tuple-element.30), calls=%async_computation.2 | async-start | bytes 262144 | tf_op jit(solution)/shard_map/all_to_all | solution.py:210
  115.5 16.9 %all-to-all-start.6 = ((bf16[8,2,2,16,128]{4,3,2,1,0:T(8,128)(2,1)}), bf16[8,2,2,16,128]{4,3,2,1,0:T(8,128)(2,1)S(1)}, u32[]{:S(2)}, u32[]{:S(2)}) async-start(bf16[8,2,2,16,128]{4,3,2,1,0:T(8,128)(2,1)} %get-tuple-element.35), calls=%async_computation.6 | async-start | bytes 262144 | tf_op jit(solution)/shard_map/all_to_all | solution.py:210
  118.9 12.1 %collective-permute-start.8 = (bf16[2,16,128]{2,1,0:T(8,128)(2,1)S(1)}, bf16[2,16,128]{2,1,0:T(8,128)(2,1)S(1)}, u32[]{:S(2)}, u32[]{:S(2)}) collective-permute-start(bf16[2,16,128]{2,1,0:T(8,128)(2,1)S(1)} %get-tuple-element.45), channel_id=1, source_target_pairs={{0,33},{1,32},{32,1},{33,0},{2,35},{3,34},{34,3},{35,2},{4,37},{5,... | collective-permute-start | bytes 24584 | tf_op jit(solution)/shard_map/ppermute | solution.py:348
  125.8 5.2 %collective-permute-start.6 = (bf16[2,16,128]{2,1,0:T(8,128)(2,1)S(1)}, bf16[2,16,128]{2,1,0:T(8,128)(2,1)S(1)}, u32[]{:S(2)}, u32[]{:S(2)}) collective-permute-start(bf16[2,16,128]{2,1,0:T(8,128)(2,1)S(1)} %get-tuple-element.47), channel_id=1, source_target_pairs={{0,1},{1,0},{32,33},{33,32},{2,3},{3,2},{34,35},{35,34},{4,5},{5,4... | collective-permute-start | bytes 24584 | tf_op jit(solution)/shard_map/ppermute | solution.py:348
  127.7 4.7 %collective-permute-start.7 = (bf16[2,16,128]{2,1,0:T(8,128)(2,1)S(1)}, bf16[2,16,128]{2,1,0:T(8,128)(2,1)S(1)}, u32[]{:S(2)}, u32[]{:S(2)}) collective-permute-start(bf16[2,16,128]{2,1,0:T(8,128)(2,1)S(1)} %get-tuple-element.48), channel_id=1, source_target_pairs={{0,32},{1,33},{32,0},{33,1},{2,34},{3,35},{34,2},{35,3},{4,36},{5,... | collective-permute-start | bytes 24584 | tf_op jit(solution)/shard_map/ppermute | solution.py:348
  132.8 19.2 %copy-start.7 = (bf16[64,128]{1,0:T(8,128)(2,1)S(1)}, bf16[64,128]{1,0:T(8,128)(2,1)}, u32[]{:S(2)}) copy-start(bf16[64,128]{1,0:T(8,128)(2,1)} %get-tuple-element.40.forward) | copy-start | bytes 49156

commit v10 on v9

--- a/solution.py
+++ b/solution.py
@@ -57,11 +57,12 @@
     at = at + extent
     packed[at : at + sides_1.shape[1]] = sides_1[0]
     at = at + sides_1.shape[1]
-    for side, (source, target, count) in enumerate(((ls, lt, lc), (us, ut, uc))):
+    for side, refs in enumerate(((ls, lt, lc), (us, ut, uc))):
+        source, target, count = (ref[...] for ref in refs)
         for g in range(2):
             row = (2 * side + g) * 2 * blocks
             for b in range(blocks):
-                goal = jnp.where(b < count[g], target[g, b], NOWHERE)
+                goal = jnp.where(b < count[0, g], target[g, b], NOWHERE)
                 index[row + b : row + b + 1] = jnp.full((1, extent), source[g, b], jnp.int32)
                 index[row + blocks + b : row + blocks + b + 1] = jnp.full((1, extent), goal, jnp.int32)
     packed[at : at + index.shape[0]] = index[...].astype(F32).astype(BF16)
@@ -241,12 +242,13 @@
     tile_rows = blocks * extent
 
     first_sizes = [tile_rows, extent, side_extent, 8 * blocks]
+    numbers = (low_source, low_target, low_count[None], up_source, up_target, up_count[None])
     packed, copies, forward_2 = pl.pallas_call(
         first_kernel,
         grid=(1,),
         in_specs=[one_of(sides, 1), one_of(sides, 2), one_of(low_inv, 1), one_of(low_inv, 2)]
         + [one_of(low_tiles, 0), one_of(low_rows, 0)]
-        + [scalars()] * 6,
+        + [whole(array) for array in numbers],
         out_shape=[
             jax.ShapeDtypeStruct((sum(first_sizes), extent), BF16),
             jax.ShapeDtypeStruct((high, side_extent, extent), BF16),
@@ -261,7 +263,7 @@
         compiler_params=pltpu.CompilerParams(vmem_limit_bytes=56 << 20),
     )(
         *(sides, sides, low_inv, low_inv, low_tiles, low_rows),
-        *(low_source, low_target, low_count, up_source, up_target, up_count),
+        *numbers,
     )
     z_mate = swapped(packed, "zl")
     copies = copies.reshape(-1, rows, extent)

time: 154 us -> 154 us (level)
  no operation moved by 1% of the time
where the time goes in v10:
time: 154 us; the launch traced here: 153 us
  blocking collectives  61 us (40%)
  starting transfers between devices  59.8 us (39%)
  waiting for transfers between devices  23.1 us (15%)
  Pallas kernels  7.27 us (5%)
    all_to_all x2, blocking collectives, row_exchange(): return lax.all_to_all(chunks, ('x', 'y'), 0, 0, tiled=True)  25.3 us
    all_to_all x1, blocking collectives, body(): lax.all_to_all(partial.reshape(-1, rows, extent), ('zl', 'x', 'y', 'core'...  19.1 us
    ppermute x6, starting transfers between devices, swapped(): return lax.ppermute(value, axis, [(0, 1), (1, 0)])  18.1 us
    all_to_all x1, blocking collectives, gather_column(): got = lax.all_to_all(copies, 'zh', 0, 0, tiled=True)  16.6 us
    all_to_all x1, starting transfers between devices, body(): column = lax.all_to_all(copies, ('zh', 'zl', 'core'), 0, 0, tiled=True)  15.4 us
    all_to_all x2, waiting for transfers between devices, gather_column(): got = lax.all_to_all(copies, 'zh', 0, 0, tiled=True)  13.8 us
    ppermute x3, starting transfers between devices, body(): lax.ppermute(done[step], GROUP, [(i, i ^ step) for i in range(SPLIT)])  12 us
    all_to_all x2, starting transfers between devices, gather_column(): got = lax.all_to_all(copies, 'zh', 0, 0, tiled=True)  7.5 us
  transfers between devices with their start and end apart: 13, of which 4 were waited for; matrix products, arithmetic and copies ran while one was open for 0% of the time, Pallas kernels for 1%

profile of v10, /device:TPU:1, one launch (start us, length us, event | category | flops | bytes accessed | tf_op | source)
XLA Modules:
  0.0 152.8 jit_solution(9638895479265116763)
XLA Ops:
  0.0 2.0 %shard_map.127 = (bf16[736,128]{1,0:T(8,128)(2,1)}, bf16[8,64,128]{2,1,0:T(8,128)(2,1)}, bf16[64,128]{1,0:T(8,128)(2,1)}) custom-call(bf16[3,64,128]{2,1,0:T(8,128)(2,1)} %bitcast.57, bf16[3,64,128]{2,1,0:T(8,128)(2,1)} %bitcast.58, bf16[3,128,128]{2,1,0:T(8,128)(2,1)} %bitcast.47, bf16[3,128,128]{2,1,0:T(8,128)(2,1)} %bitcast.48, ...), custom_call_target="tpu_custom_call" | custom-call | tf_op jit(solution)/shard_map/pallas_call | solution.py:246
  2.0 4.5 %collective-permute-start = (bf16[736,128]{1,0:T(8,128)(2,1)}, bf16[736,128]{1,0:T(8,128)(2,1)S(1)}, u32[]{:S(2)}, u32[]{:S(2)}) collective-permute-start(bf16[736,128]{1,0:T(8,128)(2,1)} %get-tuple-element.26.refs_0_.refs_4_), channel_id=1, source_target_pairs={{0,32},{32,0},{1,33},{33,1},{2,34},{34,2},{3,35},{35,3},{4,36},{36... | collective-permute-start | bytes 565256 | tf_op jit(solution)/shard_map/ppermute | solution.py:87
  6.5 15.4 %all-to-all-start = ((bf16[32,16,128]{2,1,0:T(8,128)(2,1)}), bf16[32,16,128]{2,1,0:T(8,128)(2,1)S(1)}, u32[]{:S(2)}, u32[]{:S(2)}) async-start(bf16[32,16,128]{2,1,0:T(8,128)(2,1)} %bitcast.67), calls=%async_computation | async-start | bytes 262144 | tf_op jit(solution)/shard_map/all_to_all | solution.py:270
  22.0 2.1 %collective-permute-start.1 = (bf16[736,128]{1,0:T(8,128)(2,1)S(1)}, bf16[736,128]{1,0:T(8,128)(2,1)S(1)}, u32[]{:S(2)}, u32[]{:S(2)}) collective-permute-start(bf16[736,128]{1,0:T(8,128)(2,1)S(1)} %copy-done), channel_id=1, source_target_pairs={{0,1},{1,0},{2,3},{3,2},{4,5},{5,4},{6,7},{7,6},{8,9},{9,8},{10,11... | collective-permute-start | bytes 565256 | tf_op jit(solution)/shard_map/ppermute | solution.py:87
  24.2 2.3 %collective-permute-start.2 = (bf16[736,128]{1,0:T(8,128)(2,1)S(1)}, bf16[736,128]{1,0:T(8,128)(2,1)S(1)}, u32[]{:S(2)}, u32[]{:S(2)}) collective-permute-start(bf16[736,128]{1,0:T(8,128)(2,1)S(1)} %collective-permute-done.refs_2_.refs_6_), channel_id=1, source_target_pairs={{0,1},{1,0},{2,3},{3,2},{4,5},{5,4},{6,7},{7,6},{8,9},{9,8},{10,11... | collective-permute-start | bytes 565256 | tf_op jit(solution)/shard_map/ppermute | solution.py:87
  26.6 0.9 copy-done.5
  27.9 3.3 %collective-permute-start.4 = (bf16[1984,128]{1,0:T(8,128)(2,1)S(1)}, bf16[1984,128]{1,0:T(8,128)(2,1)S(1)}, u32[]{:S(2)}, u32[]{:S(2)}) collective-permute-start(bf16[1984,128]{1,0:T(8,128)(2,1)S(1)} %shard_map.130.refs_0_.refs_4_.refs_8_), channel_id=1, source_target_pairs={{0,32},{32,0},{1,33},{33,1},{2,34},{34,2},{3,35},{35,3},{4,36},{36... | collective-permute-start | bytes 1523720 | tf_op jit(solution)/shard_map/ppermute | solution.py:87
  31.5 6.3 %all-to-all-done = bf16[32,16,128]{2,1,0:T(8,128)(2,1)S(1)} async-done(((bf16[32,16,128]{2,1,0:T(8,128)(2,1)}), bf16[32,16,128]{2,1,0:T(8,128)(2,1)S(1)}, u32[]{:S(2)}, u32[]{:S(2)}) %all-to-all-start) | async-done | bytes 131104 | tf_op jit(solution)/shard_map/all_to_all | solution.py:270
  37.8 1.1 shard_map.128
  38.9 6.8 %all-to-all-start.1 = ((bf16[16,2,2,16,128]{4,3,2,1,0:T(8,128)(2,1)}), bf16[16,2,2,16,128]{4,3,2,1,0:T(8,128)(2,1)S(1)}, u32[]{:S(2)}, u32[]{:S(2)}) async-start(bf16[16,2,2,16,128]{4,3,2,1,0:T(8,128)(2,1)} %bitcast.14), calls=%async_computation.1 | async-start | bytes 524288 | tf_op jit(solution)/shard_map/all_to_all | solution.py:207
  45.6 3.9 %collective-permute-start.3 = (bf16[1984,128]{1,0:T(8,128)(2,1)S(1)}, bf16[1984,128]{1,0:T(8,128)(2,1)S(1)}, u32[]{:S(2)}, u32[]{:S(2)}) collective-permute-start(bf16[1984,128]{1,0:T(8,128)(2,1)S(1)} %shard_map.130.refs_0_.refs_4_.refs_8_), channel_id=1, source_target_pairs={{0,1},{1,0},{2,3},{3,2},{4,5},{5,4},{6,7},{7,6},{8,9},{9,8},{10,11... | collective-permute-start | bytes 1523720 | tf_op jit(solution)/shard_map/ppermute | solution.py:87
  49.6 1.9 %collective-permute-start.5 = (bf16[1984,128]{1,0:T(8,128)(2,1)S(1)}, bf16[1984,128]{1,0:T(8,128)(2,1)S(1)}, u32[]{:S(2)}, u32[]{:S(2)}) collective-permute-start(bf16[1984,128]{1,0:T(8,128)(2,1)S(1)} %collective-permute-done.4.refs_2_.refs_6_.refs_10_), channel_id=1, source_target_pairs={{0,1},{1,0},{2,3},{3,2},{4,5},{5,4},{6,7},{7,6},{8,9},{9,8},{10,11... | collective-permute-start | bytes 1523720 | tf_op jit(solution)/shard_map/ppermute | solution.py:87
  51.5 1.5 all-to-all-done.1.got
  53.8 4.1 %all-to-all-start.2 = ((bf16[8,2,2,16,128]{4,3,2,1,0:T(8,128)(2,1)}), bf16[8,2,2,16,128]{4,3,2,1,0:T(8,128)(2,1)S(1)}, u32[]{:S(2)}, u32[]{:S(2)}) async-start(bf16[8,2,2,16,128]{4,3,2,1,0:T(8,128)(2,1)} %get-tuple-element.30), calls=%async_computation.2 | async-start | bytes 262144 | tf_op jit(solution)/shard_map/all_to_all | solution.py:211
  58.0 13.8 %all-to-all-done.2 = bf16[8,2,2,16,128]{4,3,2,1,0:T(8,128)(2,1)S(1)} async-done(((bf16[8,2,2,16,128]{4,3,2,1,0:T(8,128)(2,1)}), bf16[8,2,2,16,128]{4,3,2,1,0:T(8,128)(2,1)S(1)}, u32[]{:S(2)}, u32[]{:S(2)}) %all-to-all-start.2) | async-done | bytes 131104 | tf_op jit(solution)/shard_map/all_to_all | solution.py:211
  72.2 14.6 %all_to_all.40.got = bf16[16,2,2,16,128]{4,3,2,1,0:T(8,128)(2,1)S(1)} all-to-all(bf16[16,2,2,16,128]{4,3,2,1,0:T(8,128)(2,1)S(1)} %bitcast.43), channel_id=1, replica_groups=mesh['zh'=8,'zl'=2,'x'=4,'y'=4,'core'=2] {'x','y'}, dimensions={0} | all-to-all | bytes 524288 | tf_op jit(solution)/shard_map/all_to_all | solution.py:207
  87.0 16.6 %all_to_all.41 = bf16[8,2,2,16,128]{4,3,2,1,0:T(8,128)(2,1)S(1)} all-to-all(bf16[8,2,2,16,128]{4,3,2,1,0:T(8,128)(2,1)S(1)} %get-tuple-element.32), channel_id=1, replica_groups=mesh['zh'=8,'zl'=2,'x'=4,'y'=4,'core'=2] {'zh'}, dimensions={0} | all-to-all | bytes 262144 | tf_op jit(solution)/shard_map/all_to_all | solution.py:211
  104.0 10.7 %all_to_all.42.got = bf16[16,2,2,16,128]{4,3,2,1,0:T(8,128)(2,1)S(1)} all-to-all(bf16[16,2,2,16,128]{4,3,2,1,0:T(8,128)(2,1)S(1)} %bitcast.60), channel_id=1, replica_groups=mesh['zh'=8,'zl'=2,'x'=4,'y'=4,'core'=2] {'x','y'}, dimensions={0} | all-to-all | bytes 524288 | tf_op jit(solution)/shard_map/all_to_all | solution.py:207
  115.6 3.4 %all-to-all-start.6 = ((bf16[8,2,2,16,128]{4,3,2,1,0:T(8,128)(2,1)}), bf16[8,2,2,16,128]{4,3,2,1,0:T(8,128)(2,1)S(1)}, u32[]{:S(2)}, u32[]{:S(2)}) async-start(bf16[8,2,2,16,128]{4,3,2,1,0:T(8,128)(2,1)} %get-tuple-element.35), calls=%async_computation.6 | async-start | bytes 262144 | tf_op jit(solution)/shard_map/all_to_all | solution.py:211
  119.0 6.9 %collective-permute-start.8 = (bf16[2,16,128]{2,1,0:T(8,128)(2,1)S(1)}, bf16[2,16,128]{2,1,0:T(8,128)(2,1)S(1)}, u32[]{:S(2)}, u32[]{:S(2)}) collective-permute-start(bf16[2,16,128]{2,1,0:T(8,128)(2,1)S(1)} %get-tuple-element.45), channel_id=1, source_target_pairs={{0,33},{1,32},{32,1},{33,0},{2,35},{3,34},{34,3},{35,2},{4,37},{5,... | collective-permute-start | bytes 24584 | tf_op jit(solution)/shard_map/ppermute | solution.py:350
  125.8 1.9 %collective-permute-start.6 = (bf16[2,16,128]{2,1,0:T(8,128)(2,1)S(1)}, bf16[2,16,128]{2,1,0:T(8,128)(2,1)S(1)}, u32[]{:S(2)}, u32[]{:S(2)}) collective-permute-start(bf16[2,16,128]{2,1,0:T(8,128)(2,1)S(1)} %get-tuple-element.47), channel_id=1, source_target_pairs={{0,1},{1,0},{32,33},{33,32},{2,3},{3,2},{34,35},{35,34},{4,5},{5,4... | collective-permute-start | bytes 24584 | tf_op jit(solution)/shard_map/ppermute | solution.py:350
  127.8 3.2 %collective-permute-start.7 = (bf16[2,16,128]{2,1,0:T(8,128)(2,1)S(1)}, bf16[2,16,128]{2,1,0:T(8,128)(2,1)S(1)}, u32[]{:S(2)}, u32[]{:S(2)}) collective-permute-start(bf16[2,16,128]{2,1,0:T(8,128)(2,1)S(1)} %get-tuple-element.48), channel_id=1, source_target_pairs={{0,32},{1,33},{32,0},{33,1},{2,34},{3,35},{34,2},{35,3},{4,36},{5,... | collective-permute-start | bytes 24584 | tf_op jit(solution)/shard_map/ppermute | solution.py:350
  131.0 1.5 collective-permute-done.7.home_2
  132.9 19.1 %all_to_all.43 = bf16[64,16,128]{2,1,0:T(8,128)(2,1)S(1)} all-to-all(bf16[64,16,128]{2,1,0:T(8,128)(2,1)S(1)} %bitcast.42), channel_id=1, replica_groups=mesh['zh'=8,'zl'=2,'x'=4,'y'=4,'core'=2] {'zl','x','y','core'}, dimensions={0} | all-to-all | bytes 524288 | tf_op jit(solution)/shard_map/all_to_all | solution.py:353
  (41 shorter events, 4.7 us)
Async XLA Ops:
  0.0 26.5 %copy-start.1 = (bf16[1,1,2,4,128,128]{5,4,3,2,1,0:T(8,128)(2,1)S(1)}, bf16[1,1,2,4,128,128]{5,4,3,2,1,0:T(8,128)(2,1)}, u32[]{:S(2)}) copy-start(bf16[1,1,2,4,128,128]{5,4,3,2,1,0:T(8,128)(2,1)} %param.16) | copy-start | bytes 786436
  0.0 26.5 %copy-start.3 = (bf16[1,1,3,1,128,128]{5,4,3,2,1,0:T(8,128)(2,1)S(1)}, bf16[1,1,3,1,128,128]{5,4,3,2,1,0:T(8,128)(2,1)}, u32[]{:S(2)}) copy-start(bf16[1,1,3,1,128,128]{5,4,3,2,1,0:T(8,128)(2,1)} %param.15) | copy-start | bytes 294916
  0.0 26.5 %copy-start.4 = (bf16[1,1,3,1,64,128]{5,4,3,2,1,0:T(8,128)(2,1)S(1)}, bf16[1,1,3,1,64,128]{5,4,3,2,1,0:T(8,128)(2,1)}, u32[]{:S(2)}) copy-start(bf16[1,1,3,1,64,128]{5,4,3,2,1,0:T(8,128)(2,1)} %param.13) | copy-start | bytes 147460
  2.0 20.0 %copy-start = (bf16[736,128]{1,0:T(8,128)(2,1)S(1)}, bf16[736,128]{1,0:T(8,128)(2,1)}, u32[]{:S(2)}) copy-start(bf16[736,128]{1,0:T(8,128)(2,1)} %get-tuple-element.26.refs_0_.refs_4_) | copy-start | bytes 565252
  2.0 20.0 %collective-permute-start = (bf16[736,128]{1,0:T(8,128)(2,1)}, bf16[736,128]{1,0:T(8,128)(2,1)S(1)}, u32[]{:S(2)}, u32[]{:S(2)}) collective-permute-start(bf16[736,128]{1,0:T(8,128)(2,1)} %get-tuple-element.26.refs_0_.refs_4_), channel_id=1, source_target_pairs={{0,32},{32,0},{1,33},{33,1},{2,34},{34,2},{3,35},{35,3},{4,36},{36... | collective-permute-start | bytes 565256 | tf_op jit(solution)/shard_map/ppermute | solution.py:87
  6.5 20.1 %copy-start.2 = (bf16[1,1,3,1,128,128]{5,4,3,2,1,0:T(8,128)(2,1)S(1)}, bf16[1,1,3,1,128,128]{5,4,3,2,1,0:T(8,128)(2,1)}, u32[]{:S(2)}) copy-start(bf16[1,1,3,1,128,128]{5,4,3,2,1,0:T(8,128)(2,1)} %param.14) | copy-start | bytes 294916
  6.5 31.3 %all-to-all-start = ((bf16[32,16,128]{2,1,0:T(8,128)(2,1)}), bf16[32,16,128]{2,1,0:T(8,128)(2,1)S(1)}, u32[]{:S(2)}, u32[]{:S(2)}) async-start(bf16[32,16,128]{2,1,0:T(8,128)(2,1)} %bitcast.67), calls=%async_computation | async-start | bytes 262144 | tf_op jit(solution)/shard_map/all_to_all | solution.py:270
  22.0 9.3 %collective-permute-start.1 = (bf16[736,128]{1,0:T(8,128)(2,1)S(1)}, bf16[736,128]{1,0:T(8,128)(2,1)S(1)}, u32[]{:S(2)}, u32[]{:S(2)}) collective-permute-start(bf16[736,128]{1,0:T(8,128)(2,1)S(1)} %copy-done), channel_id=1, source_target_pairs={{0,1},{1,0},{2,3},{3,2},{4,5},{5,4},{6,7},{7,6},{8,9},{9,8},{10,11... | collective-permute-start | bytes 565256 | tf_op jit(solution)/shard_map/ppermute | solution.py:87
  24.2 2.4 %copy-start.8 = (s32[1,1,2,4,128]{4,3,2,1,0:T(4,128)S(1)}, s32[1,1,2,4,128]{4,3,2,1,0:T(4,128)}, u32[]{:S(2)}) copy-start(s32[1,1,2,4,128]{4,3,2,1,0:T(4,128)} %param.24) | copy-start | bytes 12292
  24.2 2.4 %copy-start.6 = (s32[1,1,2,4,128]{4,3,2,1,0:T(4,128)S(1)}, s32[1,1,2,4,128]{4,3,2,1,0:T(4,128)}, u32[]{:S(2)}) copy-start(s32[1,1,2,4,128]{4,3,2,1,0:T(4,128)} %param.19) | copy-start | bytes 12292
  24.2 7.2 %collective-permute-start.2 = (bf16[736,128]{1,0:T(8,128)(2,1)S(1)}, bf16[736,128]{1,0:T(8,128)(2,1)S(1)}, u32[]{:S(2)}, u32[]{:S(2)}) collective-permute-start(bf16[736,128]{1,0:T(8,128)(2,1)S(1)} %collective-permute-done.refs_2_.refs_6_), channel_id=1, source_target_pairs={{0,1},{1,0},{2,3},{3,2},{4,5},{5,4},{6,7},{7,6},{8,9},{9,8},{10,11... | collective-permute-start | bytes 565256 | tf_op jit(solution)/shard_map/ppermute | solution.py:87
  26.6 1.0 copy-start.5
  27.9 21.7 %collective-permute-start.4 = (bf16[1984,128]{1,0:T(8,128)(2,1)S(1)}, bf16[1984,128]{1,0:T(8,128)(2,1)S(1)}, u32[]{:S(2)}, u32[]{:S(2)}) collective-permute-start(bf16[1984,128]{1,0:T(8,128)(2,1)S(1)} %shard_map.130.refs_0_.refs_4_.refs_8_), channel_id=1, source_target_pairs={{0,32},{32,0},{1,33},{33,1},{2,34},{34,2},{3,35},{35,3},{4,36},{36... | collective-permute-start | bytes 1523720 | tf_op jit(solution)/shard_map/ppermute | solution.py:87
  38.9 14.1 %all-to-all-start.1 = ((bf16[16,2,2,16,128]{4,3,2,1,0:T(8,128)(2,1)}), bf16[16,2,2,16,128]{4,3,2,1,0:T(8,128)(2,1)S(1)}, u32[]{:S(2)}, u32[]{:S(2)}) async-start(bf16[16,2,2,16,128]{4,3,2,1,0:T(8,128)(2,1)} %bitcast.14), calls=%async_computation.1 | async-start | bytes 524288 | tf_op jit(solution)/shard_map/all_to_all | solution.py:207
  45.6 12.3 %collective-permute-start.3 = (bf16[1984,128]{1,0:T(8,128)(2,1)S(1)}, bf16[1984,128]{1,0:T(8,128)(2,1)S(1)}, u32[]{:S(2)}, u32[]{:S(2)}) collective-permute-start(bf16[1984,128]{1,0:T(8,128)(2,1)S(1)} %shard_map.130.refs_0_.refs_4_.refs_8_), channel_id=1, source_target_pairs={{0,1},{1,0},{2,3},{3,2},{4,5},{5,4},{6,7},{7,6},{8,9},{9,8},{10,11... | collective-permute-start | bytes 1523720 | tf_op jit(solution)/shard_map/ppermute | solution.py:87
  49.6 8.4 %collective-permute-start.5 = (bf16[1984,128]{1,0:T(8,128)(2,1)S(1)}, bf16[1984,128]{1,0:T(8,128)(2,1)S(1)}, u32[]{:S(2)}, u32[]{:S(2)}) collective-permute-start(bf16[1984,128]{1,0:T(8,128)(2,1)S(1)} %collective-permute-done.4.refs_2_.refs_6_.refs_10_), channel_id=1, source_target_pairs={{0,1},{1,0},{2,3},{3,2},{4,5},{5,4},{6,7},{7,6},{8,9},{9,8},{10,11... | collective-permute-start | bytes 1523720 | tf_op jit(solution)/shard_map/ppermute | solution.py:87
  53.8 18.0 %all-to-all-start.2 = ((bf16[8,2,2,16,128]{4,3,2,1,0:T(8,128)(2,1)}), bf16[8,2,2,16,128]{4,3,2,1,0:T(8,128)(2,1)S(1)}, u32[]{:S(2)}, u32[]{:S(2)}) async-start(bf16[8,2,2,16,128]{4,3,2,1,0:T(8,128)(2,1)} %get-tuple-element.30), calls=%async_computation.2 | async-start | bytes 262144 | tf_op jit(solution)/shard_map/all_to_all | solution.py:211
  115.6 16.9 %all-to-all-start.6 = ((bf16[8,2,2,16,128]{4,3,2,1,0:T(8,128)(2,1)}), bf16[8,2,2,16,128]{4,3,2,1,0:T(8,128)(2,1)S(1)}, u32[]{:S(2)}, u32[]{:S(2)}) async-start(bf16[8,2,2,16,128]{4,3,2,1,0:T(8,128)(2,1)} %get-tuple-element.35), calls=%async_computation.6 | async-start | bytes 262144 | tf_op jit(solution)/shard_map/all_to_all | solution.py:211
  119.0 12.1 %collective-permute-start.8 = (bf16[2,16,128]{2,1,0:T(8,128)(2,1)S(1)}, bf16[2,16,128]{2,1,0:T(8,128)(2,1)S(1)}, u32[]{:S(2)}, u32[]{:S(2)}) collective-permute-start(bf16[2,16,128]{2,1,0:T(8,128)(2,1)S(1)} %get-tuple-element.45), channel_id=1, source_target_pairs={{0,33},{1,32},{32,1},{33,0},{2,35},{3,34},{34,3},{35,2},{4,37},{5,... | collective-permute-start | bytes 24584 | tf_op jit(solution)/shard_map/ppermute | solution.py:350
  125.8 5.2 %collective-permute-start.6 = (bf16[2,16,128]{2,1,0:T(8,128)(2,1)S(1)}, bf16[2,16,128]{2,1,0:T(8,128)(2,1)S(1)}, u32[]{:S(2)}, u32[]{:S(2)}) collective-permute-start(bf16[2,16,128]{2,1,0:T(8,128)(2,1)S(1)} %get-tuple-element.47), channel_id=1, source_target_pairs={{0,1},{1,0},{32,33},{33,32},{2,3},{3,2},{34,35},{35,34},{4,5},{5,4... | collective-permute-start | bytes 24584 | tf_op jit(solution)/shard_map/ppermute | solution.py:350
  127.8 4.7 %collective-permute-start.7 = (bf16[2,16,128]{2,1,0:T(8,128)(2,1)S(1)}, bf16[2,16,128]{2,1,0:T(8,128)(2,1)S(1)}, u32[]{:S(2)}, u32[]{:S(2)}) collective-permute-start(bf16[2,16,128]{2,1,0:T(8,128)(2,1)S(1)} %get-tuple-element.48), channel_id=1, source_target_pairs={{0,32},{1,33},{32,0},{33,1},{2,34},{3,35},{34,2},{35,3},{4,36},{5,... | collective-permute-start | bytes 24584 | tf_op jit(solution)/shard_map/ppermute | solution.py:350
  132.9 19.1 %copy-start.7 = (bf16[64,128]{1,0:T(8,128)(2,1)S(1)}, bf16[64,128]{1,0:T(8,128)(2,1)}, u32[]{:S(2)}) copy-start(bf16[64,128]{1,0:T(8,128)(2,1)} %get-tuple-element.40.forward) | copy-start | bytes 49156
